TPU v7x, 32 devices: a whole 2x2x4 slice. The times are simulated.
32 devices in a mesh: dp: 2 (over x), expert: 16 (over z, y, core).
Axes of the slice: x: 2, y: 2, z: 4, core: 2. Of those that a mesh axis runs over, the one named last changes fastest.
Arguments:
- tokens: bfloat16 [4096, 2048], P(('dp', 'expert')), may hold values from -6 to 6
- out_grad: bfloat16 [4096, 2048], P(('dp', 'expert')), may hold values from -6 to 6
- expert_ids: int32 [4096, 6], P(('dp', 'expert')), may hold values from 0 to 15, all different within a row; in each aligned block of 128 rows (0 to 127, 128 to 255, ...) at most 49 rows name the same one
- gate_weights: float32 [4096, 6], P(('dp', 'expert')), may hold values from 0.05 to 1
- trained: int32 [4], replicated, may hold values from 0 to 15, as said below
- w_in: bfloat16 [16, 2048, 1408], P('expert'), may hold values from -0.125 to 0.125
- w_down: bfloat16 [16, 704, 2048], P('expert'), may hold values from -0.21875 to 0.21875
- saved: bfloat16 [2, 16, 784, 1408], P('dp', 'expert'), may hold values from -6 to 6
Outputs:
- in_grad: bfloat16 [4096, 2048], P(('dp', 'expert'))
- weight_grad: bfloat16 [16, 2048, 2112], P('expert', 'dp')
Inputs may be any that keep to these rules, and one draw needn't show every extreme that they name: `expert_ids`: among the 128 tokens of one device no expert is named more than 49 times, a bound that some block reaches; a token names 6 different experts. `trained`: 4 different expert ids; the ids 0 and 15 are always among them.
All inputs are finite; a program needn't handle non-finite values.
Results may differ from a plain program's by a relative error of at most 0.017.
Values may be sent and summed in bfloat16 or wider, within the bound.
No kernel may reach another device: no remote copies, remote signals or barrier semaphores. Data moves between devices by JAX's collectives and lax.ppermute only.
A program may use at most 128 MiB of HBM per device.

v0:
```python
import functools

import jax
import jax.numpy as jnp
from jax import lax
from jax.experimental import pallas as pl
from jax.experimental.pallas import tpu as pltpu
from jax.sharding import PartitionSpec as P

AXIS = "expert"
CORES = 2
CONTRACT_LAST = (((1,), (1,)), ((), ()))
CONTRACT_FIRST = (((0,), (0,)), ((), ()))


def chip_cycle(chips):
    width = 1
    while (2 * width) ** 2 <= chips:
        width *= 2
    height = chips // width
    if width == 1:
        return list(range(chips))
    order = [row * width for row in range(height)]
    for back, row in enumerate(reversed(range(height))):
        columns = range(1, width) if back % 2 == 0 else range(width - 1, 0, -1)
        order += [row * width + column for column in columns]
    return order


def row_tile(rows):
    return max(t for t in range(16, 129, 16) if rows % t == 0)


def gather_kernel(js, slot_ref, gate_ref, *refs, count, planes, cap, tile, gated):
    chunks, out_ref, buf, sems = refs[:count], refs[count], refs[count + 1], refs[count + 2]
    block = buf.shape[1] // count
    copies = []
    for i, chunk in enumerate(chunks):
        for plane in range(planes):
            start = pl.multiple_of(js[i] * block, block)
            copies.append(
                pltpu.make_async_copy(
                    chunk.at[pl.ds(plane * block, block)],
                    buf.at[plane, pl.ds(start, block)],
                    sems.at[i, plane],
                )
            )
    for copy in copies:
        copy.start()
    for copy in copies:
        copy.wait()
    rows, width = out_ref.shape[1], out_ref.shape[2]
    for plane in range(planes):
        for first in range(0, rows, tile):
            low, high = first // cap, (first + tile - 1) // cap + 1
            window = slice(low * block, high * block)
            slots = slot_ref[plane : plane + 1, window]
            labels = lax.broadcasted_iota(jnp.int32, (tile, (high - low) * block), 0) + first
            hit = labels == slots
            onehot = hit.astype(jnp.float32).astype(jnp.bfloat16)
            if gated:
                scale = jnp.sum(
                    jnp.where(hit, gate_ref[plane : plane + 1, window], 0.0), axis=1, keepdims=True
                )
            for left in range(0, width, 512):
                values = jnp.dot(
                    onehot, buf[plane, window, left : left + 512], preferred_element_type=jnp.float32
                )
                if gated:
                    values = values * scale
                out_ref[plane, first : first + tile, left : left + 512] = values.astype(jnp.bfloat16)


def gather_rows(js, slots, gates, chunks, rows, cap, gated):
    planes, count = slots.shape[0], len(chunks)
    block, width = chunks[0].shape[0] // planes, chunks[0].shape[1]
    flops = 2 * planes * rows * 4 * block * width
    return pl.pallas_call(
        functools.partial(
            gather_kernel, count=count, planes=planes, cap=cap, tile=row_tile(rows), gated=gated
        ),
        out_shape=jax.ShapeDtypeStruct((planes, rows, width), jnp.bfloat16),
        grid_spec=pltpu.PrefetchScalarGridSpec(
            num_scalar_prefetch=1,
            grid=(1,),
            in_specs=[pl.BlockSpec(slots.shape, lambda i, js: (0, 0))] * 2
            + [pl.BlockSpec(memory_space=pl.ANY)] * count,
            out_specs=pl.BlockSpec((planes, rows, width), lambda i, js: (0, 0, 0)),
            scratch_shapes=[
                pltpu.VMEM((planes, count * block, width), jnp.bfloat16),
                pltpu.SemaphoreType.DMA((count, planes)),
            ],
        ),
        compiler_params=pltpu.CompilerParams(vmem_limit_bytes=40 * 2**20),
        cost_estimate=pl.CostEstimate(
            flops=flops, bytes_accessed=planes * (count * block + rows) * width * 2, transcendentals=0
        ),
        name="gather_rows",
    )(js, slots, gates, *chunks)


def scatter_kernel(js, slot_ref, grad_ref, *refs, count, cap, span):
    outs, buf, sems = refs[:count], refs[count], refs[count + 1]
    block, width = buf.shape[1], buf.shape[2]
    rows = grad_ref.shape[0]
    copies = []
    for i, out in enumerate(outs):
        j = js[i]
        first = pl.multiple_of(jnp.minimum(j * cap // 16 * 16, rows - span), 16)
        slots = slot_ref[pl.ds(j, 1), :]
        labels = lax.broadcasted_iota(jnp.int32, (span, block), 0) + first
        onehot = (labels == slots).astype(jnp.float32).astype(jnp.bfloat16)
        for left in range(0, width, 512):
            values = lax.dot_general(
                onehot,
                grad_ref[pl.ds(first, span), left : left + 512],
                CONTRACT_FIRST,
                preferred_element_type=jnp.float32,
            )
            buf[i, :, left : left + 512] = values.astype(jnp.bfloat16)
        copy = pltpu.make_async_copy(buf.at[i], out, sems.at[i])
        copy.start()
        copies.append(copy)
    for copy in copies:
        copy.wait()


def scatter_rows(js, slots, grads, cap):
    count, block = slots.shape
    rows, width = grads.shape
    span = min(rows, -(-(cap + 15) // 16) * 16)
    return pl.pallas_call(
        functools.partial(scatter_kernel, count=count, cap=cap, span=span),
        out_shape=[jax.ShapeDtypeStruct((block, width), jnp.bfloat16)] * count,
        grid_spec=pltpu.PrefetchScalarGridSpec(
            num_scalar_prefetch=1,
            grid=(1,),
            in_specs=[
                pl.BlockSpec(slots.shape, lambda i, js: (0, 0)),
                pl.BlockSpec(grads.shape, lambda i, js: (0, 0)),
            ],
            out_specs=[pl.BlockSpec(memory_space=pl.ANY)] * count,
            scratch_shapes=[
                pltpu.VMEM((count, block, width), jnp.bfloat16),
                pltpu.SemaphoreType.DMA((count,)),
            ],
        ),
        compiler_params=pltpu.CompilerParams(vmem_limit_bytes=40 * 2**20),
        cost_estimate=pl.CostEstimate(
            flops=2 * count * span * block * width,
            bytes_accessed=(rows + count * block) * width * 2,
            transcendentals=0,
        ),
        name="scatter_rows",
    )(js, slots, grads)


def per_device(tokens, out_grad, expert_ids, gate_weights, trained, w_in, w_down, saved):
    groups, replicas = lax.axis_size(AXIS), lax.axis_size("dp")
    chips = groups // CORES
    tok_count, model_width = tokens.shape
    slot_total = saved.shape[2]
    cap = slot_total // groups
    hidden_units = w_down.shape[1]
    cut = model_width // replicas
    me, replica = lax.axis_index(AXIS), lax.axis_index("dp")

    order = chip_cycle(chips)
    after = {order[i]: order[(i + 1) % chips] for i in range(chips)}
    ahead = [(CORES * c + k, CORES * after[c] + k) for c in range(chips) for k in range(CORES)]
    behind = [(b, a) for a, b in ahead]
    swap = [(i, i ^ 1) for i in range(groups)]
    place = {c: i for i, c in enumerate(order)}
    table = jnp.array(
        [[order[(place[c] + d) % chips] for d in range(chips)] for c in range(chips)], jnp.int32
    )
    chip_at = lax.dynamic_slice(table, (me // CORES, 0), (1, chips))[0]
    core = me % CORES
    js = jnp.concatenate([CORES * chip_at + core, CORES * chip_at + 1 - core])

    def ring_gather(value, far):
        held = {0: value}
        up = down = value
        for step in range(1, max(far, chips - 1 - far) + 1):
            if step <= far:
                up = lax.ppermute(up, AXIS, ahead)
                held[(-step) % chips] = up
            if step <= chips - 1 - far:
                down = lax.ppermute(down, AXIS, behind)
                held[step] = down
        own = [held[d] for d in range(chips)]
        return own + [lax.ppermute(x, AXIS, swap) for x in own]

    def shifted(value, shift):
        return lax.ppermute(value, "dp", [(r, (r + shift) % replicas) for r in range(replicas)])

    def columns(value, owner):
        return lax.dynamic_slice_in_dim(value, owner * cut, cut, 1)

    labels = jnp.arange(groups, dtype=jnp.int32)
    chosen = expert_ids[None, :, :] == labels[:, None, None]
    routed = jnp.any(chosen, axis=2)
    gate = jnp.sum(jnp.where(chosen, gate_weights[None], 0.0), axis=2)
    earlier = jnp.triu(jnp.ones((tok_count, tok_count), jnp.bfloat16), 1)
    rank = jnp.dot(routed.astype(jnp.bfloat16), earlier, preferred_element_type=jnp.float32)
    slot = jnp.where(routed, rank + (me * cap).astype(jnp.float32), -1.0)
    info = lax.all_to_all(
        jnp.stack([slot, gate], axis=1), AXIS, split_axis=0, concat_axis=0, tiled=True
    )
    slots = info[:, 0, :].astype(jnp.int32)
    gates = info[:, 1, :]

    far = chips // 2
    grad_chunks = ring_gather(out_grad, far)
    halves = jnp.concatenate(
        [columns(tokens, replica)]
        + [shifted(columns(tokens, (replica + i) % replicas), i) for i in range(1, replicas)],
        axis=0,
    )
    token_chunks = ring_gather(halves, chips - 1 - far)
    plane_slots = [info[:, 0, :]] + [shifted(info[:, 0, :], i) for i in range(1, replicas)]
    all_slots = jnp.stack(plane_slots).reshape(replicas, groups * tok_count).astype(jnp.int32)

    s = gather_rows(
        js, slots.reshape(1, -1), gates.reshape(1, -1), grad_chunks, slot_total, cap, True
    )[0]
    saved_rows = saved.reshape(slot_total, 2 * hidden_units).astype(jnp.float32)
    gate_pre = saved_rows[:, :hidden_units]
    up_pre = saved_rows[:, hidden_units:]
    hidden_grad = lax.dot_general(s, w_down[0], CONTRACT_LAST, preferred_element_type=jnp.float32)
    sigmoid_gate = jax.nn.sigmoid(gate_pre)
    activated = gate_pre * sigmoid_gate
    pre_grad = jnp.concatenate(
        [
            hidden_grad * up_pre * sigmoid_gate * (1.0 + gate_pre * (1.0 - sigmoid_gate)),
            hidden_grad * activated,
        ],
        axis=1,
    ).astype(jnp.bfloat16)
    hidden = (activated * up_pre).astype(jnp.bfloat16)
    slot_grads = lax.dot_general(
        pre_grad, w_in[0], CONTRACT_LAST, preferred_element_type=jnp.float32
    ).astype(jnp.bfloat16)

    parts = scatter_rows(js, slots, slot_grads, cap)
    total = {}
    for d in sorted(range(chips), key=lambda d: -min(d, chips - d)):
        total[d] = parts[d].astype(jnp.float32) + lax.ppermute(
            parts[chips + d], AXIS, swap
        ).astype(jnp.float32)
    up_hops = chips - 1 - far
    up, down = total[up_hops], total[up_hops + 1]
    for step in range(max(up_hops, chips - 1 - up_hops)):
        if step < up_hops:
            got = lax.ppermute(up.astype(jnp.bfloat16), AXIS, ahead)
            up = got.astype(jnp.float32)
            if step < up_hops - 1:
                up = up + total[up_hops - 1 - step]
        if step < chips - 1 - up_hops:
            got = lax.ppermute(down.astype(jnp.bfloat16), AXIS, behind)
            down = got.astype(jnp.float32)
            if step < chips - 2 - up_hops:
                down = down + total[up_hops + 2 + step]
    in_grad = (total[0] + up + down).astype(jnp.bfloat16)

    def down_part(owner):
        return lax.dot_general(
            hidden, columns(s, owner), CONTRACT_FIRST, preferred_element_type=jnp.float32
        )

    grad_down = down_part(replica)
    grad_in = None
    x = gather_rows(js, all_slots, all_slots.astype(jnp.float32), token_chunks, slot_total, cap, False)
    for i in range(replicas):
        other = pre_grad if i == 0 else shifted(pre_grad, i)
        part = lax.dot_general(other, x[i], CONTRACT_FIRST, preferred_element_type=jnp.float32)
        grad_in = part if grad_in is None else grad_in + part
        if i:
            sent = down_part((replica + i) % replicas).astype(jnp.bfloat16)
            grad_down = grad_down + shifted(sent, i).astype(jnp.float32)
    trained_flag = jnp.any(trained == me).astype(jnp.float32)
    weight = (jnp.concatenate([grad_in, grad_down], axis=0) * trained_flag).astype(jnp.bfloat16)
    return in_grad, weight.T[None]


def solution(mesh):
    return jax.shard_map(
        per_device,
        mesh=mesh,
        in_specs=(
            P(("dp", "expert"), None),
            P(("dp", "expert"), None),
            P(("dp", "expert"), None),
            P(("dp", "expert"), None),
            P(),
            P("expert", None, None),
            P("expert", None, None),
            P("dp", "expert", None, None),
        ),
        out_specs=(P(("dp", "expert"), None), P("expert", "dp", None)),
        check_vma=False,
    )
```

profile of v0, /device:TPU:0, one launch (start us, length us, event | category | flops | bytes accessed | tf_op | source)
XLA Modules:
  0.0 235.9 jit_solution(1520683528251840713)
XLA Ops:
  0.6 3.1 %collective-permute-start.3 = (bf16[128,2048]{1,0:T(8,128)(2,1)}, bf16[128,2048]{1,0:T(8,128)(2,1)S(1)}, u32[]{:S(2)}, u32[]{:S(2)}) collective-permute-start(bf16[128,2048]{1,0:T(8,128)(2,1)} %refs_0_.1), channel_id=1, source_target_pairs={{0,4},{1,5},{2,0},{3,1},{4,8},{5,9},{6,2},{7,3},{8,12},{9,13},{10,... | collective-permute-start | bytes 1572872 | tf_op jit(solution)/shard_map/ppermute | solution.py:186
  3.7 12.1 %collective-permute-done.3.refs_7_ = bf16[128,2048]{1,0:T(8,128)(2,1)S(1)} collective-permute-done((bf16[128,2048]{1,0:T(8,128)(2,1)}, bf16[128,2048]{1,0:T(8,128)(2,1)S(1)}, u32[]{:S(2)}, u32[]{:S(2)}) %collective-permute-start.3) | collective-permute-done | bytes 524320 | tf_op jit(solution)/shard_map/ppermute | solution.py:186
  15.8 1.8 collective-permute-start.4
  17.6 1.9 constant_dynamic-slice_fusion.1
  21.0 5.8 %collective-permute-done.31 = bf16[128,1024]{1,0:T(8,128)(2,1)} collective-permute-done((bf16[128,1024]{1,0:T(8,128)(2,1)}, bf16[128,1024]{1,0:T(8,128)(2,1)}, u32[]{:S(2)}, u32[]{:S(2)}) %collective-permute-start.31) | collective-permute-done | bytes 262176 | tf_op jit(solution)/shard_map/ppermute | solution.py:195
  26.8 1.9 pad_maximum_fusion.1.refs_0_
  33.4 5.8 %all-to-all-start = ((f32[16,2,128]{2,1,0:T(2,128)}), f32[16,2,128]{2,1,0:T(2,128)S(1)}, u32[]{:S(2)}, u32[]{:S(2)}) async-start(f32[16,2,128]{2,1,0:T(2,128)} %copy.17), calls=%async_computation | async-start | bytes 32768 | tf_op jit(solution)/shard_map/all_to_all | solution.py:207
  40.0 1.9 collective-permute-start.36
  41.9 1.9 collective-permute-done.32.refs_1_
  43.8 8.4 %collective-permute-done.1.refs_2_ = bf16[128,2048]{1,0:T(8,128)(2,1)} collective-permute-done((bf16[128,2048]{1,0:T(8,128)(2,1)}, bf16[128,2048]{1,0:T(8,128)(2,1)}, u32[]{:S(2)}, u32[]{:S(2)}) %collective-permute-start.1) | collective-permute-done | bytes 524320 | tf_op jit(solution)/shard_map/ppermute | solution.py:189
  54.3 4.0 %bitcast_convert_fusion = f32[784,1408]{1,0:T(8,128)} fusion(bf16[1,1,784,1408]{3,2,1,0:T(8,128)(2,1)} %param.16), kind=kLoop, calls=%fused_computation.17 | loop fusion | flops 1103872 | bytes 6623232 | tf_op jit(solution)/shard_map/convert_element_type | solution.py:227
  60.4 3.0 %collective-permute-done.2.refs_3_ = bf16[128,2048]{1,0:T(8,128)(2,1)} collective-permute-done((bf16[128,2048]{1,0:T(8,128)(2,1)}, bf16[128,2048]{1,0:T(8,128)(2,1)}, u32[]{:S(2)}, u32[]{:S(2)}) %collective-permute-start.2) | collective-permute-done | bytes 524320 | tf_op jit(solution)/shard_map/ppermute | solution.py:189
  63.4 2.5 %collective-permute-done.6.refs_4_ = bf16[128,2048]{1,0:T(8,128)(2,1)} collective-permute-done((bf16[128,2048]{1,0:T(8,128)(2,1)}, bf16[128,2048]{1,0:T(8,128)(2,1)}, u32[]{:S(2)}, u32[]{:S(2)}) %collective-permute-start.6) | collective-permute-done | bytes 524320 | tf_op jit(solution)/shard_map/ppermute | solution.py:186
  73.2 5.8 %gather_rows.2 = bf16[1,784,2048]{2,1,0:T(8,128)(2,1)S(1)} custom-call(s32[16]{0:T(128)S(1)} %pad_add_fusion.js, s32[1,2048]{1,0:T(1,128)S(1)} %get-tuple-element.42.slot_ref, f32[1,2048]{1,0:T(1,128)S(1)} %get-tuple-element.43.gate_ref, bf16[128,2048]{1,0:T(8,128)(2,1)S(1)} %copy-done.4, bf16[128,2048]{1,0:T(8,128)(2,1)} %collective-permute-done.refs_1_, ...), custom_call_target="tpu_custom_call" | custom-call | flops 1644167168 | bytes 11599872 | tf_op jit(solution)/shard_map/gather_rows/pallas_call | solution.py:78
  79.1 4.5 %multiply_convert_fusion.2 = (bf16[784,704]{1,0:T(8,128)(2,1)S(1)}, bf16[784,704]{1,0:T(8,128)(2,1)S(1)}, bf16[784,704]{1,0:T(8,128)(2,1)}) fusion(f32[784,1408]{1,0:T(8,128)S(1)} %copy-done.40, bf16[1,704,2048]{2,1,0:T(8,128)(2,1)S(1)} %copy-done, bf16[1,784,2048]{2,1,0:T(8,128)(2,1)S(1)} %gather_rows.2), kind=kOutput, calls=%fused_computation.13 | convolution fusion | flops 2269008896 | bytes 13821952 | tf_op jit(solution)/shard_map/dot_general | solution.py:230
  85.5 8.1 %fusion.4.grad_ref = bf16[784,2048]{1,0:T(8,128)(2,1)S(1)} fusion(bf16[784,1408]{1,0:T(8,128)(2,1)S(1)} %pad_maximum_fusion, bf16[1,2048,1408]{2,1,0:T(8,128)(2,1)} %param.14), kind=kOutput, calls=%fused_computation.6 | convolution fusion | flops 4523065344 | bytes 11186176 | tf_op jit(solution)/shard_map/dot_general | solution.py:241
  93.6 6.3 %scatter_rows.1 = (bf16[128,2048]{1,0:T(8,128)(2,1)S(1)}, bf16[128,2048]{1,0:T(8,128)(2,1)S(1)}, bf16[128,2048]{1,0:T(8,128)(2,1)S(1)}, bf16[128,2048]{1,0:T(8,1...) custom-call(s32[16]{0:T(128)S(1)} %pad_add_fusion.js, ...), custom_call_target="tpu_custom_call" | custom-call | flops 536870912 | bytes 11599872 | tf_op jit(solution)/shard_map/scatter_rows/pallas_call | solution.py:132
  114.7 9.1 %collective-permute-done.34.refs_3_ = bf16[256,1024]{1,0:T(8,128)(2,1)} collective-permute-done((bf16[256,1024]{1,0:T(8,128)(2,1)}, bf16[256,1024]{1,0:T(8,128)(2,1)}, u32[]{:S(2)}, u32[]{:S(2)}) %collective-permute-start.34) | collective-permute-done | bytes 524320 | tf_op jit(solution)/shard_map/ppermute | solution.py:189
  130.1 3.1 %convolution_convert_fusion = bf16[704,1024]{1,0:T(8,128)(2,1)S(1)} fusion(bf16[784,704]{1,0:T(8,128)(2,1)} %get-tuple-element.36, bf16[1,784,2048]{2,1,0:T(8,128)(2,1)S(1)} %copy-done.3, s32[]{:T(128)S(6)} %select_n.48), kind=kOutput, calls=%fused_computation.18 | convolution fusion | flops 1131085824 | bytes 4151300 | tf_op jit(solution)/shard_map/dot_general | solution.py:267
  133.3 5.7 %collective-permute-done.35.refs_4_ = bf16[256,1024]{1,0:T(8,128)(2,1)S(1)} collective-permute-done((bf16[256,1024]{1,0:T(8,128)(2,1)}, bf16[256,1024]{1,0:T(8,128)(2,1)S(1)}, u32[]{:S(2)}, u32[]{:S(2)}) %collective-permute-start.35) | collective-permute-done | bytes 524320 | tf_op jit(solution)/shard_map/ppermute | solution.py:189
  140.6 7.7 %collective-permute-done.23 = bf16[128,2048]{1,0:T(8,128)(2,1)S(1)} collective-permute-done((bf16[128,2048]{1,0:T(8,128)(2,1)S(1)}, bf16[128,2048]{1,0:T(8,128)(2,1)S(1)}, u32[]{:S(2)}, u32[]{:S(2)}) %collective-permute-start.23) | collective-permute-done | bytes 524320 | tf_op jit(solution)/shard_map/ppermute | solution.py:260
  150.7 5.3 %gather_rows.3 = bf16[2,784,1024]{2,1,0:T(8,128)(2,1)S(1)} custom-call(s32[16]{0:T(128)S(1)} %pad_add_fusion.js, s32[2,2048]{1,0:T(2,128)S(1)} %get-tuple-element.40.slot_ref, f32[2,2048]{1,0:T(2,128)S(1)} %get-tuple-element.39.gate_ref, bf16[256,1024]{1,0:T(8,128)(2,1)} %pad_maximum_fusion.1.refs_0_, bf16[256,1024]{1,0:T(8,128)(2,1)} %collective-permute-done.32.refs_1_, ...), custom_call_target="tpu_custom_call" | custom-call | flops 1644167168 | bytes 11599872 | tf_op jit(solution)/shard_map/gather_rows/pallas_call | solution.py:78
  156.9 3.5 %collective-permute-done.17 = bf16[128,2048]{1,0:T(8,128)(2,1)S(1)} collective-permute-done((bf16[128,2048]{1,0:T(8,128)(2,1)S(1)}, bf16[128,2048]{1,0:T(8,128)(2,1)S(1)}, u32[]{:S(2)}, u32[]{:S(2)}) %collective-permute-start.17) | collective-permute-done | bytes 524320 | tf_op jit(solution)/shard_map/ppermute | solution.py:255
  161.3 3.2 %collective-permute-done.25 = bf16[128,2048]{1,0:T(8,128)(2,1)S(1)} collective-permute-done((bf16[128,2048]{1,0:T(8,128)(2,1)S(1)}, bf16[128,2048]{1,0:T(8,128)(2,1)S(1)}, u32[]{:S(2)}, u32[]{:S(2)}) %collective-permute-start.25) | collective-permute-done | bytes 524320 | tf_op jit(solution)/shard_map/ppermute | solution.py:260
  166.2 8.0 %collective-permute-done.48 = bf16[704,1024]{1,0:T(8,128)(2,1)} collective-permute-done((bf16[704,1024]{1,0:T(8,128)(2,1)S(1)}, bf16[704,1024]{1,0:T(8,128)(2,1)}, u32[]{:S(2)}, u32[]{:S(2)}) %collective-permute-start.48) | collective-permute-done | bytes 1441824 | tf_op jit(solution)/shard_map/ppermute | solution.py:195
  175.9 3.1 %convert_add_fusion = f32[704,1024]{1,0:T(8,128)S(1)} fusion(bf16[704,1024]{1,0:T(8,128)(2,1)} %collective-permute-done.48, bf16[784,704]{1,0:T(8,128)(2,1)S(1)} %copy-done.44, bf16[1,784,2048]{2,1,0:T(8,128)(2,1)S(1)} %copy-done.3, s32[]{:T(128)S(6)} %select_n.46), kind=kOutput, calls=%fused_computation.10 | convolution fusion | flops 1131806720 | bytes 7135236 | tf_op jit(solution)/shard_map/dot_general | solution.py:267
  180.6 5.6 %collective-permute-done.27 = bf16[128,2048]{1,0:T(8,128)(2,1)S(1)} collective-permute-done((bf16[128,2048]{1,0:T(8,128)(2,1)S(1)}, bf16[128,2048]{1,0:T(8,128)(2,1)S(1)}, u32[]{:S(2)}, u32[]{:S(2)}) %collective-permute-start.27) | collective-permute-done | bytes 524320 | tf_op jit(solution)/shard_map/ppermute | solution.py:260
  188.9 31.5 %collective-permute-done.47 = bf16[784,1408]{1,0:T(8,128)(2,1)S(1)} collective-permute-done((bf16[784,1408]{1,0:T(8,128)(2,1)S(1)}, bf16[784,1408]{1,0:T(8,128)(2,1)S(1)}, u32[]{:S(2)}, u32[]{:S(2)}) %collective-permute-start.47) | collective-permute-done | bytes 2207776 | tf_op jit(solution)/shard_map/ppermute | solution.py:195
  220.5 3.2 %fusion.11 = f32[1408,1024]{1,0:T(8,128)S(1)} fusion(bf16[784,1408]{1,0:T(8,128)(2,1)S(1)} %collective-permute-done.47, bf16[2,784,1024]{2,1,0:T(8,128)(2,1)S(1)} %gather_rows.3), kind=kOutput, calls=%fused_computation.20 | convolution fusion | flops 2260729856 | bytes 9580544 | tf_op jit(solution)/shard_map/dot_general | solution.py:276
  223.7 5.0 %convolution_add_fusion = f32[1408,1024]{1,0:T(8,128)} fusion(f32[1408,1024]{1,0:T(8,128)S(1)} %fusion.11, bf16[784,1408]{1,0:T(8,128)(2,1)S(1)} %copy-done.42, bf16[2,784,1024]{2,1,0:T(8,128)(2,1)S(1)} %gather_rows.3), kind=kOutput, calls=%fused_computation.5 | convolution fusion | flops 2262171648 | bytes 15347712 | tf_op jit(solution)/shard_map/dot_general | solution.py:276
  228.7 4.8 %fusion.3 = bf16[1,1024,2112]{1,2,0:T(8,128)(2,1)} fusion(f32[704,1024]{1,0:T(8,128)S(1)} %convert_add_fusion, f32[1408,1024]{1,0:T(8,128)} %convolution_add_fusion, f32[]{:T(128)S(6)} %convert_element_type.175), kind=kLoop, calls=%fused_computation.4 | loop fusion | flops 6488064 | bytes 12976132 | tf_op jit(solution)/shard_map/broadcast_in_dim | solution.py:283
  233.6 2.3 add_convert_fusion
  (191 shorter events, 54.2 us)
Async XLA Ops:
  0.6 15.2 %collective-permute-start.3 = (bf16[128,2048]{1,0:T(8,128)(2,1)}, bf16[128,2048]{1,0:T(8,128)(2,1)S(1)}, u32[]{:S(2)}, u32[]{:S(2)}) collective-permute-start(bf16[128,2048]{1,0:T(8,128)(2,1)} %refs_0_.1), channel_id=1, source_target_pairs={{0,4},{1,5},{2,0},{3,1},{4,8},{5,9},{6,2},{7,3},{8,12},{9,13},{10,... | collective-permute-start | bytes 1572872 | tf_op jit(solution)/shard_map/ppermute | solution.py:186
  3.7 25.5 %collective-permute-start = (bf16[128,2048]{1,0:T(8,128)(2,1)}, bf16[128,2048]{1,0:T(8,128)(2,1)}, u32[]{:S(2)}, u32[]{:S(2)}) collective-permute-start(bf16[128,2048]{1,0:T(8,128)(2,1)} %refs_0_.1), channel_id=1, source_target_pairs={{4,0},{5,1},{0,2},{1,3},{8,4},{9,5},{2,6},{3,7},{12,8},{13,9},{6,1... | collective-permute-start | bytes 1572872 | tf_op jit(solution)/shard_map/ppermute | solution.py:189
  15.8 14.9 %collective-permute-start.4 = (bf16[128,2048]{1,0:T(8,128)(2,1)S(1)}, bf16[128,2048]{1,0:T(8,128)(2,1)}, u32[]{:S(2)}, u32[]{:S(2)}) collective-permute-start(bf16[128,2048]{1,0:T(8,128)(2,1)S(1)} %collective-permute-done.3.refs_7_), channel_id=1, source_target_pairs={{0,4},{1,5},{2,0},{3,1},{4,8},{5,9},{6,2},{7,3},{8,12},{9,13},{10,... | collective-permute-start | bytes 1572872 | tf_op jit(solution)/shard_map/ppermute | solution.py:186
  21.0 21.0 %collective-permute-start.7 = (bf16[128,2048]{1,0:T(8,128)(2,1)}, bf16[128,2048]{1,0:T(8,128)(2,1)}, u32[]{:S(2)}, u32[]{:S(2)}) collective-permute-start(bf16[128,2048]{1,0:T(8,128)(2,1)} %refs_0_.1), channel_id=1, source_target_pairs={{0,1},{1,0},{2,3},{3,2},{4,5},{5,4},{6,7},{7,6},{8,9},{9,8},{10,11... | collective-permute-start | bytes 1572872 | tf_op jit(solution)/shard_map/ppermute | solution.py:192
  28.7 15.2 %collective-permute-start.32 = (bf16[256,1024]{1,0:T(8,128)(2,1)}, bf16[256,1024]{1,0:T(8,128)(2,1)}, u32[]{:S(2)}, u32[]{:S(2)}) collective-permute-start(bf16[256,1024]{1,0:T(8,128)(2,1)} %pad_maximum_fusion.1.refs_0_), channel_id=1, source_target_pairs={{4,0},{5,1},{0,2},{1,3},{8,4},{9,5},{2,6},{3,7},{12,8},{13,9},{6,1... | collective-permute-start | bytes 1572872 | tf_op jit(solution)/shard_map/ppermute | solution.py:189
  29.2 23.0 %collective-permute-start.1 = (bf16[128,2048]{1,0:T(8,128)(2,1)}, bf16[128,2048]{1,0:T(8,128)(2,1)}, u32[]{:S(2)}, u32[]{:S(2)}) collective-permute-start(bf16[128,2048]{1,0:T(8,128)(2,1)} %collective-permute-done.refs_1_), channel_id=1, source_target_pairs={{4,0},{5,1},{0,2},{1,3},{8,4},{9,5},{2,6},{3,7},{12,8},{13,9},{6,1... | collective-permute-start | bytes 1572872 | tf_op jit(solution)/shard_map/ppermute | solution.py:189
  30.7 22.2 %collective-permute-start.5 = (bf16[128,2048]{1,0:T(8,128)(2,1)}, bf16[128,2048]{1,0:T(8,128)(2,1)}, u32[]{:S(2)}, u32[]{:S(2)}) collective-permute-start(bf16[128,2048]{1,0:T(8,128)(2,1)} %collective-permute-done.4.refs_6_), channel_id=1, source_target_pairs={{0,4},{1,5},{2,0},{3,1},{4,8},{5,9},{6,2},{7,3},{8,12},{9,13},{10,... | collective-permute-start | bytes 1572872 | tf_op jit(solution)/shard_map/ppermute | solution.py:186
  33.4 32.6 %all-to-all-start = ((f32[16,2,128]{2,1,0:T(2,128)}), f32[16,2,128]{2,1,0:T(2,128)S(1)}, u32[]{:S(2)}, u32[]{:S(2)}) async-start(f32[16,2,128]{2,1,0:T(2,128)} %copy.17), calls=%async_computation | async-start | bytes 32768 | tf_op jit(solution)/shard_map/all_to_all | solution.py:207
  40.0 18.3 %collective-permute-start.36 = (bf16[256,1024]{1,0:T(8,128)(2,1)}, bf16[256,1024]{1,0:T(8,128)(2,1)}, u32[]{:S(2)}, u32[]{:S(2)}) collective-permute-start(bf16[256,1024]{1,0:T(8,128)(2,1)} %pad_maximum_fusion.1.refs_0_), channel_id=1, source_target_pairs={{0,4},{1,5},{2,0},{3,1},{4,8},{5,9},{6,2},{7,3},{8,12},{9,13},{10,... | collective-permute-start | bytes 1572872 | tf_op jit(solution)/shard_map/ppermute | solution.py:186
  41.9 16.4 %collective-permute-start.14 = (bf16[128,2048]{1,0:T(8,128)(2,1)}, bf16[128,2048]{1,0:T(8,128)(2,1)S(1)}, u32[]{:S(2)}, u32[]{:S(2)}) collective-permute-start(bf16[128,2048]{1,0:T(8,128)(2,1)} %copy-done.5), channel_id=1, source_target_pairs={{0,1},{1,0},{2,3},{3,2},{4,5},{5,4},{6,7},{7,6},{8,9},{9,8},{10,11... | collective-permute-start | bytes 1572872 | tf_op jit(solution)/shard_map/ppermute | solution.py:192
  43.8 15.7 %collective-permute-start.8 = (bf16[128,2048]{1,0:T(8,128)(2,1)}, bf16[128,2048]{1,0:T(8,128)(2,1)S(1)}, u32[]{:S(2)}, u32[]{:S(2)}) collective-permute-start(bf16[128,2048]{1,0:T(8,128)(2,1)} %collective-permute-done.refs_1_), channel_id=1, source_target_pairs={{0,1},{1,0},{2,3},{3,2},{4,5},{5,4},{6,7},{7,6},{8,9},{9,8},{10,11... | collective-permute-start | bytes 1572872 | tf_op jit(solution)/shard_map/ppermute | solution.py:192
  66.0 18.2 %collective-permute-start.30 = (f32[16,128]{1,0:T(8,128)S(1)}, f32[16,128]{1,0:T(8,128)S(1)}, u32[]{:S(2)}, u32[]{:S(2)}) collective-permute-start(f32[16,128]{1,0:T(8,128)S(1)} %bitcast.58), channel_id=1, source_target_pairs={{0,16},{16,0},{1,17},{17,1},{2,18},{18,2},{3,19},{19,3},{4,20},{20... | collective-permute-start | bytes 24584 | tf_op jit(solution)/shard_map/ppermute | solution.py:195
  67.6 43.8 %collective-permute-start.39 = (bf16[256,1024]{1,0:T(8,128)(2,1)}, bf16[256,1024]{1,0:T(8,128)(2,1)S(1)}, u32[]{:S(2)}, u32[]{:S(2)}) collective-permute-start(bf16[256,1024]{1,0:T(8,128)(2,1)} %pad_maximum_fusion.1.refs_0_), channel_id=1, source_target_pairs={{0,1},{1,0},{2,3},{3,2},{4,5},{5,4},{6,7},{7,6},{8,9},{9,8},{10,11... | collective-permute-start | bytes 1572872 | tf_op jit(solution)/shard_map/ppermute | solution.py:192
  67.8 41.8 %collective-permute-start.33 = (bf16[256,1024]{1,0:T(8,128)(2,1)}, bf16[256,1024]{1,0:T(8,128)(2,1)}, u32[]{:S(2)}, u32[]{:S(2)}) collective-permute-start(bf16[256,1024]{1,0:T(8,128)(2,1)} %collective-permute-done.32.refs_1_), channel_id=1, source_target_pairs={{4,0},{5,1},{0,2},{1,3},{8,4},{9,5},{2,6},{3,7},{12,8},{13,9},{6,1... | collective-permute-start | bytes 1572872 | tf_op jit(solution)/shard_map/ppermute | solution.py:189
  69.5 44.6 %collective-permute-start.40 = (bf16[256,1024]{1,0:T(8,128)(2,1)}, bf16[256,1024]{1,0:T(8,128)(2,1)}, u32[]{:S(2)}, u32[]{:S(2)}) collective-permute-start(bf16[256,1024]{1,0:T(8,128)(2,1)} %collective-permute-done.32.refs_1_), channel_id=1, source_target_pairs={{0,1},{1,0},{2,3},{3,2},{4,5},{5,4},{6,7},{7,6},{8,9},{9,8},{10,11... | collective-permute-start | bytes 1572872 | tf_op jit(solution)/shard_map/ppermute | solution.py:192
  69.5 44.0 %collective-permute-start.37 = (bf16[256,1024]{1,0:T(8,128)(2,1)}, bf16[256,1024]{1,0:T(8,128)(2,1)}, u32[]{:S(2)}, u32[]{:S(2)}) collective-permute-start(bf16[256,1024]{1,0:T(8,128)(2,1)} %collective-permute-done.36.refs_7_), channel_id=1, source_target_pairs={{0,4},{1,5},{2,0},{3,1},{4,8},{5,9},{6,2},{7,3},{8,12},{9,13},{10,... | collective-permute-start | bytes 1572872 | tf_op jit(solution)/shard_map/ppermute | solution.py:186
  84.2 30.5 %collective-permute-start.46 = (bf16[256,1024]{1,0:T(8,128)(2,1)}, bf16[256,1024]{1,0:T(8,128)(2,1)}, u32[]{:S(2)}, u32[]{:S(2)}) collective-permute-start(bf16[256,1024]{1,0:T(8,128)(2,1)} %collective-permute-done.36.refs_7_), channel_id=1, source_target_pairs={{0,1},{1,0},{2,3},{3,2},{4,5},{5,4},{6,7},{7,6},{8,9},{9,8},{10,11... | collective-permute-start | bytes 1572872 | tf_op jit(solution)/shard_map/ppermute | solution.py:192
  109.7 14.2 %collective-permute-start.34 = (bf16[256,1024]{1,0:T(8,128)(2,1)}, bf16[256,1024]{1,0:T(8,128)(2,1)}, u32[]{:S(2)}, u32[]{:S(2)}) collective-permute-start(bf16[256,1024]{1,0:T(8,128)(2,1)} %collective-permute-done.33.refs_2_), channel_id=1, source_target_pairs={{4,0},{5,1},{0,2},{1,3},{8,4},{9,5},{2,6},{3,7},{12,8},{13,9},{6,1... | collective-permute-start | bytes 1572872 | tf_op jit(solution)/shard_map/ppermute | solution.py:189
  113.5 14.7 %collective-permute-start.41 = (bf16[256,1024]{1,0:T(8,128)(2,1)}, bf16[256,1024]{1,0:T(8,128)(2,1)S(1)}, u32[]{:S(2)}, u32[]{:S(2)}) collective-permute-start(bf16[256,1024]{1,0:T(8,128)(2,1)} %collective-permute-done.33.refs_2_), channel_id=1, source_target_pairs={{0,1},{1,0},{2,3},{3,2},{4,5},{5,4},{6,7},{7,6},{8,9},{9,8},{10,11... | collective-permute-start | bytes 1572872 | tf_op jit(solution)/shard_map/ppermute | solution.py:192
  114.1 14.1 %collective-permute-start.38 = (bf16[256,1024]{1,0:T(8,128)(2,1)}, bf16[256,1024]{1,0:T(8,128)(2,1)S(1)}, u32[]{:S(2)}, u32[]{:S(2)}) collective-permute-start(bf16[256,1024]{1,0:T(8,128)(2,1)} %collective-permute-done.37.refs_6_), channel_id=1, source_target_pairs={{0,4},{1,5},{2,0},{3,1},{4,8},{5,9},{6,2},{7,3},{8,12},{9,13},{10,... | collective-permute-start | bytes 1572872 | tf_op jit(solution)/shard_map/ppermute | solution.py:186
  123.8 15.1 %collective-permute-start.35 = (bf16[256,1024]{1,0:T(8,128)(2,1)}, bf16[256,1024]{1,0:T(8,128)(2,1)S(1)}, u32[]{:S(2)}, u32[]{:S(2)}) collective-permute-start(bf16[256,1024]{1,0:T(8,128)(2,1)} %collective-permute-done.34.refs_3_), channel_id=1, source_target_pairs={{4,0},{5,1},{0,2},{1,3},{8,4},{9,5},{2,6},{3,7},{12,8},{13,9},{6,1... | collective-permute-start | bytes 1572872 | tf_op jit(solution)/shard_map/ppermute | solution.py:189
  128.7 19.6 %collective-permute-start.23 = (bf16[128,2048]{1,0:T(8,128)(2,1)S(1)}, bf16[128,2048]{1,0:T(8,128)(2,1)S(1)}, u32[]{:S(2)}, u32[]{:S(2)}) collective-permute-start(bf16[128,2048]{1,0:T(8,128)(2,1)S(1)} %add_convert_fusion.4), channel_id=1, source_target_pairs={{4,0},{5,1},{0,2},{1,3},{8,4},{9,5},{2,6},{3,7},{12,8},{13,9},{6,1... | collective-permute-start | bytes 1572872 | tf_op jit(solution)/shard_map/ppermute | solution.py:260
  139.6 34.6 %collective-permute-start.48 = (bf16[704,1024]{1,0:T(8,128)(2,1)S(1)}, bf16[704,1024]{1,0:T(8,128)(2,1)}, u32[]{:S(2)}, u32[]{:S(2)}) collective-permute-start(bf16[704,1024]{1,0:T(8,128)(2,1)S(1)} %convolution_convert_fusion), channel_id=1, source_target_pairs={{0,16},{16,0},{1,17},{17,1},{2,18},{18,2},{3,19},{19,3},{4,20},{20... | collective-permute-start | bytes 4325384 | tf_op jit(solution)/shard_map/ppermute | solution.py:195
  140.6 15.4 %collective-permute-start.18 = (bf16[128,2048]{1,0:T(8,128)(2,1)S(1)}, bf16[128,2048]{1,0:T(8,128)(2,1)S(1)}, u32[]{:S(2)}, u32[]{:S(2)}) collective-permute-start(bf16[128,2048]{1,0:T(8,128)(2,1)S(1)} %copy-done.37), channel_id=1, source_target_pairs={{0,1},{1,0},{2,3},{3,2},{4,5},{5,4},{6,7},{7,6},{8,9},{9,8},{10,11... | collective-permute-start | bytes 1572872 | tf_op jit(solution)/shard_map/ppermute | solution.py:248
  150.1 14.3 %collective-permute-start.25 = (bf16[128,2048]{1,0:T(8,128)(2,1)S(1)}, bf16[128,2048]{1,0:T(8,128)(2,1)S(1)}, u32[]{:S(2)}, u32[]{:S(2)}) collective-permute-start(bf16[128,2048]{1,0:T(8,128)(2,1)S(1)} %add_convert_fusion.3), channel_id=1, source_target_pairs={{4,0},{5,1},{0,2},{1,3},{8,4},{9,5},{2,6},{3,7},{12,8},{13,9},{6,1... | collective-permute-start | bytes 1572872 | tf_op jit(solution)/shard_map/ppermute | solution.py:260
  156.1 64.4 %collective-permute-start.47 = (bf16[784,1408]{1,0:T(8,128)(2,1)S(1)}, bf16[784,1408]{1,0:T(8,128)(2,1)S(1)}, u32[]{:S(2)}, u32[]{:S(2)}) collective-permute-start(bf16[784,1408]{1,0:T(8,128)(2,1)S(1)} %copy-done.42), channel_id=1, source_target_pairs={{0,16},{16,0},{1,17},{17,1},{2,18},{18,2},{3,19},{19,3},{4,20},{20... | collective-permute-start | bytes 6623240 | tf_op jit(solution)/shard_map/ppermute | solution.py:195
  160.4 18.5 %collective-permute-start.20 = (bf16[128,2048]{1,0:T(8,128)(2,1)S(1)}, bf16[128,2048]{1,0:T(8,128)(2,1)S(1)}, u32[]{:S(2)}, u32[]{:S(2)}) collective-permute-start(bf16[128,2048]{1,0:T(8,128)(2,1)S(1)} %copy-done.33), channel_id=1, source_target_pairs={{0,1},{1,0},{2,3},{3,2},{4,5},{5,4},{6,7},{7,6},{8,9},{9,8},{10,11... | collective-permute-start | bytes 1572872 | tf_op jit(solution)/shard_map/ppermute | solution.py:248
  160.7 19.9 %collective-permute-start.28 = (bf16[128,2048]{1,0:T(8,128)(2,1)S(1)}, bf16[128,2048]{1,0:T(8,128)(2,1)S(1)}, u32[]{:S(2)}, u32[]{:S(2)}) collective-permute-start(bf16[128,2048]{1,0:T(8,128)(2,1)S(1)} %copy-done.31), channel_id=1, source_target_pairs={{0,1},{1,0},{2,3},{3,2},{4,5},{5,4},{6,7},{7,6},{8,9},{9,8},{10,11... | collective-permute-start | bytes 1572872 | tf_op jit(solution)/shard_map/ppermute | solution.py:248
  164.5 14.6 %collective-permute-start.19 = (bf16[128,2048]{1,0:T(8,128)(2,1)S(1)}, bf16[128,2048]{1,0:T(8,128)(2,1)S(1)}, u32[]{:S(2)}, u32[]{:S(2)}) collective-permute-start(bf16[128,2048]{1,0:T(8,128)(2,1)S(1)} %add_convert_fusion.6), channel_id=1, source_target_pairs={{0,4},{1,5},{2,0},{3,1},{4,8},{5,9},{6,2},{7,3},{8,12},{9,13},{10,... | collective-permute-start | bytes 1572872 | tf_op jit(solution)/shard_map/ppermute | solution.py:255
  179.0 54.6 %collective-permute-start.15 = (bf16[128,2048]{1,0:T(8,128)(2,1)S(1)}, bf16[128,2048]{1,0:T(8,128)(2,1)S(1)}, u32[]{:S(2)}, u32[]{:S(2)}) collective-permute-start(bf16[128,2048]{1,0:T(8,128)(2,1)S(1)} %copy-done.29), channel_id=1, source_target_pairs={{0,1},{1,0},{2,3},{3,2},{4,5},{5,4},{6,7},{7,6},{8,9},{9,8},{10,11... | collective-permute-start | bytes 1572872 | tf_op jit(solution)/shard_map/ppermute | solution.py:248
  180.2 53.4 %collective-permute-start.21 = (bf16[128,2048]{1,0:T(8,128)(2,1)}, bf16[128,2048]{1,0:T(8,128)(2,1)}, u32[]{:S(2)}, u32[]{:S(2)}) collective-permute-start(bf16[128,2048]{1,0:T(8,128)(2,1)} %add_convert_fusion.5), channel_id=1, source_target_pairs={{0,4},{1,5},{2,0},{3,1},{4,8},{5,9},{6,2},{7,3},{8,12},{9,13},{10,... | collective-permute-start | bytes 1572872 | tf_op jit(solution)/shard_map/ppermute | solution.py:255
  187.3 46.3 %collective-permute-start.29 = (bf16[128,2048]{1,0:T(8,128)(2,1)}, bf16[128,2048]{1,0:T(8,128)(2,1)}, u32[]{:S(2)}, u32[]{:S(2)}) collective-permute-start(bf16[128,2048]{1,0:T(8,128)(2,1)} %add_convert_fusion.1), channel_id=1, source_target_pairs={{4,0},{5,1},{0,2},{1,3},{8,4},{9,5},{2,6},{3,7},{12,8},{13,9},{6,1... | collective-permute-start | bytes 1572872 | tf_op jit(solution)/shard_map/ppermute | solution.py:260
  (63 other events, 590.5 us)
where the time goes:
time: 237 us; the launch traced here: 236 us
  waiting for transfers between devices  109 us (46%)
  starting transfers between devices  40.2 us (17%)
  matrix products  27.1 us (11%)
  other arithmetic  20.9 us (9%)
  local copies, waits for them, and re-layouts  19 us (8%)
  Pallas kernels  17.4 us (7%)
    ppermute x4, waiting for transfers between devices, shifted(): lax.ppermute(value, 'dp', [(r, (r + shift) % replicas) for r in range(rep...  45.4 us
    ppermute x7, waiting for transfers between devices, ring_gather(): down = lax.ppermute(down, AXIS, behind)  28.2 us
    unnamed x90, local copies, waits for them, and re-layouts  16.5 us
    ppermute x4, waiting for transfers between devices, per_device(): got = lax.ppermute(down.astype(jnp.bfloat16), AXIS, behind)  16.5 us
    ppermute x7, waiting for transfers between devices, ring_gather(): up = lax.ppermute(up, AXIS, ahead)  15.9 us
    pallas_call x2, Pallas kernels, gather_rows(): pl.pallas_call(functools.partial(gather_kernel, count=count, planes=plane...  11.1 us
    ppermute x7, starting transfers between devices, ring_gather(): up = lax.ppermute(up, AXIS, ahead)  9.97 us
    dot_general x2, matrix products, per_device(): lax.dot_general(other, x[i], CONTRACT_FIRST, preferred_element_type=jnp.f...  8.27 us
  transfers between devices with their start and end apart: 50, of which 15 were waited for; matrix products, arithmetic and copies ran while one was open for 20% of the time, Pallas kernels for 7%

commit v1 on v0

v1 whole, which is shorter than its diff:
```python
import functools

import jax
import jax.numpy as jnp
from jax import lax
from jax.experimental import pallas as pl
from jax.experimental.pallas import tpu as pltpu
from jax.sharding import PartitionSpec as P

AXIS = "expert"
CORES = 2
CONTRACT_LAST = (((1,), (1,)), ((), ()))
CONTRACT_FIRST = (((0,), (0,)), ((), ()))


def chip_cycle(chips):
    width = 1
    while (2 * width) ** 2 <= chips:
        width *= 2
    height = chips // width
    if width == 1:
        return list(range(chips))
    order = [row * width for row in range(height)]
    for back, row in enumerate(reversed(range(height))):
        columns = range(1, width) if back % 2 == 0 else range(width - 1, 0, -1)
        order += [row * width + column for column in columns]
    return order


def after_all(*values):
    return lax.optimization_barrier(values)


def split_rows(value, count):
    tiles = value.shape[0] // 8
    ends = [8 * (tiles * (i + 1) // count) for i in range(count - 1)] + [value.shape[0]]
    return [value[a:b] for a, b in zip([0] + ends[:-1], ends)]


def windows(rows, cap, devices, group):
    span = min(rows, -(-(group * cap + 15) // 16) * 16)
    return [min(d * cap // 16 * 16, rows - span) for d in range(0, devices, group)], span


def gather_kernel(js, slot_ref, gate_ref, *refs, count, planes, cap, group, gated):
    chunks, out_hbm, buf, out_ref, in_sems, out_sems = refs[:count], *refs[count:]
    block = buf.shape[1] // count
    rows, width = out_ref.shape[1], out_ref.shape[2]
    for plane in range(planes):
        for i, chunk in enumerate(chunks):
            start = pl.multiple_of(js[i] * block, block)
            pltpu.make_async_copy(
                chunk.at[pl.ds(plane * block, block)],
                buf.at[plane, pl.ds(start, block)],
                in_sems.at[plane, js[i]],
            ).start()
    firsts, span = windows(rows, cap, count, group)
    firsts = firsts + [rows]
    copies = []
    for plane in range(planes):
        done = 0
        for g in range(count // group):
            first = firsts[g]
            for j in range(g * group, (g + 1) * group):
                window = buf.at[plane, pl.ds(j * block, block)]
                pltpu.make_async_copy(window, window, in_sems.at[plane, j]).wait()
            window = slice(g * group * block, (g + 1) * group * block)
            labels = lax.broadcasted_iota(jnp.int32, (span, group * block), 0) + first
            hit = labels == slot_ref[plane : plane + 1, window]
            onehot = hit.astype(jnp.float32).astype(jnp.bfloat16)
            if gated:
                gates = gate_ref[plane : plane + 1, window]
                scale = jnp.sum(jnp.where(hit, gates, 0.0), axis=1, keepdims=True)
            again = max(0, done - first)
            for left in range(0, width, 512):
                lanes = slice(left, left + 512)
                values = jnp.dot(
                    onehot, buf[plane, window, lanes], preferred_element_type=jnp.float32
                )
                if gated:
                    values = values * scale
                values = values.astype(jnp.bfloat16)
                if again:
                    out_ref[plane, first : first + again, lanes] += values[:again]
                if again < span:
                    out_ref[plane, first + again : first + span, lanes] = values[again:]
            done = first + span
            place = pl.ds(first, firsts[g + 1] - first)
            copy = pltpu.make_async_copy(
                out_ref.at[plane, place], out_hbm.at[plane, place], out_sems.at[plane, g]
            )
            copy.start()
            copies.append(copy)
    for copy in copies:
        copy.wait()


def gather_rows(js, slots, gates, chunks, rows, cap, gated):
    planes, count, group = slots.shape[0], len(chunks), CORES
    block, width = chunks[0].shape[0] // planes, chunks[0].shape[1]
    return pl.pallas_call(
        functools.partial(
            gather_kernel, count=count, planes=planes, cap=cap, group=group, gated=gated
        ),
        out_shape=jax.ShapeDtypeStruct((planes, rows, width), jnp.bfloat16),
        grid_spec=pltpu.PrefetchScalarGridSpec(
            num_scalar_prefetch=1,
            grid=(1,),
            in_specs=[pl.BlockSpec(slots.shape, lambda i, js: (0, 0))] * 2
            + [pl.BlockSpec(memory_space=pl.ANY)] * count,
            out_specs=pl.BlockSpec(memory_space=pltpu.HBM),
            scratch_shapes=[
                pltpu.VMEM((planes, count * block, width), jnp.bfloat16),
                pltpu.VMEM((planes, rows, width), jnp.bfloat16),
                pltpu.SemaphoreType.DMA((planes, count)),
                pltpu.SemaphoreType.DMA((planes, count // group)),
            ],
        ),
        compiler_params=pltpu.CompilerParams(vmem_limit_bytes=58 * 2**20),
        cost_estimate=pl.CostEstimate(
            flops=0,
            bytes_accessed=2 * planes * (count * block + rows) * width * 2,
            transcendentals=0,
        ),
        name="gather_rows",
    )(js, slots, gates, *chunks)


def scatter_kernel(js, slot_ref, grad_ref, *refs, groups, cap, span):
    outs, buf, sems = refs[:-2], refs[-2], refs[-1]
    block, width = buf.shape[1], buf.shape[2]
    rows, listed = grad_ref.shape[0], sum(groups)
    copies, x = [], 0
    for g, size in enumerate(groups):
        for at in range(size):
            for side in range(CORES):
                i = side * listed + x
                j = js[i]
                first = pl.multiple_of(jnp.minimum(j * cap // 16 * 16, rows - span), 16)
                slots = slot_ref[pl.ds(j, 1), :]
                labels = lax.broadcasted_iota(jnp.int32, (span, block), 0) + first
                onehot = (labels == slots).astype(jnp.float32).astype(jnp.bfloat16)
                for left in range(0, width, 512):
                    values = lax.dot_general(
                        onehot,
                        grad_ref[pl.ds(first, span), left : left + 512],
                        CONTRACT_FIRST,
                        preferred_element_type=jnp.float32,
                    )
                    buf[i, :, left : left + 512] = values.astype(jnp.bfloat16)
                out = outs[CORES * g + side].at[pl.ds(at * block, block)]
                copies.append(pltpu.make_async_copy(buf.at[i], out, sems.at[i]))
                copies[-1].start()
            x += 1
    for copy in copies:
        copy.wait()


def scatter_rows(js, slots, grads, cap, groups):
    count, block = slots.shape
    rows, width = grads.shape
    span = min(rows, -(-(cap + 15) // 16) * 16)
    return pl.pallas_call(
        functools.partial(scatter_kernel, groups=groups, cap=cap, span=span),
        out_shape=[
            jax.ShapeDtypeStruct((size * block, width), jnp.bfloat16)
            for size in groups
            for side in range(CORES)
        ],
        grid_spec=pltpu.PrefetchScalarGridSpec(
            num_scalar_prefetch=1,
            grid=(1,),
            in_specs=[
                pl.BlockSpec(slots.shape, lambda i, js: (0, 0)),
                pl.BlockSpec(grads.shape, lambda i, js: (0, 0)),
            ],
            out_specs=[pl.BlockSpec(memory_space=pltpu.HBM)] * (CORES * len(groups)),
            scratch_shapes=[
                pltpu.VMEM((count, block, width), jnp.bfloat16),
                pltpu.SemaphoreType.DMA((count,)),
            ],
        ),
        compiler_params=pltpu.CompilerParams(vmem_limit_bytes=58 * 2**20),
        cost_estimate=pl.CostEstimate(
            flops=2 * count * span * block * width,
            bytes_accessed=2 * (rows + count * block) * width * 2,
            transcendentals=0,
        ),
        name="scatter_rows",
    )(js, slots, grads)


def per_device(tokens, out_grad, expert_ids, gate_weights, trained, w_in, w_down, saved):
    groups, replicas = lax.axis_size(AXIS), lax.axis_size("dp")
    chips = groups // CORES
    tok_count, model_width = tokens.shape
    slot_total = saved.shape[2]
    cap = slot_total // groups
    hidden_units = w_down.shape[1]
    cut = model_width // replicas
    me, replica = lax.axis_index(AXIS), lax.axis_index("dp")
    shifts = range(1, replicas)

    far = chips // 2
    order = chip_cycle(chips)
    place = {c: i for i, c in enumerate(order)}

    def at(device, steps):
        return order[(place[device // CORES] + (steps if device % CORES == 0 else -steps)) % chips]

    along = [(i, CORES * at(i, 1) + i % CORES) for i in range(groups)]
    across = [(i, CORES * at(i, 1) + 1 - i % CORES) for i in range(groups)]
    swap = [(i, i ^ 1) for i in range(groups)]
    names = [("a", 0), ("b", 0)]
    names += [(kind, i) for i in range(1, far + 1) for kind in "ab" if (kind, i) != ("b", far)]
    pairs = names[:1] + names[2:]

    def device_at(device, name, way):
        kind, steps = name
        return CORES * at(device, way * steps) + (device % CORES if kind == "a" else 1 - device % CORES)

    def listing(labels, way):
        table = [
            [device_at(i, name, way) for name in labels]
            + [device_at(i ^ 1, name, way) for name in labels]
            for i in range(groups)
        ]
        return lax.dynamic_slice(jnp.array(table, jnp.int32), (me, 0), (1, 2 * len(labels)))[0]

    leaving = pairs[:0:-1]
    leaving = sorted(leaving, key=lambda name: (-name[1], name[0] == "a")) + [("a", 0)]
    sizes = [1, 2, len(leaving) - 3]
    work = {"js": listing(pairs, -1), "leaving": listing(leaving, 1)}

    def shifted(value, shift):
        return lax.ppermute(value, "dp", [(r, (r + shift) % replicas) for r in range(replicas)])

    def columns(value, owner):
        return lax.dynamic_slice_in_dim(value, owner * cut, cut, 1)

    def together(*places):
        values = after_all(*[box[key] for box, key in places])
        for (box, key), value in zip(places, values):
            box[key] = value

    came = {}

    def send(pieces, label, i):
        for shift in shifts:
            came[label, i, shift] = shifted(pieces[i], shift)
        return [(came, (label, i, shift)) for shift in shifts]

    def whole(label, count, shift):
        return jnp.concatenate([came[label, i, shift] for i in range(count)], axis=0)

    def hop(blocks, kind, step):
        blocks[kind, step] = lax.ppermute(blocks[kind, step - 1], AXIS, along)
        return blocks, (kind, step)

    def exchange(blocks, name):
        blocks["other", name] = lax.ppermute(blocks[name], AXIS, swap)
        return blocks, ("other", name)

    def all_blocks(blocks):
        return [blocks[name] for name in pairs] + [blocks["other", name] for name in pairs]

    labels = jnp.arange(groups, dtype=jnp.int32)
    chosen = expert_ids[None, :, :] == labels[:, None, None]
    routed = jnp.any(chosen, axis=2)
    gate = jnp.sum(jnp.where(chosen, gate_weights[None], 0.0), axis=2)
    earlier = jnp.triu(jnp.ones((tok_count, tok_count), jnp.bfloat16), 1)
    rank = jnp.dot(routed.astype(jnp.bfloat16), earlier, preferred_element_type=jnp.float32)
    slot = jnp.where(routed, rank + (me * cap).astype(jnp.float32), -1.0)
    listed = [gate, slot] + [shifted(slot, i) for i in shifts]
    halves = [columns(tokens, (replica + i) % replicas) for i in range(replicas)]
    work["halves"] = jnp.concatenate(
        [halves[0]] + [shifted(halves[i], i) for i in shifts], axis=0
    )
    saved_rows = saved.reshape(slot_total, 2 * hidden_units)
    gate_pre, up_pre = saved_rows[:, :hidden_units], saved_rows[:, hidden_units:]
    saved_pieces = split_rows(saved_rows, 2)

    grads = {("a", 0): out_grad}
    grads["b", 0] = exchange(grads, ("a", 0))[0]["other", ("a", 0)]
    for step in range(1, far + 1):
        moved = [hop(grads, "a", step)]
        if step < far:
            hop(grads, "b", step)
        if step == 2:
            moved += [(work, key) for key in ("js", "leaving", "halves")]
        elif step == 3:
            moved += [exchange(grads, (kind, 1)) for kind in "ab"]
        elif step == far:
            moved += [exchange(grads, (kind, 2)) for kind in "ab"]
            work["gates"] = work["info"][:, 0, :].reshape(1, -1)
            all_slots = jnp.swapaxes(work["info"][:, 1:, :], 0, 1).astype(jnp.int32)
            work["slots"] = all_slots.reshape(replicas, -1)
            work["own"] = all_slots[0]
            moved += [(work, key) for key in ("gates", "slots", "own")]
            moved += send(saved_pieces, "saved", 0)
        together(*moved)
        if step == 1:
            work["info"] = lax.all_to_all(
                jnp.stack(listed, axis=1), AXIS, split_axis=0, concat_axis=0, tiled=True
            )
        elif step == far - 1:
            together((work, "info"), (grads, ("b", step)))
    held = {("a", 0): work["halves"]}
    held["b", 0] = exchange(held, ("a", 0))[0]["other", ("a", 0)]
    together((held, ("a", 0)), (grads, ("b", far - 1)))
    for step in range(1, far + 1):
        hop(held, "a", step)
        if step < far:
            hop(held, "b", step)
    for blocks in (grads, held):
        for name in pairs:
            if ("other", name) not in blocks:
                exchange(blocks, name)
    js, gates, all_slots = work["js"], work["gates"], work["slots"]

    def pre_grads(hidden_grad, gate_pre, up_pre):
        gate_pre, up_pre = gate_pre.astype(jnp.float32), up_pre.astype(jnp.float32)
        sigmoid_gate = jax.nn.sigmoid(gate_pre)
        activated = gate_pre * sigmoid_gate
        gate_grad = hidden_grad * up_pre * sigmoid_gate * (1.0 + gate_pre * (1.0 - sigmoid_gate))
        up_grad = hidden_grad * activated
        hidden = activated * up_pre
        return [value.astype(jnp.bfloat16) for value in (gate_grad, up_grad, hidden)]

    def down_part(owner):
        return lax.dot_general(
            hidden, columns(s, owner), CONTRACT_FIRST, preferred_element_type=jnp.float32
        )

    s = gather_rows(js, all_slots[:1], gates, all_blocks(grads), slot_total, cap, True)[0]
    hidden_grad = lax.dot_general(s, w_down[0], CONTRACT_LAST, preferred_element_type=jnp.float32)
    gate_grad, up_grad, hidden = pre_grads(hidden_grad, gate_pre, up_pre)
    hidden_pieces = split_rows(hidden_grad.astype(jnp.bfloat16), 2)
    work["pre_grad"] = jnp.concatenate([gate_grad, up_grad], axis=1)
    together((work, "pre_grad"), *send(saved_pieces, "saved", 1))
    slot_grads = lax.dot_general(
        work["pre_grad"], w_in[0], CONTRACT_LAST, preferred_element_type=jnp.float32
    ).astype(jnp.bfloat16)
    parts = scatter_rows(work["leaving"], work["own"], slot_grads, cap, sizes)
    kept, sent = parts[::CORES], parts[1::CORES]
    others = [down_part((replica + i) % replicas).astype(jnp.bfloat16) for i in shifts]
    swapped = [lax.ppermute(value, AXIS, swap) for value in sent]
    moved = [(swapped, 0), (held, ("a", far)), (held, ("b", far - 1))]
    together(*moved, *send(hidden_pieces, "hidden", 0))

    def total(name):
        g, row = 0, leaving.index(name)
        while row >= sizes[g]:
            g, row = g + 1, row - sizes[g]
        values = [
            lax.slice_in_dim(x[g], row * tok_count, (row + 1) * tok_count) for x in (kept, swapped)
        ]
        return values[0].astype(jnp.float32) + values[1].astype(jnp.float32)

    def over_slots(values):
        return sum(
            lax.dot_general(values[i], x[i], CONTRACT_FIRST, preferred_element_type=jnp.float32)
            for i in range(replicas)
        )

    down_pieces = [split_rows(other, 3) for other in others]
    sums = {}
    for n, (kind, steps) in enumerate(leaving[:-1]):
        value = total((kind, steps))
        if (kind, steps + 1) in sums:
            value = value + sums[kind, steps + 1].astype(jnp.float32)
        last = (kind, steps) == ("b", 1)
        sums[kind, steps] = lax.ppermute(
            value.astype(jnp.bfloat16), AXIS, across if last else along
        )
        if n == 1:
            together((sums, (kind, steps)), *send(hidden_pieces, "hidden", 1))
        elif n in (3, 5):
            for i in shifts:
                came["down", n // 2 - 1, i] = shifted(down_pieces[i - 1][n // 2 - 1], i)
                together((sums, (kind, steps)), (came, ("down", n // 2 - 1, i)))
    for i in shifts:
        came["down", 2, i] = shifted(down_pieces[i - 1][2], i)

    x = gather_rows(
        js, all_slots, all_slots.astype(jnp.float32), all_blocks(held), slot_total, cap, False
    )
    gate_grads, up_grads = [gate_grad], [up_grad]
    for i in shifts:
        other = whole("saved", 2, i)
        other = pre_grads(
            whole("hidden", 2, i).astype(jnp.float32),
            other[:, :hidden_units],
            other[:, hidden_units:],
        )
        gate_grads.append(other[0])
        up_grads.append(other[1])
    grad_down = down_part(replica)
    for i in shifts:
        grad_down = grad_down + whole("down", 3, i).astype(jnp.float32)
    weight = jnp.concatenate([over_slots(gate_grads), over_slots(up_grads), grad_down], axis=0)
    trained_flag = jnp.any(trained == me).astype(jnp.float32)
    work["weight"] = (weight * trained_flag).astype(jnp.bfloat16)
    together((work, "weight"), (sums, ("a", 1)))
    in_grad = total(("a", 0)) + sums["a", 1].astype(jnp.float32)
    if far > 1:
        in_grad = in_grad + sums["b", 1].astype(jnp.float32)
    return in_grad.astype(jnp.bfloat16), work["weight"].T[None]


def solution(mesh):
    return jax.shard_map(
        per_device,
        mesh=mesh,
        in_specs=(
            P(("dp", "expert"), None),
            P(("dp", "expert"), None),
            P(("dp", "expert"), None),
            P(("dp", "expert"), None),
            P(),
            P("expert", None, None),
            P("expert", None, None),
            P("dp", "expert", None, None),
        ),
        out_specs=(P(("dp", "expert"), None), P("expert", "dp", None)),
        check_vma=False,
    )
```

time: 237 us -> 197 us (0.83)
  waiting for transfers between devices: 109 us -> 59.8 us
  starting transfers between devices: 40.2 us -> 51.1 us
  other arithmetic: 20.9 us -> 13.6 us
  matrix products: 27.1 us -> 31.8 us
  Pallas kernels: 17.4 us -> 21.6 us
  local copies, waits for them, and re-layouts: 19 us -> 16.6 us
    ppermute x4 -> x9, waiting for transfers between devices: 45.4 us -> 16.8 us  [shifted(): lax.ppermute(value, 'dp', [(r, (r + shift) % replicas) for r in range(rep...]
    ppermute x45 -> x40, waiting for transfers between devices: 64.1 us -> 38.9 us  [the longest x14 20.1 us: hop(): blocks[kind, step] = lax.ppermute(blocks[kind, step - 1], AXIS, along)]
    unnamed x90 -> x58, local copies, waits for them, and re-layouts: 16.5 us -> 3.69 us
    ppermute x4 -> x9, starting transfers between devices: 4.92 us -> 11.6 us  [shifted(): lax.ppermute(value, 'dp', [(r, (r + shift) % replicas) for r in range(rep...]
    slice x0 -> x5, local copies, waits for them, and re-layouts: none -> 5.6 us  [the longest x4 5 us: split_rows(): return [value[a:b] for a, b in zip([0] + ends[:-1], ends)]]
    ppermute x45 -> x40, starting transfers between devices: 29.5 us -> 34.5 us  [the longest x14 22.5 us: hop(): blocks[kind, step] = lax.ppermute(blocks[kind, step - 1], AXIS, along)]
    broadcast_in_dim x1 -> x0, other arithmetic: 4.81 us -> none  [per_device(): return (in_grad, weight.T[None])]
    all_to_all x1, waiting for transfers between devices: 0.01 us -> 4.12 us  [per_device(): lax.all_to_all(jnp.stack(listed, axis=1), AXIS, split_axis=0, concat_axis...]
  transfers between devices with their start and end apart: 50 -> 50, of which waited for: 15 -> 14; matrix products, arithmetic and copies ran while one was open for 20% -> 30% of each run, Pallas kernels for 7% -> 11%
where the time goes in v1:
time: 197 us; the launch traced here: 196 us
  waiting for transfers between devices  59.8 us (30%)
  starting transfers between devices  51.1 us (26%)
  matrix products  31.8 us (16%)
  Pallas kernels  21.6 us (11%)
  local copies, waits for them, and re-layouts  16.6 us (8%)
  other arithmetic  13.6 us (7%)
    ppermute x14, starting transfers between devices, hop(): blocks[kind, step] = lax.ppermute(blocks[kind, step - 1], AXIS, along)  22.5 us
    ppermute x14, waiting for transfers between devices, hop(): blocks[kind, step] = lax.ppermute(blocks[kind, step - 1], AXIS, along)  20.1 us
    ppermute x7, waiting for transfers between devices, per_device(): lax.ppermute(value.astype(jnp.bfloat16), AXIS, across if last else along)  18.8 us
    ppermute x9, waiting for transfers between devices, shifted(): lax.ppermute(value, 'dp', [(r, (r + shift) % replicas) for r in range(rep...  16.8 us
    pallas_call x2, Pallas kernels, gather_rows(): pl.pallas_call(functools.partial(gather_kernel, count=count, planes=plane...  15.2 us
    dot_general x4, matrix products, over_slots(): lax.dot_general(values[i], x[i], CONTRACT_FIRST, preferred_element_type=j...  11.9 us
    ppermute x9, starting transfers between devices, shifted(): lax.ppermute(value, 'dp', [(r, (r + shift) % replicas) for r in range(rep...  11.6 us
    ppermute x7, starting transfers between devices, per_device(): lax.ppermute(value.astype(jnp.bfloat16), AXIS, across if last else along)  7.64 us
  transfers between devices with their start and end apart: 50, of which 14 were waited for; matrix products, arithmetic and copies ran while one was open for 30% of the time, Pallas kernels for 11%

profile of v1, /device:TPU:0, one launch (start us, length us, event | category | flops | bytes accessed | tf_op | source)
XLA Modules:
  0.0 196.4 jit_solution(1493536130965972094)
XLA Ops:
  1.2 2.6 %collective-permute-start = (bf16[128,2048]{1,0:T(8,128)(2,1)}, bf16[128,2048]{1,0:T(8,128)(2,1)}, u32[]{:S(2)}, u32[]{:S(2)}) collective-permute-start(bf16[128,2048]{1,0:T(8,128)(2,1)} %refs_0_.1), channel_id=1, source_target_pairs={{0,4},{1,3},{2,0},{3,7},{4,8},{5,1},{6,2},{7,11},{8,12},{9,5},{10,... | collective-permute-start | bytes 1572872 | tf_op jit(solution)/shard_map/ppermute | solution.py:257
  11.2 2.1 %collective-permute-start.1 = (bf16[128,2048]{1,0:T(8,128)(2,1)}, bf16[128,2048]{1,0:T(8,128)(2,1)}, u32[]{:S(2)}, u32[]{:S(2)}) collective-permute-start(bf16[128,2048]{1,0:T(8,128)(2,1)} %collective-permute-done.refs_1_), channel_id=1, source_target_pairs={{0,4},{1,3},{2,0},{3,7},{4,8},{5,1},{6,2},{7,11},{8,12},{9,5},{10,... | collective-permute-start | bytes 1572872 | tf_op jit(solution)/shard_map/ppermute | solution.py:257
  13.3 3.5 %collective-permute-done.6.refs_2_ = bf16[128,2048]{1,0:T(8,128)(2,1)} collective-permute-done((bf16[128,2048]{1,0:T(8,128)(2,1)S(1)}, bf16[128,2048]{1,0:T(8,128)(2,1)}, u32[]{:S(2)}, u32[]{:S(2)}) %collective-permute-start.6) | collective-permute-done | bytes 524320 | tf_op jit(solution)/shard_map/ppermute | solution.py:257
  16.8 2.1 %collective-permute-start.10 = (bf16[128,2048]{1,0:T(8,128)(2,1)}, bf16[128,2048]{1,0:T(8,128)(2,1)}, u32[]{:S(2)}, u32[]{:S(2)}) collective-permute-start(bf16[128,2048]{1,0:T(8,128)(2,1)} %collective-permute-done.6.refs_2_), channel_id=1, source_target_pairs={{0,4},{1,3},{2,0},{3,7},{4,8},{5,1},{6,2},{7,11},{8,12},{9,5},{10,... | collective-permute-start | bytes 1572872 | tf_op jit(solution)/shard_map/ppermute | solution.py:257
  25.4 2.7 %collective-permute-done.10.refs_4_ = bf16[128,2048]{1,0:T(8,128)(2,1)} collective-permute-done((bf16[128,2048]{1,0:T(8,128)(2,1)}, bf16[128,2048]{1,0:T(8,128)(2,1)}, u32[]{:S(2)}, u32[]{:S(2)}) %collective-permute-start.10) | collective-permute-done | bytes 524320 | tf_op jit(solution)/shard_map/ppermute | solution.py:257
  28.1 2.1 %collective-permute-start.13 = (bf16[128,2048]{1,0:T(8,128)(2,1)}, bf16[128,2048]{1,0:T(8,128)(2,1)}, u32[]{:S(2)}, u32[]{:S(2)}) collective-permute-start(bf16[128,2048]{1,0:T(8,128)(2,1)} %collective-permute-done.10.refs_4_), channel_id=1, source_target_pairs={{0,4},{1,3},{2,0},{3,7},{4,8},{5,1},{6,2},{7,11},{8,12},{9,5},{10,... | collective-permute-start | bytes 1572872 | tf_op jit(solution)/shard_map/ppermute | solution.py:257
  30.2 3.1 %slice_bitcast_fusion.6 = (bf16[392,1408]{1,0:T(8,128)(2,1)}, bf16[392,1408]{1,0:T(8,128)(2,1)}) fusion(bf16[1,1,784,1408]{3,2,1,0:T(8,128)(2,1)} %param.17), kind=kLoop, calls=%fused_computation.53 | loop fusion | bytes 4415488 | tf_op jit(solution)/shard_map/slice | solution.py:37
  35.4 4.9 %all-to-all-start = ((f32[16,3,128]{2,1,0:T(4,128)}), f32[16,3,128]{2,1,0:T(4,128)S(1)}, u32[]{:S(2)}, u32[]{:S(2)}) async-start(f32[16,3,128]{2,1,0:T(4,128)} %copy.18), calls=%async_computation | async-start | bytes 65536 | tf_op jit(solution)/shard_map/all_to_all | solution.py:303
  42.8 4.1 %all-to-all-done = f32[16,3,128]{2,1,0:T(4,128)S(1)} async-done(((f32[16,3,128]{2,1,0:T(4,128)}), f32[16,3,128]{2,1,0:T(4,128)S(1)}, u32[]{:S(2)}, u32[]{:S(2)}) %all-to-all-start) | async-done | bytes 24608 | tf_op jit(solution)/shard_map/all_to_all | solution.py:303
  48.2 10.9 %collective-permute-done.14 = bf16[392,1408]{1,0:T(8,128)(2,1)} collective-permute-done((bf16[392,1408]{1,0:T(8,128)(2,1)}, bf16[392,1408]{1,0:T(8,128)(2,1)}, u32[]{:S(2)}, u32[]{:S(2)}) %collective-permute-start.14) | collective-permute-done | bytes 1103904 | tf_op jit(solution)/shard_map/ppermute | solution.py:236
  64.3 4.2 %collective-permute-done.22.refs_2_ = bf16[256,1024]{1,0:T(8,128)(2,1)} collective-permute-done((bf16[256,1024]{1,0:T(8,128)(2,1)}, bf16[256,1024]{1,0:T(8,128)(2,1)}, u32[]{:S(2)}, u32[]{:S(2)}) %collective-permute-start.22) | collective-permute-done | bytes 524320 | tf_op jit(solution)/shard_map/ppermute | solution.py:257
  68.9 5.3 %collective-permute-done.20.refs_1_ = bf16[256,1024]{1,0:T(8,128)(2,1)} collective-permute-done((bf16[256,1024]{1,0:T(8,128)(2,1)S(1)}, bf16[256,1024]{1,0:T(8,128)(2,1)}, u32[]{:S(2)}, u32[]{:S(2)}) %collective-permute-start.20) | collective-permute-done | bytes 524320 | tf_op jit(solution)/shard_map/ppermute | solution.py:257
  74.5 7.2 %gather_rows.2 = bf16[1,784,2048]{2,1,0:T(8,128)(2,1)} custom-call(s32[16]{0:T(128)} %get-tuple-element.45.js, s32[1,2048]{1,0:T(1,128)} %slice.106.slot_ref, f32[1,2048]{1,0:T(1,128)} %slice_bitcast_fusion.9.gate_ref, bf16[128,2048]{1,0:T(8,128)(2,1)} %refs_0_.1, bf16[128,2048]{1,0:T(8,128)(2,1)} %collective-permute-done.refs_1_, ...), custom_call_target="tpu_custom_call" | custom-call | bytes 23199744 | tf_op jit(solution)/shard_map/gather_rows/pallas_call | solution.py:101
  81.8 6.6 %fusion.11 = (bf16[784,704]{1,0:T(8,128)(2,1)S(1)}, bf16[784,704]{1,0:T(8,128)(2,1)S(1)}, bf16[784,704]{1,0:T(8,128)(2,1)}) fusion(bf16[784,1408]{1,0:T(8,128)(2,1)S(1)} %bitcast.60, bf16[1,704,2048]{2,1,0:T(8,128)(2,1)S(1)} %copy-done, bf16[1,784,2048]{2,1,0:T(8,128)(2,1)} %gather_rows.2), kind=kOutput, calls=%fused_computation.21 | convolution fusion | flops 2269560832 | bytes 11614208 | tf_op jit(solution)/shard_map/dot_general | solution.py:336
  91.0 6.6 %fusion.3.grad_ref = bf16[784,2048]{1,0:T(8,128)(2,1)} fusion(bf16[784,1408]{1,0:T(8,128)(2,1)S(1)} %pad_maximum_fusion, bf16[1,2048,1408]{2,1,0:T(8,128)(2,1)S(1)} %bitcast.70), kind=kOutput, calls=%fused_computation.10 | convolution fusion | flops 4523065344 | bytes 11186176 | tf_op jit(solution)/shard_map/dot_general | solution.py:341
  97.7 6.5 %scatter_rows.1 = (bf16[128,2048]{1,0:T(8,128)(2,1)}, bf16[128,2048]{1,0:T(8,128)(2,1)}, bf16[256,2048]{1,0:T(8,128)(2,1)}, bf16[256,2048]{1,0:T(8,128)(2,1)}, b...) custom-call(s32[16]{0:T(128)} %get-tuple-element.40.js, s32[16,128]{1,0:T(8,128)} %slice_bitcast_fusion.8.slot_ref, ...), custom_call_target="tpu_custom_call" | custom-call | flops 536870912 | bytes 23199744 | tf_op jit(solution)/shard_map/scatter_rows/pallas_call | solution.py:163
  104.7 2.2 %collective-permute-start.28 = (bf16[256,1024]{1,0:T(8,128)(2,1)}, bf16[256,1024]{1,0:T(8,128)(2,1)}, u32[]{:S(2)}, u32[]{:S(2)}) collective-permute-start(bf16[256,1024]{1,0:T(8,128)(2,1)} %collective-permute-done.24.refs_4_), channel_id=1, source_target_pairs={{0,4},{1,3},{2,0},{3,7},{4,8},{5,1},{6,2},{7,11},{8,12},{9,5},{10,... | collective-permute-start | bytes 1572872 | tf_op jit(solution)/shard_map/ppermute | solution.py:257
  111.9 2.3 %collective-permute-done.28.refs_6_ = bf16[256,1024]{1,0:T(8,128)(2,1)} collective-permute-done((bf16[256,1024]{1,0:T(8,128)(2,1)}, bf16[256,1024]{1,0:T(8,128)(2,1)}, u32[]{:S(2)}, u32[]{:S(2)}) %collective-permute-start.28) | collective-permute-done | bytes 524320 | tf_op jit(solution)/shard_map/ppermute | solution.py:257
  114.2 2.4 %constant_dynamic-update-slice_fusion.1 = bf16[784,1408]{1,0:T(8,128)(2,1)} fusion(bf16[392,1408]{1,0:T(8,128)(2,1)} %collective-permute-done.14), kind=kLoop, calls=%fused_computation.81 | loop fusion | bytes 2207744
  117.2 5.1 %collective-permute-done.29 = bf16[392,704]{1,0:T(8,128)(2,1)} collective-permute-done((bf16[392,704]{1,0:T(8,128)(2,1)S(1)}, bf16[392,704]{1,0:T(8,128)(2,1)}, u32[]{:S(2)}, u32[]{:S(2)}) %collective-permute-start.29) | collective-permute-done | bytes 551968 | tf_op jit(solution)/shard_map/ppermute | solution.py:236
  125.6 3.4 %convolution_convert_fusion = bf16[704,1024]{1,0:T(8,128)(2,1)S(1)} fusion(bf16[1,784,2048]{2,1,0:T(8,128)(2,1)} %gather_rows.2, s32[]{:T(128)S(6)} %select_n.43, bf16[784,1408]{1,0:T(8,128)(2,1)S(1)} %bitcast.61), kind=kOutput, calls=%fused_computation.39 | convolution fusion | flops 1135501312 | bytes 5455876 | tf_op jit(solution)/shard_map/dot_general | solution.py:331
  129.9 4.4 %collective-permute-done.45 = bf16[128,2048]{1,0:T(8,128)(2,1)S(1)} collective-permute-done((bf16[128,2048]{1,0:T(8,128)(2,1)S(1)}, bf16[128,2048]{1,0:T(8,128)(2,1)S(1)}, u32[]{:S(2)}, u32[]{:S(2)}) %collective-permute-start.45) | collective-permute-done | bytes 524320 | tf_op jit(solution)/shard_map/ppermute | solution.py:373
  135.8 2.6 %add_convert_fusion.3 = (bf16[128,2048]{1,0:T(8,128)(2,1)}, bf16[128,2048]{1,0:T(8,128)(2,1)}) fusion(bf16[128,2048]{1,0:T(8,128)(2,1)S(1)} %collective-permute-done.45, bf16[256,2048]{1,0:T(8,128)(2,1)} %collective-permute-done.37, bf16[256,2048]{1,0:T(8,128)(2,1)S(1)} %copy-done.13), kind=kLoop, calls=%fused_computation.60 | loop fusion | flops 2621440 | bytes 3670016 | tf_op jit(solution)/shard_map/convert_element_type | solution.py:374
  140.4 2.3 %constant_dynamic-update-slice_fusion = bf16[784,1408]{1,0:T(8,128)(2,1)} fusion(bf16[784,1408]{1,0:T(8,128)(2,1)} %constant_dynamic-update-slice_fusion.1, bf16[392,1408]{1,0:T(8,128)(2,1)} %collective-permute-done.18), kind=kLoop, calls=%fused_computation.80 | loop fusion | bytes 2207744 | tf_op jit(solution)/shard_map/concatenate | solution.py:254
  145.7 7.9 %gather_rows.3 = bf16[2,784,1024]{2,1,0:T(8,128)(2,1)} custom-call(s32[16]{0:T(128)} %get-tuple-element.45.js, s32[2,2048]{1,0:T(2,128)} %bitcast.65, f32[2,2048]{1,0:T(2,128)} %convert_element_type.164.gate_ref, bf16[256,1024]{1,0:T(8,128)(2,1)} %copy-done.7, bf16[256,1024]{1,0:T(8,128)(2,1)} %collective-permute-done.20.refs_1_, ...), custom_call_target="tpu_custom_call" | custom-call | bytes 23199744 | tf_op jit(solution)/shard_map/gather_rows/pallas_call | solution.py:101
  155.7 4.9 %fusion.30 = f32[704,1024]{1,0:T(8,128)S(1)} fusion(bf16[2,784,1024]{2,1,0:T(8,128)(2,1)} %gather_rows.3, bf16[784,1408]{1,0:T(8,128)(2,1)} %constant_dynamic-update-slice_fusion, bf16[392,704]{1,0:T(8,128)(2,1)} %collective-permute-done.39, bf16[392,704]{1,0:T(8,128)(2,1)} %collective-permute-done.29), kind=kOutput, calls=%fused_computation.47 | convolution fusion | flops 1139195904 | bytes 8101888 | tf_op jit(solution)/shard_map/dot_general | solution.py:362
  160.6 3.0 %collective-permute-done.46 = bf16[128,2048]{1,0:T(8,128)(2,1)S(1)} collective-permute-done((bf16[128,2048]{1,0:T(8,128)(2,1)}, bf16[128,2048]{1,0:T(8,128)(2,1)S(1)}, u32[]{:S(2)}, u32[]{:S(2)}) %collective-permute-start.46) | collective-permute-done | bytes 524320 | tf_op jit(solution)/shard_map/ppermute | solution.py:373
  168.7 3.5 %fusion.29 = f32[704,1024]{1,0:T(8,128)S(1)} fusion(bf16[2,784,1024]{2,1,0:T(8,128)(2,1)S(1)} %copy-done.3, bf16[784,1408]{1,0:T(8,128)(2,1)} %constant_dynamic-update-slice_fusion, bf16[392,704]{1,0:T(8,128)(2,1)} %collective-permute-done.39, bf16[392,704]{1,0:T(8,128)(2,1)} %collective-permute-done.29), kind=kOutput, calls=%fused_computation.46 | convolution fusion | flops 1136436224 | bytes 6897664 | tf_op jit(solution)/shard_map/dot_general | solution.py:362
  172.2 7.8 %collective-permute-done.40 = bf16[128,2048]{1,0:T(8,128)(2,1)S(1)} collective-permute-done((bf16[128,2048]{1,0:T(8,128)(2,1)S(1)}, bf16[128,2048]{1,0:T(8,128)(2,1)S(1)}, u32[]{:S(2)}, u32[]{:S(2)}) %collective-permute-start.40) | collective-permute-done | bytes 524320 | tf_op jit(solution)/shard_map/ppermute | solution.py:373
  185.7 3.6 %collective-permute-done.42 = bf16[128,2048]{1,0:T(8,128)(2,1)S(1)} collective-permute-done((bf16[128,2048]{1,0:T(8,128)(2,1)S(1)}, bf16[128,2048]{1,0:T(8,128)(2,1)S(1)}, u32[]{:S(2)}, u32[]{:S(2)}) %collective-permute-start.42) | collective-permute-done | bytes 524320 | tf_op jit(solution)/shard_map/ppermute | solution.py:373
  189.3 3.2 %convert_add_fusion = f32[704,1024]{1,0:T(8,128)S(1)} fusion(bf16[1,784,2048]{2,1,0:T(8,128)(2,1)S(1)} %copy-done.2, s32[]{:T(128)S(6)} %select_n.47, bf16[240,1024]{1,0:T(8,128)(2,1)S(1)} %collective-permute-done.44, bf16[232,1024]{1,0:T(8,128)(2,1)} %collective-permute-done.43, bf16[232,1024]{1,0:T(8,128)(2,1)} %collective-permute-done.41, ...), kind=kOutput, calls=%fused_computation.18 | convolution fusion | flops 1139826688 | bytes 8339460 | tf_op jit(solution)/shard_map/dot_general | solution.py:331
  192.5 2.7 %fusion = bf16[2112,1024]{1,0:T(8,128)(2,1)} fusion(f32[704,1024]{1,0:T(8,128)S(1)} %convert_add_fusion, f32[704,1024]{1,0:T(8,128)S(1)} %convolution_add_fusion, f32[704,1024]{1,0:T(8,128)S(1)} %convolution_add_fusion.1, f32[]{:T(128)S(6)} %convert_element_type.185), kind=kLoop, calls=%fused_computation.1 | loop fusion | flops 8650752 | bytes 12976132 | tf_op jit(solution)/shard_map/convert_element_type | solution.py:403
  (165 shorter events, 58.7 us)
Async XLA Ops:
  3.8 13.0 %collective-permute-start.6 = (bf16[128,2048]{1,0:T(8,128)(2,1)S(1)}, bf16[128,2048]{1,0:T(8,128)(2,1)}, u32[]{:S(2)}, u32[]{:S(2)}) collective-permute-start(bf16[128,2048]{1,0:T(8,128)(2,1)S(1)} %collective-permute-done.5.refs_8_), channel_id=1, source_target_pairs={{0,4},{1,3},{2,0},{3,7},{4,8},{5,1},{6,2},{7,11},{8,12},{9,5},{10,... | collective-permute-start | bytes 1572872 | tf_op jit(solution)/shard_map/ppermute | solution.py:257
  7.7 14.8 %collective-permute-start.2 = (bf16[128,1024]{1,0:T(8,128)(2,1)}, bf16[128,1024]{1,0:T(8,128)(2,1)}, u32[]{:S(2)}, u32[]{:S(2)}) collective-permute-start(bf16[128,1024]{1,0:T(8,128)(2,1)} %get-tuple-element.94), channel_id=1, source_target_pairs={{0,16},{16,0},{1,17},{17,1},{2,18},{18,2},{3,19},{19,3},{4,20},{20... | collective-permute-start | bytes 786440 | tf_op jit(solution)/shard_map/ppermute | solution.py:236
  19.7 13.5 %collective-permute-start.12 = (f32[16,128]{1,0:T(8,128)S(1)}, f32[16,128]{1,0:T(8,128)S(1)}, u32[]{:S(2)}, u32[]{:S(2)}) collective-permute-start(f32[16,128]{1,0:T(8,128)S(1)} %fusion.35), channel_id=1, source_target_pairs={{0,16},{16,0},{1,17},{17,1},{2,18},{18,2},{3,19},{19,3},{4,20},{20... | collective-permute-start | bytes 24584 | tf_op jit(solution)/shard_map/ppermute | solution.py:236
  23.6 16.7 %collective-permute-start.4 = (bf16[128,2048]{1,0:T(8,128)(2,1)}, bf16[128,2048]{1,0:T(8,128)(2,1)}, u32[]{:S(2)}, u32[]{:S(2)}) collective-permute-start(bf16[128,2048]{1,0:T(8,128)(2,1)} %collective-permute-done.refs_1_), channel_id=1, source_target_pairs={{0,1},{1,0},{2,3},{3,2},{4,5},{5,4},{6,7},{7,6},{8,9},{9,8},{10,11... | collective-permute-start | bytes 1572872 | tf_op jit(solution)/shard_map/ppermute | solution.py:261
  23.7 17.1 %collective-permute-start.3 = (bf16[128,2048]{1,0:T(8,128)(2,1)}, bf16[128,2048]{1,0:T(8,128)(2,1)}, u32[]{:S(2)}, u32[]{:S(2)}) collective-permute-start(bf16[128,2048]{1,0:T(8,128)(2,1)} %collective-permute-done.1.refs_3_), channel_id=1, source_target_pairs={{0,4},{1,3},{2,0},{3,7},{4,8},{5,1},{6,2},{7,11},{8,12},{9,5},{10,... | collective-permute-start | bytes 1572872 | tf_op jit(solution)/shard_map/ppermute | solution.py:257
  25.3 15.6 %collective-permute-start.7 = (bf16[128,2048]{1,0:T(8,128)(2,1)}, bf16[128,2048]{1,0:T(8,128)(2,1)}, u32[]{:S(2)}, u32[]{:S(2)}) collective-permute-start(bf16[128,2048]{1,0:T(8,128)(2,1)} %collective-permute-done.6.refs_2_), channel_id=1, source_target_pairs={{0,1},{1,0},{2,3},{3,2},{4,5},{5,4},{6,7},{7,6},{8,9},{9,8},{10,11... | collective-permute-start | bytes 1572872 | tf_op jit(solution)/shard_map/ppermute | solution.py:261
  28.1 14.8 %collective-permute-start.13 = (bf16[128,2048]{1,0:T(8,128)(2,1)}, bf16[128,2048]{1,0:T(8,128)(2,1)}, u32[]{:S(2)}, u32[]{:S(2)}) collective-permute-start(bf16[128,2048]{1,0:T(8,128)(2,1)} %collective-permute-done.10.refs_4_), channel_id=1, source_target_pairs={{0,4},{1,3},{2,0},{3,7},{4,8},{5,1},{6,2},{7,11},{8,12},{9,5},{10,... | collective-permute-start | bytes 1572872 | tf_op jit(solution)/shard_map/ppermute | solution.py:257
  33.2 25.8 %collective-permute-start.14 = (bf16[392,1408]{1,0:T(8,128)(2,1)}, bf16[392,1408]{1,0:T(8,128)(2,1)}, u32[]{:S(2)}, u32[]{:S(2)}) collective-permute-start(bf16[392,1408]{1,0:T(8,128)(2,1)} %get-tuple-element.86), channel_id=1, source_target_pairs={{0,16},{16,0},{1,17},{17,1},{2,18},{18,2},{3,19},{19,3},{4,20},{20... | collective-permute-start | bytes 3311624 | tf_op jit(solution)/shard_map/ppermute | solution.py:236
  40.3 19.1 %collective-permute-start.9 = (bf16[128,2048]{1,0:T(8,128)(2,1)}, bf16[128,2048]{1,0:T(8,128)(2,1)}, u32[]{:S(2)}, u32[]{:S(2)}) collective-permute-start(bf16[128,2048]{1,0:T(8,128)(2,1)} %collective-permute-done.1.refs_3_), channel_id=1, source_target_pairs={{0,1},{1,0},{2,3},{3,2},{4,5},{5,4},{6,7},{7,6},{8,9},{9,8},{10,11... | collective-permute-start | bytes 1572872 | tf_op jit(solution)/shard_map/ppermute | solution.py:261
  40.8 18.3 %collective-permute-start.21 = (bf16[256,1024]{1,0:T(8,128)(2,1)S(1)}, bf16[256,1024]{1,0:T(8,128)(2,1)}, u32[]{:S(2)}, u32[]{:S(2)}) collective-permute-start(bf16[256,1024]{1,0:T(8,128)(2,1)S(1)} %pad_maximum_fusion.4.refs_0_), channel_id=1, source_target_pairs={{0,1},{1,0},{2,3},{3,2},{4,5},{5,4},{6,7},{7,6},{8,9},{9,8},{10,11... | collective-permute-start | bytes 1572872 | tf_op jit(solution)/shard_map/ppermute | solution.py:261
  40.9 18.5 %collective-permute-start.8 = (bf16[128,2048]{1,0:T(8,128)(2,1)}, bf16[128,2048]{1,0:T(8,128)(2,1)}, u32[]{:S(2)}, u32[]{:S(2)}) collective-permute-start(bf16[128,2048]{1,0:T(8,128)(2,1)} %collective-permute-done.3.refs_5_), channel_id=1, source_target_pairs={{0,4},{1,3},{2,0},{3,7},{4,8},{5,1},{6,2},{7,11},{8,12},{9,5},{10,... | collective-permute-start | bytes 1572872 | tf_op jit(solution)/shard_map/ppermute | solution.py:257
  42.8 16.6 %collective-permute-start.11 = (bf16[128,2048]{1,0:T(8,128)(2,1)}, bf16[128,2048]{1,0:T(8,128)(2,1)}, u32[]{:S(2)}, u32[]{:S(2)}) collective-permute-start(bf16[128,2048]{1,0:T(8,128)(2,1)} %collective-permute-done.10.refs_4_), channel_id=1, source_target_pairs={{0,1},{1,0},{2,3},{3,2},{4,5},{5,4},{6,7},{7,6},{8,9},{9,8},{10,11... | collective-permute-start | bytes 1572872 | tf_op jit(solution)/shard_map/ppermute | solution.py:261
  59.4 14.8 %collective-permute-start.20 = (bf16[256,1024]{1,0:T(8,128)(2,1)S(1)}, bf16[256,1024]{1,0:T(8,128)(2,1)}, u32[]{:S(2)}, u32[]{:S(2)}) collective-permute-start(bf16[256,1024]{1,0:T(8,128)(2,1)S(1)} %pad_maximum_fusion.4.refs_0_), channel_id=1, source_target_pairs={{0,4},{1,3},{2,0},{3,7},{4,8},{5,1},{6,2},{7,11},{8,12},{9,5},{10,... | collective-permute-start | bytes 1572872 | tf_op jit(solution)/shard_map/ppermute | solution.py:257
  61.2 13.3 %collective-permute-start.16 = (bf16[128,2048]{1,0:T(8,128)(2,1)}, bf16[128,2048]{1,0:T(8,128)(2,1)}, u32[]{:S(2)}, u32[]{:S(2)}) collective-permute-start(bf16[128,2048]{1,0:T(8,128)(2,1)} %collective-permute-done.13.refs_6_), channel_id=1, source_target_pairs={{0,1},{1,0},{2,3},{3,2},{4,5},{5,4},{6,7},{7,6},{8,9},{9,8},{10,11... | collective-permute-start | bytes 1572872 | tf_op jit(solution)/shard_map/ppermute | solution.py:261
  62.8 27.1 %collective-permute-start.18 = (bf16[392,1408]{1,0:T(8,128)(2,1)}, bf16[392,1408]{1,0:T(8,128)(2,1)}, u32[]{:S(2)}, u32[]{:S(2)}) collective-permute-start(bf16[392,1408]{1,0:T(8,128)(2,1)} %get-tuple-element.85), channel_id=1, source_target_pairs={{0,16},{16,0},{1,17},{17,1},{2,18},{18,2},{3,19},{19,3},{4,20},{20... | collective-permute-start | bytes 3311624 | tf_op jit(solution)/shard_map/ppermute | solution.py:236
  68.6 36.2 %collective-permute-start.24 = (bf16[256,1024]{1,0:T(8,128)(2,1)}, bf16[256,1024]{1,0:T(8,128)(2,1)}, u32[]{:S(2)}, u32[]{:S(2)}) collective-permute-start(bf16[256,1024]{1,0:T(8,128)(2,1)} %collective-permute-done.22.refs_2_), channel_id=1, source_target_pairs={{0,4},{1,3},{2,0},{3,7},{4,8},{5,1},{6,2},{7,11},{8,12},{9,5},{10,... | collective-permute-start | bytes 1572872 | tf_op jit(solution)/shard_map/ppermute | solution.py:257
  74.2 15.7 %collective-permute-start.23 = (bf16[256,1024]{1,0:T(8,128)(2,1)}, bf16[256,1024]{1,0:T(8,128)(2,1)}, u32[]{:S(2)}, u32[]{:S(2)}) collective-permute-start(bf16[256,1024]{1,0:T(8,128)(2,1)} %collective-permute-done.20.refs_1_), channel_id=1, source_target_pairs={{0,4},{1,3},{2,0},{3,7},{4,8},{5,1},{6,2},{7,11},{8,12},{9,5},{10,... | collective-permute-start | bytes 1572872 | tf_op jit(solution)/shard_map/ppermute | solution.py:257
  89.9 18.7 %collective-permute-start.25 = (bf16[256,1024]{1,0:T(8,128)(2,1)}, bf16[256,1024]{1,0:T(8,128)(2,1)}, u32[]{:S(2)}, u32[]{:S(2)}) collective-permute-start(bf16[256,1024]{1,0:T(8,128)(2,1)} %collective-permute-done.23.refs_3_), channel_id=1, source_target_pairs={{0,4},{1,3},{2,0},{3,7},{4,8},{5,1},{6,2},{7,11},{8,12},{9,5},{10,... | collective-permute-start | bytes 1572872 | tf_op jit(solution)/shard_map/ppermute | solution.py:257
  104.2 20.5 %collective-permute-start.37 = (bf16[256,2048]{1,0:T(8,128)(2,1)}, bf16[256,2048]{1,0:T(8,128)(2,1)}, u32[]{:S(2)}, u32[]{:S(2)}) collective-permute-start(bf16[256,2048]{1,0:T(8,128)(2,1)} %get-tuple-element.65), channel_id=1, source_target_pairs={{0,1},{1,0},{2,3},{3,2},{4,5},{5,4},{6,7},{7,6},{8,9},{9,8},{10,11... | collective-permute-start | bytes 3145736 | tf_op jit(solution)/shard_map/ppermute | solution.py:347
  107.0 15.2 %collective-permute-start.29 = (bf16[392,704]{1,0:T(8,128)(2,1)S(1)}, bf16[392,704]{1,0:T(8,128)(2,1)}, u32[]{:S(2)}, u32[]{:S(2)}) collective-permute-start(bf16[392,704]{1,0:T(8,128)(2,1)S(1)} %get-tuple-element.91), channel_id=1, source_target_pairs={{0,16},{16,0},{1,17},{17,1},{2,18},{18,2},{3,19},{19,3},{4,20},{20... | collective-permute-start | bytes 1655816 | tf_op jit(solution)/shard_map/ppermute | solution.py:236
  108.6 13.7 %collective-permute-start.27 = (bf16[256,1024]{1,0:T(8,128)(2,1)}, bf16[256,1024]{1,0:T(8,128)(2,1)}, u32[]{:S(2)}, u32[]{:S(2)}) collective-permute-start(bf16[256,1024]{1,0:T(8,128)(2,1)} %collective-permute-done.25.refs_5_), channel_id=1, source_target_pairs={{0,4},{1,3},{2,0},{3,7},{4,8},{5,1},{6,2},{7,11},{8,12},{9,5},{10,... | collective-permute-start | bytes 1572872 | tf_op jit(solution)/shard_map/ppermute | solution.py:257
  122.3 41.3 %collective-permute-start.19 = (bf16[640,2048]{1,0:T(8,128)(2,1)}, bf16[640,2048]{1,0:T(8,128)(2,1)S(1)}, u32[]{:S(2)}, u32[]{:S(2)}) collective-permute-start(bf16[640,2048]{1,0:T(8,128)(2,1)} %get-tuple-element.58), channel_id=1, source_target_pairs={{0,1},{1,0},{2,3},{3,2},{4,5},{5,4},{6,7},{7,6},{8,9},{9,8},{10,11... | collective-permute-start | bytes 7864328 | tf_op jit(solution)/shard_map/ppermute | solution.py:347
  122.3 16.1 %collective-permute-start.33 = (bf16[256,1024]{1,0:T(8,128)(2,1)}, bf16[256,1024]{1,0:T(8,128)(2,1)S(1)}, u32[]{:S(2)}, u32[]{:S(2)}) collective-permute-start(bf16[256,1024]{1,0:T(8,128)(2,1)} %collective-permute-done.24.refs_4_), channel_id=1, source_target_pairs={{0,1},{1,0},{2,3},{3,2},{4,5},{5,4},{6,7},{7,6},{8,9},{9,8},{10,11... | collective-permute-start | bytes 1572872 | tf_op jit(solution)/shard_map/ppermute | solution.py:261
  124.1 14.3 %collective-permute-start.32 = (bf16[256,1024]{1,0:T(8,128)(2,1)}, bf16[256,1024]{1,0:T(8,128)(2,1)S(1)}, u32[]{:S(2)}, u32[]{:S(2)}) collective-permute-start(bf16[256,1024]{1,0:T(8,128)(2,1)} %collective-permute-done.23.refs_3_), channel_id=1, source_target_pairs={{0,1},{1,0},{2,3},{3,2},{4,5},{5,4},{6,7},{7,6},{8,9},{9,8},{10,11... | collective-permute-start | bytes 1572872 | tf_op jit(solution)/shard_map/ppermute | solution.py:261
  124.2 14.7 %collective-permute-start.35 = (bf16[256,1024]{1,0:T(8,128)(2,1)}, bf16[256,1024]{1,0:T(8,128)(2,1)S(1)}, u32[]{:S(2)}, u32[]{:S(2)}) collective-permute-start(bf16[256,1024]{1,0:T(8,128)(2,1)} %collective-permute-done.28.refs_6_), channel_id=1, source_target_pairs={{0,1},{1,0},{2,3},{3,2},{4,5},{5,4},{6,7},{7,6},{8,9},{9,8},{10,11... | collective-permute-start | bytes 1572872 | tf_op jit(solution)/shard_map/ppermute | solution.py:261
  134.3 19.3 %collective-permute-start.39 = (bf16[392,704]{1,0:T(8,128)(2,1)S(1)}, bf16[392,704]{1,0:T(8,128)(2,1)}, u32[]{:S(2)}, u32[]{:S(2)}) collective-permute-start(bf16[392,704]{1,0:T(8,128)(2,1)S(1)} %get-tuple-element.92), channel_id=1, source_target_pairs={{0,16},{16,0},{1,17},{17,1},{2,18},{18,2},{3,19},{19,3},{4,20},{20... | collective-permute-start | bytes 1655816 | tf_op jit(solution)/shard_map/ppermute | solution.py:236
  138.9 15.3 %collective-permute-start.38 = (bf16[128,2048]{1,0:T(8,128)(2,1)}, bf16[128,2048]{1,0:T(8,128)(2,1)}, u32[]{:S(2)}, u32[]{:S(2)}) collective-permute-start(bf16[128,2048]{1,0:T(8,128)(2,1)} %get-tuple-element.88), channel_id=1, source_target_pairs={{0,4},{1,3},{2,0},{3,7},{4,8},{5,1},{6,2},{7,11},{8,12},{9,5},{10,... | collective-permute-start | bytes 1572872 | tf_op jit(solution)/shard_map/ppermute | solution.py:373
  143.6 28.6 %collective-permute-start.41 = (bf16[232,1024]{1,0:T(8,128)(2,1)}, bf16[232,1024]{1,0:T(8,128)(2,1)}, u32[]{:S(2)}, u32[]{:S(2)}) collective-permute-start(bf16[232,1024]{1,0:T(8,128)(2,1)} %get-tuple-element.90), channel_id=1, source_target_pairs={{0,16},{16,0},{1,17},{17,1},{2,18},{18,2},{3,19},{19,3},{4,20},{20... | collective-permute-start | bytes 1425416 | tf_op jit(solution)/shard_map/ppermute | solution.py:236
  144.2 41.5 %collective-permute-start.43 = (bf16[232,1024]{1,0:T(8,128)(2,1)}, bf16[232,1024]{1,0:T(8,128)(2,1)}, u32[]{:S(2)}, u32[]{:S(2)}) collective-permute-start(bf16[232,1024]{1,0:T(8,128)(2,1)} %get-tuple-element.89), channel_id=1, source_target_pairs={{0,16},{16,0},{1,17},{17,1},{2,18},{18,2},{3,19},{19,3},{4,20},{20... | collective-permute-start | bytes 1425416 | tf_op jit(solution)/shard_map/ppermute | solution.py:236
  153.6 35.6 %collective-permute-start.44 = (bf16[240,1024]{1,0:T(8,128)(2,1)}, bf16[240,1024]{1,0:T(8,128)(2,1)S(1)}, u32[]{:S(2)}, u32[]{:S(2)}) collective-permute-start(bf16[240,1024]{1,0:T(8,128)(2,1)} %slice.150), channel_id=1, source_target_pairs={{0,16},{16,0},{1,17},{17,1},{2,18},{18,2},{3,19},{19,3},{4,20},{20... | collective-permute-start | bytes 1474568 | tf_op jit(solution)/shard_map/ppermute | solution.py:236
  165.2 14.9 %collective-permute-start.47 = (bf16[128,2048]{1,0:T(8,128)(2,1)S(1)}, bf16[128,2048]{1,0:T(8,128)(2,1)S(1)}, u32[]{:S(2)}, u32[]{:S(2)}) collective-permute-start(bf16[128,2048]{1,0:T(8,128)(2,1)S(1)} %get-tuple-element.80), channel_id=1, source_target_pairs={{0,4},{1,3},{2,0},{3,7},{4,8},{5,1},{6,2},{7,11},{8,12},{9,5},{10,... | collective-permute-start | bytes 1572872 | tf_op jit(solution)/shard_map/ppermute | solution.py:373
  166.7 13.3 %collective-permute-start.40 = (bf16[128,2048]{1,0:T(8,128)(2,1)S(1)}, bf16[128,2048]{1,0:T(8,128)(2,1)S(1)}, u32[]{:S(2)}, u32[]{:S(2)}) collective-permute-start(bf16[128,2048]{1,0:T(8,128)(2,1)S(1)} %get-tuple-element.81), channel_id=1, source_target_pairs={{0,4},{1,3},{2,0},{3,7},{4,8},{5,1},{6,2},{7,11},{8,12},{9,5},{10,... | collective-permute-start | bytes 1572872 | tf_op jit(solution)/shard_map/ppermute | solution.py:373
  (46 other events, 571.9 us)

commit v2 on v1

v2 whole, which is shorter than its diff:
```python
import functools

import jax
import jax.numpy as jnp
from jax import lax
from jax.experimental import pallas as pl
from jax.experimental.pallas import tpu as pltpu
from jax.sharding import PartitionSpec as P

AXIS = "expert"
CORES = 2
CONTRACT_LAST = (((1,), (1,)), ((), ()))
CONTRACT_FIRST = (((0,), (0,)), ((), ()))


def chip_cycle(chips):
    width = 1
    while (2 * width) ** 2 <= chips:
        width *= 2
    height = chips // width
    if width == 1:
        return list(range(chips))
    order = [row * width for row in range(height)]
    for back, row in enumerate(reversed(range(height))):
        columns = range(1, width) if back % 2 == 0 else range(width - 1, 0, -1)
        order += [row * width + column for column in columns]
    return order


def after_all(*values):
    return lax.optimization_barrier(values)


def ahead_by(value, microseconds, after=()):
    return pl.pallas_call(
        lambda *refs: None,
        out_shape=jax.ShapeDtypeStruct(value.shape, value.dtype),
        in_specs=[pl.BlockSpec(memory_space=pltpu.HBM)] + [pl.BlockSpec(memory_space=pl.ANY)] * len(after),
        out_specs=pl.BlockSpec(memory_space=pltpu.HBM),
        input_output_aliases={0: 0},
        cost_estimate=pl.CostEstimate(
            flops=0, bytes_accessed=int(microseconds * 3.0e6), transcendentals=0
        ),
        name="ahead_by",
    )(value, *after)


def split_rows(value, count, tile=16):
    tiles = value.shape[0] // tile
    ends = [tile * (tiles * (i + 1) // count) for i in range(count - 1)] + [value.shape[0]]
    return [value[a:b] for a, b in zip([0] + ends[:-1], ends)]


def windows(rows, cap, devices, group):
    span = min(rows, -(-(group * cap + 15) // 16) * 16)
    return [min(d * cap // 16 * 16, rows - span) for d in range(0, devices, group)], span


def gather_kernel(js, slot_ref, gate_ref, *refs, count, planes, cap, group, gated):
    chunks, (out_hbm, buf, out_ref, in_sems, out_sems) = refs[:-5], refs[-5:]
    block = buf.shape[1] // count
    rows, width = out_ref.shape[1], out_ref.shape[2]
    blocks = [
        chunk.at[pl.ds(first, planes * block)]
        for chunk in chunks
        for first in range(0, chunk.shape[0], planes * block)
    ]
    for plane in range(planes):
        for i, source in enumerate(blocks):
            start = pl.multiple_of(js[i] * block, block)
            pltpu.make_async_copy(
                source.at[pl.ds(plane * block, block)],
                buf.at[plane, pl.ds(start, block)],
                in_sems.at[plane, js[i]],
            ).start()
    firsts, span = windows(rows, cap, count, group)
    firsts = firsts + [rows]
    copies = []
    for plane in range(planes):
        done = 0
        for g in range(count // group):
            first = firsts[g]
            for j in range(g * group, (g + 1) * group):
                window = buf.at[plane, pl.ds(j * block, block)]
                pltpu.make_async_copy(window, window, in_sems.at[plane, j]).wait()
            window = slice(g * group * block, (g + 1) * group * block)
            labels = lax.broadcasted_iota(jnp.int32, (span, group * block), 0) + first
            hit = labels == slot_ref[plane : plane + 1, window]
            onehot = hit.astype(jnp.float32).astype(jnp.bfloat16)
            if gated:
                gates = gate_ref[plane : plane + 1, window]
                scale = jnp.sum(jnp.where(hit, gates, 0.0), axis=1, keepdims=True)
            again = max(0, done - first)
            for left in range(0, width, 512):
                lanes = slice(left, left + 512)
                values = jnp.dot(
                    onehot, buf[plane, window, lanes], preferred_element_type=jnp.float32
                )
                if gated:
                    values = values * scale
                values = values.astype(jnp.bfloat16)
                if again:
                    out_ref[plane, first : first + again, lanes] += values[:again]
                if again < span:
                    out_ref[plane, first + again : first + span, lanes] = values[again:]
            done = first + span
            place = pl.ds(first, firsts[g + 1] - first)
            copy = pltpu.make_async_copy(
                out_ref.at[plane, place], out_hbm.at[plane, place], out_sems.at[plane, g]
            )
            copy.start()
            copies.append(copy)
    for copy in copies:
        copy.wait()


def gather_rows(js, slots, gates, chunks, rows, cap, gated):
    planes, count, group = slots.shape[0], js.shape[0], CORES
    block, width = slots.shape[1] // count, chunks[0].shape[1]
    return pl.pallas_call(
        functools.partial(
            gather_kernel, count=count, planes=planes, cap=cap, group=group, gated=gated
        ),
        out_shape=jax.ShapeDtypeStruct((planes, rows, width), jnp.bfloat16),
        grid_spec=pltpu.PrefetchScalarGridSpec(
            num_scalar_prefetch=1,
            grid=(1,),
            in_specs=[pl.BlockSpec(slots.shape, lambda i, js: (0, 0))] * 2
            + [pl.BlockSpec(memory_space=pl.ANY)] * len(chunks),
            out_specs=pl.BlockSpec(memory_space=pltpu.HBM),
            scratch_shapes=[
                pltpu.VMEM((planes, count * block, width), jnp.bfloat16),
                pltpu.VMEM((planes, rows, width), jnp.bfloat16),
                pltpu.SemaphoreType.DMA((planes, count)),
                pltpu.SemaphoreType.DMA((planes, count // group)),
            ],
        ),
        compiler_params=pltpu.CompilerParams(vmem_limit_bytes=58 * 2**20),
        cost_estimate=pl.CostEstimate(
            flops=0,
            bytes_accessed=int(2 * planes * (count * block + rows) * width * 2),
            transcendentals=0,
        ),
        name="gather_rows",
    )(js, slots, gates, *chunks)


def scatter_kernel(js, slot_ref, grad_ref, *refs, sizes, cap, span):
    outs, buf, sems = refs[:-2], refs[-2], refs[-1]
    count, block, width = buf.shape
    rows = grad_ref.shape[0]
    listed = count // CORES
    copies = []
    places = [(n, at) for n, size in enumerate(sizes) for at in range(size)]
    for order in range(count):
        x, side = order // CORES, order % CORES
        i, (n, at) = x + side * listed, places[x]
        j = js[i]
        first = pl.multiple_of(jnp.minimum(j * cap // 16 * 16, rows - span), 16)
        slots = slot_ref[pl.ds(j, 1), :]
        labels = lax.broadcasted_iota(jnp.int32, (span, block), 0) + first
        onehot = (labels == slots).astype(jnp.float32).astype(jnp.bfloat16)
        for left in range(0, width, 512):
            values = lax.dot_general(
                onehot,
                grad_ref[pl.ds(first, span), left : left + 512],
                CONTRACT_FIRST,
                preferred_element_type=jnp.float32,
            )
            buf[i, :, left : left + 512] = values.astype(jnp.bfloat16)
        out = outs[n + side * len(sizes)].at[pl.ds(at * block, block)]
        copies.append(pltpu.make_async_copy(buf.at[i], out, sems.at[i]))
        copies[-1].start()
    for copy in copies:
        copy.wait()


def scatter_rows(js, slots, grads, cap, sizes):
    count, block = slots.shape
    rows, width = grads.shape
    span = min(rows, -(-(cap + 15) // 16) * 16)
    return pl.pallas_call(
        functools.partial(scatter_kernel, sizes=sizes, cap=cap, span=span),
        out_shape=[jax.ShapeDtypeStruct((n * block, width), jnp.bfloat16) for n in sizes] * CORES,
        grid_spec=pltpu.PrefetchScalarGridSpec(
            num_scalar_prefetch=1,
            grid=(1,),
            in_specs=[
                pl.BlockSpec(slots.shape, lambda i, js: (0, 0)),
                pl.BlockSpec(grads.shape, lambda i, js: (0, 0)),
            ],
            out_specs=[pl.BlockSpec(memory_space=pltpu.HBM)] * (CORES * len(sizes)),
            scratch_shapes=[
                pltpu.VMEM((count, block, width), jnp.bfloat16),
                pltpu.SemaphoreType.DMA((count,)),
            ],
        ),
        compiler_params=pltpu.CompilerParams(vmem_limit_bytes=58 * 2**20),
        cost_estimate=pl.CostEstimate(
            flops=2 * count * span * block * width,
            bytes_accessed=int(2 * (rows + count * block) * width * 2),
            transcendentals=0,
        ),
        name="scatter_rows",
    )(js, slots, grads)


def per_device(tokens, out_grad, expert_ids, gate_weights, trained, w_in, w_down, saved):
    groups, replicas = lax.axis_size(AXIS), lax.axis_size("dp")
    chips = groups // CORES
    tok_count, model_width = tokens.shape
    slot_total = saved.shape[2]
    cap = slot_total // groups
    hidden_units = w_down.shape[1]
    cut = model_width // replicas
    me, replica = lax.axis_index(AXIS), lax.axis_index("dp")
    shifts = range(1, replicas)

    far = chips // 2
    order = chip_cycle(chips)
    place = {c: i for i, c in enumerate(order)}

    def at(device, steps):
        return order[(place[device // CORES] + (steps if device % CORES == 0 else -steps)) % chips]

    along = [(i, CORES * at(i, 1) + i % CORES) for i in range(groups)]
    across = [(i, CORES * at(i, 1) + 1 - i % CORES) for i in range(groups)]
    swap = [(i, i ^ 1) for i in range(groups)]
    names = [("a", 0), ("b", 0)]
    names += [(kind, i) for i in range(1, far + 1) for kind in "ab" if (kind, i) != ("b", far)]
    pairs = names[:1] + names[2:]

    def device_at(device, name, way):
        kind, steps = name
        return CORES * at(device, way * steps) + (device % CORES if kind == "a" else 1 - device % CORES)

    def listing(own, other, way):
        table = [
            [device_at(i, name, way) for name in own] + [device_at(i ^ 1, name, way) for name in other]
            for i in range(groups)
        ]
        size = len(own) + len(other)
        return lax.dynamic_slice(jnp.array(table, jnp.int32), (me, 0), (1, size))[0]

    leaving = [("a", far)] + [(kind, i) for i in range(far - 1, 0, -1) for kind in "ab"] + [("a", 0)]
    sizes = [1] + [2] * (far - 1) + [1]
    work = {
        "js": listing(pairs, pairs, -1),
        "joint": listing(names, names[2:], -1),
        "leaving": listing(leaving, leaving, 1),
    }

    def shifted(value, shift):
        return lax.ppermute(value, "dp", [(r, (r + shift) % replicas) for r in range(replicas)])

    def columns(value, owner):
        return lax.dynamic_slice_in_dim(value, owner * cut, cut, 1)

    def together(*places):
        values = after_all(*[box[key] for box, key in places])
        for (box, key), value in zip(places, values):
            box[key] = value

    came = {}

    def send(pieces, label, i, early):
        for shift in shifts:
            value = shifted(pieces[i], shift)
            came[label, i, shift] = ahead_by(value, early) if early else value
        return [(came, (label, i, shift)) for shift in shifts]

    def whole(label, count, shift):
        return jnp.concatenate([came[label, i, shift] for i in range(count)], axis=0)

    def hop(blocks, kind, step):
        blocks[kind, step] = lax.ppermute(blocks[kind, step - 1], AXIS, along)
        return blocks, (kind, step)

    def exchange(blocks, name):
        blocks["other", name] = lax.ppermute(blocks[name], AXIS, swap)
        return blocks, ("other", name)

    def all_blocks(blocks):
        return [blocks[name] for name in pairs] + [blocks["other", name] for name in pairs]

    labels = jnp.arange(groups, dtype=jnp.int32)
    chosen = expert_ids[None, :, :] == labels[:, None, None]
    routed = jnp.any(chosen, axis=2)
    gate = jnp.sum(jnp.where(chosen, gate_weights[None], 0.0), axis=2)
    earlier = jnp.triu(jnp.ones((tok_count, tok_count), jnp.bfloat16), 1)
    rank = jnp.dot(routed.astype(jnp.bfloat16), earlier, preferred_element_type=jnp.float32)
    slot = jnp.where(routed, rank + (me * cap).astype(jnp.float32), -1.0)
    listed = [gate, slot] + [shifted(slot, i) for i in shifts]
    halves = [columns(tokens, (replica + i) % replicas) for i in range(replicas)]
    work["halves"] = jnp.concatenate(
        [halves[0]] + [shifted(halves[i], i) for i in shifts], axis=0
    )
    own_rows = saved.reshape(slot_total, 2 * hidden_units)
    gate_pre, up_pre = own_rows[:, :hidden_units], own_rows[:, hidden_units:]
    work["saved"] = own_rows

    grads = {("a", 0): out_grad}
    grads["b", 0] = exchange(grads, ("a", 0))[0]["other", ("a", 0)]
    for step in range(1, far + 1):
        moved = [hop(grads, "a", step)]
        if step < far:
            hop(grads, "b", step)
        if step == 1:
            moved += [(listed, -1), (work, "halves"), (work, "saved")]
        elif step == 2:
            moved += [(work, key) for key in ("js", "joint", "leaving", "saved")]
        elif step == 3:
            moved += [exchange(grads, (kind, 1)) for kind in "ab"] + [(saved_pieces, 1)]
        elif step == far:
            moved += [exchange(grads, (kind, 2)) for kind in "ab"]
            work["gates"] = work["info"][:, 0, :].reshape(1, -1)
            all_slots = jnp.swapaxes(work["info"][:, 1:, :], 0, 1).astype(jnp.int32)
            work["slots"] = all_slots.reshape(replicas, -1)
            work["own"] = all_slots[0]
            moved += [(work, key) for key in ("gates", "slots", "own")]
        together(*moved)
        if step == 2:
            saved_pieces[1] = work["saved"][:, hidden_units:]
        if step == 1:
            saved_pieces = [work["saved"][:, :hidden_units], None]
            work["info"] = lax.all_to_all(
                jnp.stack(listed, axis=1), AXIS, split_axis=0, concat_axis=0, tiled=True
            )
        elif step == far - 1:
            together((work, "info"), (grads, ("b", step)))
    held = {("a", 0): work["halves"]}
    exchange(held, ("a", 0))
    held["ab", 0] = jnp.concatenate([held["a", 0], held["other", ("a", 0)]], axis=0)
    together((held, ("ab", 0)), (grads, ("b", far - 1)), *send(saved_pieces, "saved", 0, 12))
    grads["a", far] = ahead_by(grads["a", far], 14)
    for name in pairs:
        if ("other", name) not in grads:
            exchange(grads, name)
    hop(held, "ab", 1)
    js, gates, all_slots = work["js"], work["gates"], work["slots"]

    def pre_grads(hidden_grad, gate_pre, up_pre):
        gate_pre, up_pre = gate_pre.astype(jnp.float32), up_pre.astype(jnp.float32)
        sigmoid_gate = jax.nn.sigmoid(gate_pre)
        activated = gate_pre * sigmoid_gate
        gate_grad = hidden_grad * up_pre * sigmoid_gate * (1.0 + gate_pre * (1.0 - sigmoid_gate))
        up_grad = hidden_grad * activated
        hidden = activated * up_pre
        return [value.astype(jnp.bfloat16) for value in (gate_grad, up_grad, hidden)]

    def down_part(owner):
        return lax.dot_general(
            hidden, columns(s, owner), CONTRACT_FIRST, preferred_element_type=jnp.float32
        )

    work["s"] = gather_rows(js, all_slots[:1], gates, all_blocks(grads), slot_total, cap, True)[0]
    together((work, "s"), (held, ("ab", 1)))
    s = work["s"]
    hidden_grad = lax.dot_general(s, w_down[0], CONTRACT_LAST, preferred_element_type=jnp.float32)
    gate_grad, up_grad, hidden = pre_grads(hidden_grad, gate_pre, up_pre)
    hidden_pieces = split_rows(hidden_grad.astype(jnp.bfloat16), 2, 8)
    work["slot_grads"] = lax.dot_general(
        jnp.concatenate([gate_grad, up_grad], axis=1), w_in[0], CONTRACT_LAST, preferred_element_type=jnp.float32
    ).astype(jnp.bfloat16)
    moved = [hop(held, "ab", 2)]
    together((work, "slot_grads"), *moved)
    parts = scatter_rows(work["leaving"], work["own"], work["slot_grads"], cap, sizes)
    for i in range(len(parts)):
        work["part", i] = parts[i]
    moved = [(work, ("part", i)) for i in range(len(parts))] + send(saved_pieces, "saved", 1, 14)
    together(*moved, hop(held, "ab", 3))
    parts = [work["part", i] for i in range(len(parts))]
    for step in range(4, far):
        hop(held, "ab", step)
    held["a", far] = lax.ppermute(
        lax.slice_in_dim(held["ab", far - 1], 0, replicas * tok_count), AXIS, along
    )
    kept, sent = parts[: len(sizes)], parts[len(sizes) :]
    others = [down_part((replica + i) % replicas).astype(jnp.bfloat16) for i in shifts]
    work["down"] = down_part(replica).astype(jnp.bfloat16)
    swapped = [lax.ppermute(value, AXIS, swap) for value in sent]

    def total(n):
        return kept[n].astype(jnp.float32) + swapped[n].astype(jnp.float32)

    def over_slots(values):
        return sum(
            lax.dot_general(values[i], x[i], CONTRACT_FIRST, preferred_element_type=jnp.float32)
            for i in range(replicas)
        )

    sums = {}
    for n in range(far):
        value = total(n)
        if n == 1:
            value = value + jnp.pad(sums["sum"].astype(jnp.float32), ((0, tok_count), (0, 0)))
        elif n:
            value = value + sums["sum"].astype(jnp.float32)
        value = value.astype(jnp.bfloat16)
        if n < far - 1:
            sums["sum"] = lax.ppermute(value, AXIS, along)
            moved = [(sums, "sum")]
        else:
            sums["a"] = lax.ppermute(value[:tok_count], AXIS, along)
            moved = [(sums, "a")]
            if far > 1:
                sums["b"] = lax.ppermute(value[tok_count:], AXIS, across)
                moved.append((sums, "b"))
        if n == 0:
            moved += [(held, ("a", far)), (work, "down")]
            moved += [(others, i) for i in range(len(others))]
            moved += send(hidden_pieces, "hidden", 0, 20)
        elif n == 1:
            moved += send(hidden_pieces, "hidden", 1, 8)
            blocks = [held["ab", i] for i in range(far)] + [held["a", far]]
            blocks += [lax.ppermute(value, AXIS, swap) for value in blocks[1:]]
            work["x"] = gather_rows(
                work["joint"], all_slots, all_slots.astype(jnp.float32), blocks, slot_total, cap, False
            )
            moved.append((work, "x"))
        elif n == 2:
            x = work["x"]
            gate_grads, up_grads = [gate_grad], [up_grad]
            for i in shifts:
                other = pre_grads(
                    whole("hidden", 2, i).astype(jnp.float32), came["saved", 0, i], came["saved", 1, i]
                )
                gate_grads.append(other[0])
                up_grads.append(other[1])
            work["gate"] = over_slots(gate_grads)
            moved += [(work, "gate")] + [(up_grads, i) for i in shifts]
        elif n == 3:
            work["up"] = over_slots(up_grads)
            moved.append((work, "up"))
        if n in (2, 3):
            for i in shifts:
                value = shifted(down_pieces[i - 1][n - 2], i)
                first = work["x"][0, :8, :128] if n == 2 else work["gate"][:8, :128]
                came["down", n - 2, i] = ahead_by(value, 8 if n == 2 else 14, (first,))
                moved.append((came, ("down", n - 2, i)))
        together(*moved)
        if n == 0:
            down_pieces = [split_rows(other, 3) for other in others]

    for i in shifts:
        came["down", 2, i] = ahead_by(shifted(down_pieces[i - 1][2], i), 14, (work["up"][:8, :128],))
    grad_down = work["down"].astype(jnp.float32)
    for i in shifts:
        grad_down = grad_down + whole("down", 3, i).astype(jnp.float32)
    weight = jnp.concatenate([work["gate"], work["up"], grad_down], axis=0)
    trained_flag = jnp.any(trained == me).astype(jnp.float32)
    work["weight"] = (weight * trained_flag).astype(jnp.bfloat16)
    together((work, "weight"), *[(sums, key) for key in ("a", "b") if key in sums])
    in_grad = total(far) + sums["a"].astype(jnp.float32)
    if far > 1:
        in_grad = in_grad + sums["b"].astype(jnp.float32)
    return in_grad.astype(jnp.bfloat16), work["weight"].T[None]


def solution(mesh):
    return jax.shard_map(
        per_device,
        mesh=mesh,
        in_specs=(
            P(("dp", "expert"), None),
            P(("dp", "expert"), None),
            P(("dp", "expert"), None),
            P(("dp", "expert"), None),
            P(),
            P("expert", None, None),
            P("expert", None, None),
            P("dp", "expert", None, None),
        ),
        out_specs=(P(("dp", "expert"), None), P("expert", "dp", None)),
        check_vma=False,
    )
```

time: 197 us -> 187 us (0.949)
  waiting for transfers between devices: 59.8 us -> 33.8 us
  other arithmetic: 13.6 us -> 25.9 us
  local copies, waits for them, and re-layouts: 16.6 us -> 24.5 us
  starting transfers between devices: 51.1 us -> 43.3 us
  matrix products: 31.8 us -> 36.4 us
    ppermute x7 -> x10, waiting for transfers between devices: 18.8 us -> 5.21 us  [the longest x1 3.3 us: per_device(): sums['a'] = lax.ppermute(value[:tok_count], AXIS, along)]
    slice x0 -> x6, local copies, waits for them, and re-layouts: none -> 9.35 us  [the longest x1 2.88 us: per_device(): saved_pieces[1] = work['saved'][:, hidden_units:]]
    ppermute x14 -> x10, starting transfers between devices: 22.5 us -> 14.5 us  [hop(): blocks[kind, step] = lax.ppermute(blocks[kind, step - 1], AXIS, along)]
    convert_element_type x4 -> x5, other arithmetic: 6.03 us -> 13.2 us  [the longest x4 10 us: per_device(): value = value.astype(jnp.bfloat16)]
    ppermute x9, waiting for transfers between devices: 16.8 us -> 11.2 us  [shifted(): lax.ppermute(value, 'dp', [(r, (r + shift) % replicas) for r in range(rep...]
    dot_general x4, matrix products: 11.9 us -> 16.8 us  [over_slots(): lax.dot_general(values[i], x[i], CONTRACT_FIRST, preferred_element_type=j...]
    ppermute x14 -> x10, waiting for transfers between devices: 20.1 us -> 16 us  [hop(): blocks[kind, step] = lax.ppermute(blocks[kind, step - 1], AXIS, along)]
    all_to_all x1, waiting for transfers between devices: 4.12 us -> 0.15 us  [per_device(): lax.all_to_all(jnp.stack(listed, axis=1), AXIS, split_axis=0, concat_axis...]
  transfers between devices with their start and end apart: 50 -> 44, of which waited for: 14 -> 14; matrix products, arithmetic and copies ran while one was open for 30% -> 43% of each run, Pallas kernels for 11% -> 11%
where the time goes in v2:
time: 187 us
  starting transfers between devices  43.3 us (23%)
  matrix products  36.4 us (19%)
  waiting for transfers between devices  33.8 us (18%)
  other arithmetic  25.9 us (14%)
  local copies, waits for them, and re-layouts  24.5 us (13%)
  Pallas kernels  21.2 us (11%)
    dot_general x4, matrix products, over_slots(): lax.dot_general(values[i], x[i], CONTRACT_FIRST, preferred_element_type=j...  16.8 us
    ppermute x10, waiting for transfers between devices, hop(): blocks[kind, step] = lax.ppermute(blocks[kind, step - 1], AXIS, along)  16 us
    pallas_call x2, Pallas kernels, gather_rows(): pl.pallas_call(functools.partial(gather_kernel, count=count, planes=plane...  14.8 us
    ppermute x10, starting transfers between devices, hop(): blocks[kind, step] = lax.ppermute(blocks[kind, step - 1], AXIS, along)  14.5 us
    ppermute x9, waiting for transfers between devices, shifted(): lax.ppermute(value, 'dp', [(r, (r + shift) % replicas) for r in range(rep...  11.2 us
    convert_element_type x4, other arithmetic, per_device(): value = value.astype(jnp.bfloat16)  10 us
    ppermute x9, starting transfers between devices, shifted(): lax.ppermute(value, 'dp', [(r, (r + shift) % replicas) for r in range(rep...  9.15 us
    dot_general x1, matrix products, per_device(): lax.dot_general(jnp.concatenate([gate_grad, up_grad], axis=1), w_in[0], C...  6.72 us
  transfers between devices with their start and end apart: 44, of which 14 were waited for; matrix products, arithmetic and copies ran while one was open for 43% of the time, Pallas kernels for 11%

profile of v2, /device:TPU:0, one launch (start us, length us, event | category | flops | bytes accessed | tf_op | source)
XLA Modules:
  0.0 186.7 jit_solution(9580404833855008879)
XLA Ops:
  1.2 2.6 %collective-permute-start = (bf16[128,2048]{1,0:T(8,128)(2,1)}, bf16[128,2048]{1,0:T(8,128)(2,1)}, u32[]{:S(2)}, u32[]{:S(2)}) collective-permute-start(bf16[128,2048]{1,0:T(8,128)(2,1)} %refs_0_.1), channel_id=1, source_target_pairs={{0,4},{1,3},{2,0},{3,7},{4,8},{5,1},{6,2},{7,11},{8,12},{9,5},{10,... | collective-permute-start | bytes 1572872 | tf_op jit(solution)/shard_map/ppermute | solution.py:276
  3.8 2.2 %collective-permute-start.7 = (bf16[128,2048]{1,0:T(8,128)(2,1)}, bf16[128,2048]{1,0:T(8,128)(2,1)}, u32[]{:S(2)}, u32[]{:S(2)}) collective-permute-start(bf16[128,2048]{1,0:T(8,128)(2,1)} %collective-permute-done.6.refs_8_), channel_id=1, source_target_pairs={{0,4},{1,3},{2,0},{3,7},{4,8},{5,1},{6,2},{7,11},{8,12},{9,5},{10,... | collective-permute-start | bytes 1572872 | tf_op jit(solution)/shard_map/ppermute | solution.py:276
  10.6 5.2 %collective-permute-done.2 = bf16[128,1024]{1,0:T(8,128)(2,1)S(1)} collective-permute-done((bf16[128,1024]{1,0:T(8,128)(2,1)S(1)}, bf16[128,1024]{1,0:T(8,128)(2,1)S(1)}, u32[]{:S(2)}, u32[]{:S(2)}) %collective-permute-start.2) | collective-permute-done | bytes 262176 | tf_op jit(solution)/shard_map/ppermute | solution.py:254
  17.7 2.4 %slice.70 = bf16[784,704]{1,0:T(8,128)(2,1)} slice(bf16[784,1408]{1,0:T(8,128)(2,1)} %bitcast.56), slice={[0:784], [0:704]} | slice | bytes 2207744 | tf_op jit(solution)/shard_map/slice | solution.py:325
  26.5 4.6 %collective-permute-done.3.refs_3_ = bf16[128,2048]{1,0:T(8,128)(2,1)} collective-permute-done((bf16[128,2048]{1,0:T(8,128)(2,1)}, bf16[128,2048]{1,0:T(8,128)(2,1)}, u32[]{:S(2)}, u32[]{:S(2)}) %collective-permute-start.3) | collective-permute-done | bytes 524320 | tf_op jit(solution)/shard_map/ppermute | solution.py:276
  31.5 5.1 %collective-permute-done.11.refs_4_ = bf16[128,2048]{1,0:T(8,128)(2,1)} collective-permute-done((bf16[128,2048]{1,0:T(8,128)(2,1)}, bf16[128,2048]{1,0:T(8,128)(2,1)}, u32[]{:S(2)}, u32[]{:S(2)}) %collective-permute-start.11) | collective-permute-done | bytes 524320 | tf_op jit(solution)/shard_map/ppermute | solution.py:276
  37.8 5.8 %all-to-all-start = ((f32[16,3,128]{2,1,0:T(4,128)}), f32[16,3,128]{2,1,0:T(4,128)S(1)}, u32[]{:S(2)}, u32[]{:S(2)}) async-start(f32[16,3,128]{2,1,0:T(4,128)} %copy.27), calls=%async_computation | async-start | bytes 65536 | tf_op jit(solution)/shard_map/all_to_all | solution.py:326
  43.6 2.1 %pad_maximum_fusion.1.refs_0_ = bf16[512,1024]{1,0:T(8,128)(2,1)} fusion(bf16[256,1024]{1,0:T(8,128)(2,1)} %collective-permute-done.14, bf16[256,1024]{1,0:T(8,128)(2,1)S(1)} %pad_maximum_fusion.3), kind=kLoop, calls=%fused_computation.60 | loop fusion | flops 2097152 | bytes 2097152 | tf_op jit(solution)/shard_map/concatenate | solution.py:333
  45.7 2.9 %slice.65 = bf16[784,704]{1,0:T(8,128)(2,1)} slice(bf16[784,1408]{1,0:T(8,128)(2,1)} %bitcast.57), slice={[0:784], [704:1408]} | slice | bytes 2207744 | tf_op jit(solution)/shard_map/slice | solution.py:323
  53.9 4.7 %collective-permute-done.9.refs_0_ = bf16[128,2048]{1,0:T(8,128)(2,1)S(1)} collective-permute-done((bf16[128,2048]{1,0:T(8,128)(2,1)}, bf16[128,2048]{1,0:T(8,128)(2,1)S(1)}, u32[]{:S(2)}, u32[]{:S(2)}) %collective-permute-start.9) | collective-permute-done | bytes 524320 | tf_op jit(solution)/shard_map/ppermute | solution.py:276
  63.0 7.2 %gather_rows.2 = bf16[1,784,2048]{2,1,0:T(8,128)(2,1)} custom-call(s32[16]{0:T(128)} %get-tuple-element.80.js, s32[1,2048]{1,0:T(1,128)} %slice.69.slot_ref, f32[1,2048]{1,0:T(1,128)} %slice_bitcast_fusion.1.gate_ref, bf16[128,2048]{1,0:T(8,128)(2,1)} %refs_0_.1, bf16[128,2048]{1,0:T(8,128)(2,1)} %collective-permute-done.refs_1_, ...), custom_call_target="tpu_custom_call" | custom-call | bytes 23199744 | tf_op jit(solution)/shard_map/gather_rows/pallas_call | solution.py:120
  72.2 6.4 %fusion.10 = (bf16[784,704]{1,0:T(8,128)(2,1)S(1)}, bf16[784,704]{1,0:T(8,128)(2,1)S(1)}, bf16[784,704]{1,0:T(8,128)(2,1)}) fusion(bf16[784,1408]{1,0:T(8,128)(2,1)S(1)} %bitcast.58, bf16[784,2048]{1,0:T(8,128)(2,1)} %bitcast.53, bf16[1,704,2048]{2,1,0:T(8,128)(2,1)S(1)} %copy-done), kind=kOutput, calls=%fused_computation.20 | convolution fusion | flops 2269560832 | bytes 11614208 | tf_op jit(solution)/shard_map/dot_general | solution.py:359
  78.6 6.7 %fusion.3.grad_ref = bf16[784,2048]{1,0:T(8,128)(2,1)} fusion(bf16[1,2048,1408]{2,1,0:T(8,128)(2,1)S(1)} %bitcast.68, bf16[784,704]{1,0:T(8,128)(2,1)S(1)} %get-tuple-element.141, bf16[784,704]{1,0:T(8,128)(2,1)S(1)} %get-tuple-element.140), kind=kOutput, calls=%fused_computation.10 | convolution fusion | flops 4527480832 | bytes 11186176 | tf_op jit(solution)/shard_map/dot_general | solution.py:362
  88.6 2.5 %fusion.61 = (bf16[392,704]{1,0:T(8,128)(2,1)}, bf16[392,704]{1,0:T(8,128)(2,1)}) fusion(bf16[784,704]{1,0:T(8,128)(2,1)} %get-tuple-element.142), kind=kLoop, calls=%fused_computation.96 | loop fusion | bytes 2207744 | tf_op jit(solution)/shard_map/slice | solution.py:51
  93.1 6.3 %scatter_rows.1 = (bf16[128,2048]{1,0:T(8,128)(2,1)}, bf16[256,2048]{1,0:T(8,128)(2,1)}, bf16[256,2048]{1,0:T(8,128)(2,1)}, bf16[256,2048]{1,0:T(8,128)(2,1)}, b...) custom-call(s32[16]{0:T(128)} %fusion.52.js, ...), custom_call_target="tpu_custom_call" | custom-call | flops 536870912 | bytes 23199744 | tf_op jit(solution)/shard_map/scatter_rows/pallas_call | solution.py:182
  100.8 3.1 %convolution_convert_fusion = bf16[704,1024]{1,0:T(8,128)(2,1)} fusion(bf16[784,2048]{1,0:T(8,128)(2,1)S(1)} %bitcast.54, s32[]{:T(128)S(6)} %select_n.45, bf16[784,1408]{1,0:T(8,128)(2,1)S(1)} %bitcast.59), kind=kOutput, calls=%fused_computation.43 | convolution fusion | flops 1135501312 | bytes 5455876 | tf_op jit(solution)/shard_map/dot_general | solution.py:352
  105.8 2.0 %collective-permute-start.28 = (bf16[256,1024]{1,0:T(8,128)(2,1)}, bf16[256,1024]{1,0:T(8,128)(2,1)}, u32[]{:S(2)}, u32[]{:S(2)}) collective-permute-start(bf16[256,1024]{1,0:T(8,128)(2,1)} %slice.73), channel_id=1, source_target_pairs={{0,4},{1,3},{2,0},{3,7},{4,8},{5,1},{6,2},{7,11},{8,12},{9,5},{10,... | collective-permute-start | bytes 1572872 | tf_op jit(solution)/shard_map/ppermute | solution.py:375
  110.6 3.2 %convolution_convert_fusion.1 = bf16[704,1024]{1,0:T(8,128)(2,1)} fusion(bf16[784,2048]{1,0:T(8,128)(2,1)S(1)} %bitcast.55, s32[]{:T(128)S(6)} %select_n.48, bf16[784,1408]{1,0:T(8,128)(2,1)S(1)} %bitcast.60), kind=kOutput, calls=%fused_computation.44 | convolution fusion | flops 1135501312 | bytes 5455876 | tf_op jit(solution)/shard_map/dot_general | solution.py:352
  113.9 5.1 %collective-permute-done.29.refs_0_ = bf16[392,704]{1,0:T(8,128)(2,1)} collective-permute-done((bf16[392,704]{1,0:T(8,128)(2,1)}, bf16[392,704]{1,0:T(8,128)(2,1)}, u32[]{:S(2)}, u32[]{:S(2)}) %collective-permute-start.29) | collective-permute-done | bytes 551968 | tf_op jit(solution)/shard_map/ppermute | solution.py:254
  121.0 3.2 %add_convert_fusion.2 = bf16[256,2048]{1,0:T(8,128)(2,1)} fusion(bf16[256,2048]{1,0:T(8,128)(2,1)} %collective-permute-done.25, bf16[256,2048]{1,0:T(8,128)(2,1)} %get-tuple-element.111, bf16[128,2048]{1,0:T(8,128)(2,1)} %collective-permute-done.27), kind=kLoop, calls=%fused_computation.40 | loop fusion | flops 3145728 | bytes 3670016 | tf_op jit(solution)/shard_map/convert_element_type | solution.py:399
  131.2 7.6 %gather_rows.3 = bf16[2,784,1024]{2,1,0:T(8,128)(2,1)} custom-call(s32[16]{0:T(128)} %get-tuple-element.117.js, s32[2,2048]{1,0:T(2,128)} %bitcast.63, f32[2,2048]{1,0:T(2,128)} %convert_element_type.149.gate_ref, bf16[512,1024]{1,0:T(8,128)(2,1)} %pad_maximum_fusion.1.refs_0_, bf16[512,1024]{1,0:T(8,128)(2,1)} %collective-permute-done.19.refs_1_, ...), custom_call_target="tpu_custom_call" | custom-call | bytes 23199744 | tf_op jit(solution)/shard_map/gather_rows/pallas_call | solution.py:120
  140.3 3.2 %add_convert_fusion.1 = bf16[256,2048]{1,0:T(8,128)(2,1)} fusion(bf16[256,2048]{1,0:T(8,128)(2,1)} %collective-permute-done.30, bf16[256,2048]{1,0:T(8,128)(2,1)} %collective-permute-done.24, bf16[256,2048]{1,0:T(8,128)(2,1)S(1)} %copy-done.19), kind=kLoop, calls=%fused_computation.39 | loop fusion | flops 3145728 | bytes 4194304 | tf_op jit(solution)/shard_map/convert_element_type | solution.py:399
  145.5 3.2 %fusion.15 = bf16[784,704]{1,0:T(8,128)(2,1)} fusion(bf16[784,704]{1,0:T(8,128)(2,1)} %ahead_by.8, bf16[392,704]{1,0:T(8,128)(2,1)S(1)} %copy-done.12, bf16[392,704]{1,0:T(8,128)(2,1)} %ahead_by.11), kind=kLoop, calls=%fused_computation.25 | loop fusion | flops 6071296 | bytes 3311616 | tf_op jit(solution)/shard_map/convert_element_type | solution.py:349
  148.7 3.3 %fusion.31 = f32[704,1024]{1,0:T(8,128)} fusion(bf16[784,704]{1,0:T(8,128)(2,1)S(1)} %copy-done.33, bf16[2,784,1024]{2,1,0:T(8,128)(2,1)S(1)} %copy-done.2), kind=kOutput, calls=%fused_computation.49 | convolution fusion | flops 1130364928 | bytes 5693440 | tf_op jit(solution)/shard_map/dot_general | solution.py:388
  153.6 5.7 %convolution_add_fusion.1 = f32[704,1024]{1,0:T(8,128)S(1)} fusion(f32[704,1024]{1,0:T(8,128)} %fusion.31, bf16[2,784,1024]{2,1,0:T(8,128)(2,1)} %gather_rows.3, bf16[784,704]{1,0:T(8,128)(2,1)} %ahead_by.8, bf16[784,704]{1,0:T(8,128)(2,1)} %ahead_by.10, bf16[392,704]{1,0:T(8,128)(2,1)S(1)} %copy-done.12, bf16[392,704]{1,0:T(8,128)(2,1)} %ahead_by.11), kind=kOutput, calls=%fused_computation.42 | convolution fusion | flops 1139916800 | bytes 10935296 | tf_op jit(solution)/shard_map/dot_general | solution.py:388
  159.3 2.7 %add_convert_fusion = bf16[256,2048]{1,0:T(8,128)(2,1)S(1)} fusion(bf16[256,2048]{1,0:T(8,128)(2,1)S(1)} %collective-permute-done.36, bf16[256,2048]{1,0:T(8,128)(2,1)} %collective-permute-done.38, bf16[256,2048]{1,0:T(8,128)(2,1)S(1)} %copy-done.18), kind=kLoop, calls=%fused_computation.38 | loop fusion | flops 3145728 | bytes 4194304 | tf_op jit(solution)/shard_map/convert_element_type | solution.py:399
  165.0 3.4 %fusion.29 = f32[704,1024]{1,0:T(8,128)} fusion(bf16[784,704]{1,0:T(8,128)(2,1)S(1)} %copy-done.31, bf16[2,784,1024]{2,1,0:T(8,128)(2,1)S(1)} %copy-done.3), kind=kOutput, calls=%fused_computation.47 | convolution fusion | flops 1130364928 | bytes 5693440 | tf_op jit(solution)/shard_map/dot_general | solution.py:388
  169.7 4.4 %convolution_add_fusion = f32[704,1024]{1,0:T(8,128)S(1)} fusion(f32[704,1024]{1,0:T(8,128)} %fusion.29, bf16[784,704]{1,0:T(8,128)(2,1)} %fusion.15, bf16[2,784,1024]{2,1,0:T(8,128)(2,1)} %gather_rows.3), kind=kOutput, calls=%fused_computation.41 | convolution fusion | flops 1131085824 | bytes 8577024 | tf_op jit(solution)/shard_map/dot_general | solution.py:388
  174.2 3.3 %collective-permute-done.39 = bf16[128,2048]{1,0:T(8,128)(2,1)} collective-permute-done((bf16[128,2048]{1,0:T(8,128)(2,1)}, bf16[128,2048]{1,0:T(8,128)(2,1)}, u32[]{:S(2)}, u32[]{:S(2)}) %collective-permute-start.39) | collective-permute-done | bytes 524320 | tf_op jit(solution)/shard_map/ppermute | solution.py:404
  178.1 2.3 %convert_add_fusion = f32[704,1024]{1,0:T(8,128)S(1)} fusion(bf16[704,1024]{1,0:T(8,128)(2,1)} %convolution_convert_fusion.1, bf16[240,1024]{1,0:T(8,128)(2,1)} %ahead_by.15, bf16[240,1024]{1,0:T(8,128)(2,1)S(1)} %copy-done.15, bf16[224,1024]{1,0:T(8,128)(2,1)} %ahead_by.13), kind=kLoop, calls=%fused_computation.17 | loop fusion | flops 5767168 | bytes 5767168 | tf_op jit(solution)/shard_map/add | solution.py:449
  181.5 2.7 %fusion = bf16[2112,1024]{1,0:T(8,128)(2,1)} fusion(f32[704,1024]{1,0:T(8,128)S(1)} %convert_add_fusion, f32[704,1024]{1,0:T(8,128)S(1)} %copy-done.8, f32[704,1024]{1,0:T(8,128)S(1)} %copy-done.6, f32[]{:T(128)S(6)} %convert_element_type.163), kind=kLoop, calls=%fused_computation.1 | loop fusion | flops 8650752 | bytes 12976132 | tf_op jit(solution)/shard_map/convert_element_type | solution.py:452
  184.2 2.5 %add_convert_fusion.3 = bf16[128,2048]{1,0:T(8,128)(2,1)} fusion(bf16[128,2048]{1,0:T(8,128)(2,1)} %collective-permute-done.40, bf16[128,2048]{1,0:T(8,128)(2,1)} %collective-permute-done.39, bf16[128,2048]{1,0:T(8,128)(2,1)} %collective-permute-done.23, bf16[128,2048]{1,0:T(8,128)(2,1)S(1)} %copy-done.20), kind=kLoop, calls=%fused_computation.61 | loop fusion | flops 2097152 | bytes 2621440 | tf_op jit(solution)/shard_map/convert_element_type | solution.py:457
  (184 shorter events, 57.3 us)
Async XLA Ops:
  1.2 16.5 %collective-permute-start = (bf16[128,2048]{1,0:T(8,128)(2,1)}, bf16[128,2048]{1,0:T(8,128)(2,1)}, u32[]{:S(2)}, u32[]{:S(2)}) collective-permute-start(bf16[128,2048]{1,0:T(8,128)(2,1)} %refs_0_.1), channel_id=1, source_target_pairs={{0,4},{1,3},{2,0},{3,7},{4,8},{5,1},{6,2},{7,11},{8,12},{9,5},{10,... | collective-permute-start | bytes 1572872 | tf_op jit(solution)/shard_map/ppermute | solution.py:276
  3.8 18.8 %collective-permute-start.7 = (bf16[128,2048]{1,0:T(8,128)(2,1)}, bf16[128,2048]{1,0:T(8,128)(2,1)}, u32[]{:S(2)}, u32[]{:S(2)}) collective-permute-start(bf16[128,2048]{1,0:T(8,128)(2,1)} %collective-permute-done.6.refs_8_), channel_id=1, source_target_pairs={{0,4},{1,3},{2,0},{3,7},{4,8},{5,1},{6,2},{7,11},{8,12},{9,5},{10,... | collective-permute-start | bytes 1572872 | tf_op jit(solution)/shard_map/ppermute | solution.py:276
  20.0 31.0 %collective-permute-start.15 = (bf16[784,704]{1,0:T(8,128)(2,1)}, bf16[784,704]{1,0:T(8,128)(2,1)}, u32[]{:S(2)}, u32[]{:S(2)}) collective-permute-start(bf16[784,704]{1,0:T(8,128)(2,1)} %slice.70), channel_id=1, source_target_pairs={{0,16},{16,0},{1,17},{17,1},{2,18},{18,2},{3,19},{19,3},{4,20},{20... | collective-permute-start | bytes 3311624 | tf_op jit(solution)/shard_map/ppermute | solution.py:254
  21.5 9.5 %collective-permute-start.3 = (bf16[128,2048]{1,0:T(8,128)(2,1)}, bf16[128,2048]{1,0:T(8,128)(2,1)}, u32[]{:S(2)}, u32[]{:S(2)}) collective-permute-start(bf16[128,2048]{1,0:T(8,128)(2,1)} %collective-permute-done.refs_1_), channel_id=1, source_target_pairs={{0,4},{1,3},{2,0},{3,7},{4,8},{5,1},{6,2},{7,11},{8,12},{9,5},{10,... | collective-permute-start | bytes 1572872 | tf_op jit(solution)/shard_map/ppermute | solution.py:276
  22.0 9.5 %collective-permute-start.14 = (bf16[256,1024]{1,0:T(8,128)(2,1)S(1)}, bf16[256,1024]{1,0:T(8,128)(2,1)}, u32[]{:S(2)}, u32[]{:S(2)}) collective-permute-start(bf16[256,1024]{1,0:T(8,128)(2,1)S(1)} %pad_maximum_fusion.3), channel_id=1, source_target_pairs={{0,1},{1,0},{2,3},{3,2},{4,5},{5,4},{6,7},{7,6},{8,9},{9,8},{10,11... | collective-permute-start | bytes 1572872 | tf_op jit(solution)/shard_map/ppermute | solution.py:280
  22.6 14.0 %collective-permute-start.11 = (bf16[128,2048]{1,0:T(8,128)(2,1)}, bf16[128,2048]{1,0:T(8,128)(2,1)}, u32[]{:S(2)}, u32[]{:S(2)}) collective-permute-start(bf16[128,2048]{1,0:T(8,128)(2,1)} %collective-permute-done.7.refs_2_), channel_id=1, source_target_pairs={{0,4},{1,3},{2,0},{3,7},{4,8},{5,1},{6,2},{7,11},{8,12},{9,5},{10,... | collective-permute-start | bytes 1572872 | tf_op jit(solution)/shard_map/ppermute | solution.py:276
  26.1 22.5 %collective-permute-start.5 = (bf16[128,2048]{1,0:T(8,128)(2,1)}, bf16[128,2048]{1,0:T(8,128)(2,1)}, u32[]{:S(2)}, u32[]{:S(2)}) collective-permute-start(bf16[128,2048]{1,0:T(8,128)(2,1)} %collective-permute-done.refs_1_), channel_id=1, source_target_pairs={{0,1},{1,0},{2,3},{3,2},{4,5},{5,4},{6,7},{7,6},{8,9},{9,8},{10,11... | collective-permute-start | bytes 1572872 | tf_op jit(solution)/shard_map/ppermute | solution.py:280
  31.0 18.0 %collective-permute-start.4 = (bf16[128,2048]{1,0:T(8,128)(2,1)}, bf16[128,2048]{1,0:T(8,128)(2,1)}, u32[]{:S(2)}, u32[]{:S(2)}) collective-permute-start(bf16[128,2048]{1,0:T(8,128)(2,1)} %collective-permute-done.3.refs_3_), channel_id=1, source_target_pairs={{0,4},{1,3},{2,0},{3,7},{4,8},{5,1},{6,2},{7,11},{8,12},{9,5},{10,... | collective-permute-start | bytes 1572872 | tf_op jit(solution)/shard_map/ppermute | solution.py:276
  31.5 17.5 %collective-permute-start.8 = (bf16[128,2048]{1,0:T(8,128)(2,1)}, bf16[128,2048]{1,0:T(8,128)(2,1)}, u32[]{:S(2)}, u32[]{:S(2)}) collective-permute-start(bf16[128,2048]{1,0:T(8,128)(2,1)} %collective-permute-done.7.refs_2_), channel_id=1, source_target_pairs={{0,1},{1,0},{2,3},{3,2},{4,5},{5,4},{6,7},{7,6},{8,9},{9,8},{10,11... | collective-permute-start | bytes 1572872 | tf_op jit(solution)/shard_map/ppermute | solution.py:280
  36.7 14.6 %collective-permute-start.13 = (bf16[128,2048]{1,0:T(8,128)(2,1)}, bf16[128,2048]{1,0:T(8,128)(2,1)}, u32[]{:S(2)}, u32[]{:S(2)}) collective-permute-start(bf16[128,2048]{1,0:T(8,128)(2,1)} %collective-permute-done.11.refs_4_), channel_id=1, source_target_pairs={{0,4},{1,3},{2,0},{3,7},{4,8},{5,1},{6,2},{7,11},{8,12},{9,5},{10,... | collective-permute-start | bytes 1572872 | tf_op jit(solution)/shard_map/ppermute | solution.py:276
  37.8 13.4 %all-to-all-start = ((f32[16,3,128]{2,1,0:T(4,128)}), f32[16,3,128]{2,1,0:T(4,128)S(1)}, u32[]{:S(2)}, u32[]{:S(2)}) async-start(f32[16,3,128]{2,1,0:T(4,128)} %copy.27), calls=%async_computation | async-start | bytes 65536 | tf_op jit(solution)/shard_map/all_to_all | solution.py:326
  49.0 12.0 %collective-permute-start.16 = (bf16[128,2048]{1,0:T(8,128)(2,1)}, bf16[128,2048]{1,0:T(8,128)(2,1)}, u32[]{:S(2)}, u32[]{:S(2)}) collective-permute-start(bf16[128,2048]{1,0:T(8,128)(2,1)} %collective-permute-done.4.refs_5_), channel_id=1, source_target_pairs={{0,1},{1,0},{2,3},{3,2},{4,5},{5,4},{6,7},{7,6},{8,9},{9,8},{10,11... | collective-permute-start | bytes 1572872 | tf_op jit(solution)/shard_map/ppermute | solution.py:280
  51.2 19.0 %collective-permute-start.19 = (bf16[512,1024]{1,0:T(8,128)(2,1)}, bf16[512,1024]{1,0:T(8,128)(2,1)}, u32[]{:S(2)}, u32[]{:S(2)}) collective-permute-start(bf16[512,1024]{1,0:T(8,128)(2,1)} %pad_maximum_fusion.1.refs_0_), channel_id=1, source_target_pairs={{0,4},{1,3},{2,0},{3,7},{4,8},{5,1},{6,2},{7,11},{8,12},{9,5},{10,... | collective-permute-start | bytes 3145736 | tf_op jit(solution)/shard_map/ppermute | solution.py:276
  59.8 28.7 %collective-permute-start.21 = (bf16[784,704]{1,0:T(8,128)(2,1)}, bf16[784,704]{1,0:T(8,128)(2,1)}, u32[]{:S(2)}, u32[]{:S(2)}) collective-permute-start(bf16[784,704]{1,0:T(8,128)(2,1)} %slice.65), channel_id=1, source_target_pairs={{0,16},{16,0},{1,17},{17,1},{2,18},{18,2},{3,19},{19,3},{4,20},{20... | collective-permute-start | bytes 3311624 | tf_op jit(solution)/shard_map/ppermute | solution.py:254
  70.3 15.4 %collective-permute-start.20 = (bf16[512,1024]{1,0:T(8,128)(2,1)}, bf16[512,1024]{1,0:T(8,128)(2,1)}, u32[]{:S(2)}, u32[]{:S(2)}) collective-permute-start(bf16[512,1024]{1,0:T(8,128)(2,1)} %collective-permute-done.19.refs_1_), channel_id=1, source_target_pairs={{0,4},{1,3},{2,0},{3,7},{4,8},{5,1},{6,2},{7,11},{8,12},{9,5},{10,... | collective-permute-start | bytes 3145736 | tf_op jit(solution)/shard_map/ppermute | solution.py:276
  85.7 15.1 %collective-permute-start.22 = (bf16[512,1024]{1,0:T(8,128)(2,1)}, bf16[512,1024]{1,0:T(8,128)(2,1)}, u32[]{:S(2)}, u32[]{:S(2)}) collective-permute-start(bf16[512,1024]{1,0:T(8,128)(2,1)} %collective-permute-done.20.refs_2_), channel_id=1, source_target_pairs={{0,4},{1,3},{2,0},{3,7},{4,8},{5,1},{6,2},{7,11},{8,12},{9,5},{10,... | collective-permute-start | bytes 3145736 | tf_op jit(solution)/shard_map/ppermute | solution.py:276
  91.1 35.1 %collective-permute-start.31 = (bf16[392,704]{1,0:T(8,128)(2,1)}, bf16[392,704]{1,0:T(8,128)(2,1)S(1)}, u32[]{:S(2)}, u32[]{:S(2)}) collective-permute-start(bf16[392,704]{1,0:T(8,128)(2,1)} %get-tuple-element.145), channel_id=1, source_target_pairs={{0,16},{16,0},{1,17},{17,1},{2,18},{18,2},{3,19},{19,3},{4,20},{20... | collective-permute-start | bytes 1655816 | tf_op jit(solution)/shard_map/ppermute | solution.py:254
  91.6 27.3 %collective-permute-start.29 = (bf16[392,704]{1,0:T(8,128)(2,1)}, bf16[392,704]{1,0:T(8,128)(2,1)}, u32[]{:S(2)}, u32[]{:S(2)}) collective-permute-start(bf16[392,704]{1,0:T(8,128)(2,1)} %get-tuple-element.146), channel_id=1, source_target_pairs={{0,16},{16,0},{1,17},{17,1},{2,18},{18,2},{3,19},{19,3},{4,20},{20... | collective-permute-start | bytes 1655816 | tf_op jit(solution)/shard_map/ppermute | solution.py:254
  105.8 13.1 %collective-permute-start.28 = (bf16[256,1024]{1,0:T(8,128)(2,1)}, bf16[256,1024]{1,0:T(8,128)(2,1)}, u32[]{:S(2)}, u32[]{:S(2)}) collective-permute-start(bf16[256,1024]{1,0:T(8,128)(2,1)} %slice.73), channel_id=1, source_target_pairs={{0,4},{1,3},{2,0},{3,7},{4,8},{5,1},{6,2},{7,11},{8,12},{9,5},{10,... | collective-permute-start | bytes 1572872 | tf_op jit(solution)/shard_map/ppermute | solution.py:375
  107.9 13.1 %collective-permute-start.25 = (bf16[256,2048]{1,0:T(8,128)(2,1)}, bf16[256,2048]{1,0:T(8,128)(2,1)}, u32[]{:S(2)}, u32[]{:S(2)}) collective-permute-start(bf16[256,2048]{1,0:T(8,128)(2,1)} %get-tuple-element.112), channel_id=1, source_target_pairs={{0,1},{1,0},{2,3},{3,2},{4,5},{5,4},{6,7},{7,6},{8,9},{9,8},{10,11... | collective-permute-start | bytes 3145736 | tf_op jit(solution)/shard_map/ppermute | solution.py:381
  109.0 12.0 %collective-permute-start.27 = (bf16[128,2048]{1,0:T(8,128)(2,1)}, bf16[128,2048]{1,0:T(8,128)(2,1)}, u32[]{:S(2)}, u32[]{:S(2)}) collective-permute-start(bf16[128,2048]{1,0:T(8,128)(2,1)} %add_convert_fusion.4), channel_id=1, source_target_pairs={{0,4},{1,3},{2,0},{3,7},{4,8},{5,1},{6,2},{7,11},{8,12},{9,5},{10,... | collective-permute-start | bytes 1572872 | tf_op jit(solution)/shard_map/ppermute | solution.py:401
  119.0 10.7 %collective-permute-start.33 = (bf16[512,1024]{1,0:T(8,128)(2,1)}, bf16[512,1024]{1,0:T(8,128)(2,1)}, u32[]{:S(2)}, u32[]{:S(2)}) collective-permute-start(bf16[512,1024]{1,0:T(8,128)(2,1)} %collective-permute-done.20.refs_2_), channel_id=1, source_target_pairs={{0,1},{1,0},{2,3},{3,2},{4,5},{5,4},{6,7},{7,6},{8,9},{9,8},{10,11... | collective-permute-start | bytes 3145736 | tf_op jit(solution)/shard_map/ppermute | solution.py:416
  124.1 15.1 %collective-permute-start.30 = (bf16[256,2048]{1,0:T(8,128)(2,1)}, bf16[256,2048]{1,0:T(8,128)(2,1)}, u32[]{:S(2)}, u32[]{:S(2)}) collective-permute-start(bf16[256,2048]{1,0:T(8,128)(2,1)} %add_convert_fusion.2), channel_id=1, source_target_pairs={{0,4},{1,3},{2,0},{3,7},{4,8},{5,1},{6,2},{7,11},{8,12},{9,5},{10,... | collective-permute-start | bytes 3145736 | tf_op jit(solution)/shard_map/ppermute | solution.py:401
  126.2 14.1 %collective-permute-start.24 = (bf16[256,2048]{1,0:T(8,128)(2,1)}, bf16[256,2048]{1,0:T(8,128)(2,1)}, u32[]{:S(2)}, u32[]{:S(2)}) collective-permute-start(bf16[256,2048]{1,0:T(8,128)(2,1)} %get-tuple-element.110), channel_id=1, source_target_pairs={{0,1},{1,0},{2,3},{3,2},{4,5},{5,4},{6,7},{7,6},{8,9},{9,8},{10,11... | collective-permute-start | bytes 3145736 | tf_op jit(solution)/shard_map/ppermute | solution.py:381
  129.6 54.6 %collective-permute-start.23 = (bf16[128,2048]{1,0:T(8,128)(2,1)}, bf16[128,2048]{1,0:T(8,128)(2,1)}, u32[]{:S(2)}, u32[]{:S(2)}) collective-permute-start(bf16[128,2048]{1,0:T(8,128)(2,1)} %get-tuple-element.108), channel_id=1, source_target_pairs={{0,1},{1,0},{2,3},{3,2},{4,5},{5,4},{6,7},{7,6},{8,9},{9,8},{10,11... | collective-permute-start | bytes 1572872 | tf_op jit(solution)/shard_map/ppermute | solution.py:381
  129.9 29.5 %collective-permute-start.38 = (bf16[256,2048]{1,0:T(8,128)(2,1)}, bf16[256,2048]{1,0:T(8,128)(2,1)}, u32[]{:S(2)}, u32[]{:S(2)}) collective-permute-start(bf16[256,2048]{1,0:T(8,128)(2,1)} %get-tuple-element.128), channel_id=1, source_target_pairs={{0,1},{1,0},{2,3},{3,2},{4,5},{5,4},{6,7},{7,6},{8,9},{9,8},{10,11... | collective-permute-start | bytes 3145736 | tf_op jit(solution)/shard_map/ppermute | solution.py:381
  130.2 22.4 %collective-permute-start.37 = (bf16[224,1024]{1,0:T(8,128)(2,1)S(1)}, bf16[224,1024]{1,0:T(8,128)(2,1)S(1)}, u32[]{:S(2)}, u32[]{:S(2)}) collective-permute-start(bf16[224,1024]{1,0:T(8,128)(2,1)S(1)} %slice.78), channel_id=1, source_target_pairs={{0,16},{16,0},{1,17},{17,1},{2,18},{18,2},{3,19},{19,3},{4,20},{20... | collective-permute-start | bytes 1376264 | tf_op jit(solution)/shard_map/ppermute | solution.py:254
  139.2 29.7 %collective-permute-start.41 = (bf16[240,1024]{1,0:T(8,128)(2,1)}, bf16[240,1024]{1,0:T(8,128)(2,1)S(1)}, u32[]{:S(2)}, u32[]{:S(2)}) collective-permute-start(bf16[240,1024]{1,0:T(8,128)(2,1)} %get-tuple-element.143), channel_id=1, source_target_pairs={{0,16},{16,0},{1,17},{17,1},{2,18},{18,2},{3,19},{19,3},{4,20},{20... | collective-permute-start | bytes 1474568 | tf_op jit(solution)/shard_map/ppermute | solution.py:254
  143.5 15.9 %collective-permute-start.36 = (bf16[256,2048]{1,0:T(8,128)(2,1)}, bf16[256,2048]{1,0:T(8,128)(2,1)S(1)}, u32[]{:S(2)}, u32[]{:S(2)}) collective-permute-start(bf16[256,2048]{1,0:T(8,128)(2,1)} %add_convert_fusion.1), channel_id=1, source_target_pairs={{0,4},{1,3},{2,0},{3,7},{4,8},{5,1},{6,2},{7,11},{8,12},{9,5},{10,... | collective-permute-start | bytes 3145736 | tf_op jit(solution)/shard_map/ppermute | solution.py:401
  152.6 25.5 %collective-permute-start.42 = (bf16[240,1024]{1,0:T(8,128)(2,1)}, bf16[240,1024]{1,0:T(8,128)(2,1)}, u32[]{:S(2)}, u32[]{:S(2)}) collective-permute-start(bf16[240,1024]{1,0:T(8,128)(2,1)} %get-tuple-element.144), channel_id=1, source_target_pairs={{0,16},{16,0},{1,17},{17,1},{2,18},{18,2},{3,19},{19,3},{4,20},{20... | collective-permute-start | bytes 1474568 | tf_op jit(solution)/shard_map/ppermute | solution.py:254
  163.1 11.0 %collective-permute-start.40 = (bf16[128,2048]{1,0:T(8,128)(2,1)}, bf16[128,2048]{1,0:T(8,128)(2,1)}, u32[]{:S(2)}, u32[]{:S(2)}) collective-permute-start(bf16[128,2048]{1,0:T(8,128)(2,1)} %get-tuple-element.147), channel_id=1, source_target_pairs={{0,5},{1,2},{2,1},{3,6},{4,9},{5,0},{6,3},{7,10},{8,13},{9,4},{10,... | collective-permute-start | bytes 1572872 | tf_op jit(solution)/shard_map/ppermute | solution.py:407
  163.1 14.3 %collective-permute-start.39 = (bf16[128,2048]{1,0:T(8,128)(2,1)}, bf16[128,2048]{1,0:T(8,128)(2,1)}, u32[]{:S(2)}, u32[]{:S(2)}) collective-permute-start(bf16[128,2048]{1,0:T(8,128)(2,1)} %get-tuple-element.148), channel_id=1, source_target_pairs={{0,4},{1,3},{2,0},{3,7},{4,8},{5,1},{6,2},{7,11},{8,12},{9,5},{10,... | collective-permute-start | bytes 1572872 | tf_op jit(solution)/shard_map/ppermute | solution.py:404
  (48 other events, 475.1 us)

commit v3 on v2

--- a/solution.py
+++ b/solution.py
@@ -306,9 +306,10 @@
         if step < far:
             hop(grads, "b", step)
         if step == 1:
-            moved += [(listed, -1), (work, "halves"), (work, "saved")]
+            together((grads, ("b", 1)), (listed, -1), (work, "halves"), (work, "saved"))
         elif step == 2:
-            moved += [(work, key) for key in ("js", "joint", "leaving", "saved")]
+            places = [(work, key) for key in ("js", "joint", "leaving", "saved")]
+            together((grads, ("a", 2)), *places)
         elif step == 3:
             moved += [exchange(grads, (kind, 1)) for kind in "ab"] + [(saved_pieces, 1)]
         elif step == far:
@@ -331,7 +332,7 @@
     held = {("a", 0): work["halves"]}
     exchange(held, ("a", 0))
     held["ab", 0] = jnp.concatenate([held["a", 0], held["other", ("a", 0)]], axis=0)
-    together((held, ("ab", 0)), (grads, ("b", far - 1)), *send(saved_pieces, "saved", 0, 12))
+    together((held, ("ab", 0)), (grads, ("b", far - 1)), *send(saved_pieces, "saved", 0, 18))
     grads["a", far] = ahead_by(grads["a", far], 14)
     for name in pairs:
         if ("other", name) not in grads:

time: 187 us -> 182 us (0.973)
  starting transfers between devices: 43.3 us -> 39.4 us
  waiting for transfers between devices: 33.8 us -> 31.5 us
    ppermute x10, waiting for transfers between devices: 16 us -> 6.1 us  [hop(): blocks[kind, step] = lax.ppermute(blocks[kind, step - 1], AXIS, along)]
    ppermute x9, waiting for transfers between devices: 11.2 us -> 16.7 us  [shifted(): lax.ppermute(value, 'dp', [(r, (r + shift) % replicas) for r in range(rep...]
    ppermute x3, starting transfers between devices: 5.66 us -> 0.56 us  [per_device(): sums['sum'] = lax.ppermute(value, AXIS, along)]
    ppermute x5, starting transfers between devices: 0.95 us -> 3.9 us  [per_device(): swapped = [lax.ppermute(value, AXIS, swap) for value in sent]]
    ppermute x9, starting transfers between devices: 9.15 us -> 11.7 us  [shifted(): lax.ppermute(value, 'dp', [(r, (r + shift) % replicas) for r in range(rep...]
    ppermute x1, waiting for transfers between devices: 3.3 us -> 5.31 us  [per_device(): sums['a'] = lax.ppermute(value[:tok_count], AXIS, along)]
    unnamed x73 -> x75, local copies, waits for them, and re-layouts: 4.33 us -> 4.92 us
  transfers between devices with their start and end apart: 44 -> 44, of which waited for: 14 -> 14; matrix products, arithmetic and copies ran while one was open for 43% -> 44% of each run, Pallas kernels for 11% -> 12%
where the time goes in v3:
time: 182 us
  starting transfers between devices  39.4 us (22%)
  matrix products  36.6 us (20%)
  waiting for transfers between devices  31.5 us (17%)
  other arithmetic  26.1 us (14%)
  local copies, waits for them, and re-layouts  25.1 us (14%)
  Pallas kernels  21.2 us (12%)
    dot_general x4, matrix products, over_slots(): lax.dot_general(values[i], x[i], CONTRACT_FIRST, preferred_element_type=j...  16.8 us
    ppermute x9, waiting for transfers between devices, shifted(): lax.ppermute(value, 'dp', [(r, (r + shift) % replicas) for r in range(rep...  16.7 us
    pallas_call x2, Pallas kernels, gather_rows(): pl.pallas_call(functools.partial(gather_kernel, count=count, planes=plane...  14.8 us
    ppermute x10, starting transfers between devices, hop(): blocks[kind, step] = lax.ppermute(blocks[kind, step - 1], AXIS, along)  14 us
    ppermute x9, starting transfers between devices, shifted(): lax.ppermute(value, 'dp', [(r, (r + shift) % replicas) for r in range(rep...  11.7 us
    convert_element_type x4, other arithmetic, per_device(): value = value.astype(jnp.bfloat16)  9.94 us
    dot_general x1, matrix products, per_device(): lax.dot_general(jnp.concatenate([gate_grad, up_grad], axis=1), w_in[0], C...  6.69 us
    dot_general x1, matrix products, per_device(): lax.dot_general(s, w_down[0], CONTRACT_LAST, preferred_element_type=jnp.f...  6.58 us
  transfers between devices with their start and end apart: 44, of which 14 were waited for; matrix products, arithmetic and copies ran while one was open for 44% of the time, Pallas kernels for 12%

profile of v3, /device:TPU:0, one launch (start us, length us, event | category | flops | bytes accessed | tf_op | source)
XLA Modules:
  0.0 181.5 jit_solution(3566796008387780219)
XLA Ops:
  1.2 2.6 %collective-permute-start = (bf16[128,2048]{1,0:T(8,128)(2,1)}, bf16[128,2048]{1,0:T(8,128)(2,1)}, u32[]{:S(2)}, u32[]{:S(2)}) collective-permute-start(bf16[128,2048]{1,0:T(8,128)(2,1)} %refs_0_.1), channel_id=1, source_target_pairs={{0,4},{1,3},{2,0},{3,7},{4,8},{5,1},{6,2},{7,11},{8,12},{9,5},{10,... | collective-permute-start | bytes 1572872 | tf_op jit(solution)/shard_map/ppermute | solution.py:276
  3.8 2.2 %collective-permute-start.3 = (bf16[128,2048]{1,0:T(8,128)(2,1)}, bf16[128,2048]{1,0:T(8,128)(2,1)}, u32[]{:S(2)}, u32[]{:S(2)}) collective-permute-start(bf16[128,2048]{1,0:T(8,128)(2,1)} %collective-permute-done.2.refs_8_), channel_id=1, source_target_pairs={{0,4},{1,3},{2,0},{3,7},{4,8},{5,1},{6,2},{7,11},{8,12},{9,5},{10,... | collective-permute-start | bytes 1572872 | tf_op jit(solution)/shard_map/ppermute | solution.py:276
  11.3 2.1 %collective-permute-start.1 = (bf16[128,2048]{1,0:T(8,128)(2,1)}, bf16[128,2048]{1,0:T(8,128)(2,1)}, u32[]{:S(2)}, u32[]{:S(2)}) collective-permute-start(bf16[128,2048]{1,0:T(8,128)(2,1)} %collective-permute-done.refs_1_), channel_id=1, source_target_pairs={{0,4},{1,3},{2,0},{3,7},{4,8},{5,1},{6,2},{7,11},{8,12},{9,5},{10,... | collective-permute-start | bytes 1572872 | tf_op jit(solution)/shard_map/ppermute | solution.py:276
  18.9 2.4 %slice.70 = bf16[784,704]{1,0:T(8,128)(2,1)} slice(bf16[784,1408]{1,0:T(8,128)(2,1)} %bitcast.56), slice={[0:784], [0:704]} | slice | bytes 2207744 | tf_op jit(solution)/shard_map/slice | solution.py:326
  28.1 2.1 %collective-permute-start.13 = (bf16[128,2048]{1,0:T(8,128)(2,1)}, bf16[128,2048]{1,0:T(8,128)(2,1)}, u32[]{:S(2)}, u32[]{:S(2)}) collective-permute-start(bf16[128,2048]{1,0:T(8,128)(2,1)} %collective-permute-done.11.refs_4_), channel_id=1, source_target_pairs={{0,4},{1,3},{2,0},{3,7},{4,8},{5,1},{6,2},{7,11},{8,12},{9,5},{10,... | collective-permute-start | bytes 1572872 | tf_op jit(solution)/shard_map/ppermute | solution.py:276
  30.8 4.9 %all-to-all-start = ((f32[16,3,128]{2,1,0:T(4,128)}), f32[16,3,128]{2,1,0:T(4,128)S(1)}, u32[]{:S(2)}, u32[]{:S(2)}) async-start(f32[16,3,128]{2,1,0:T(4,128)} %copy.27), calls=%async_computation | async-start | bytes 65536 | tf_op jit(solution)/shard_map/all_to_all | solution.py:327
  35.8 2.9 %slice.65 = bf16[784,704]{1,0:T(8,128)(2,1)} slice(bf16[784,1408]{1,0:T(8,128)(2,1)} %bitcast.57), slice={[0:784], [704:1408]} | slice | bytes 2207744 | tf_op jit(solution)/shard_map/slice | solution.py:324
  39.2 1.9 %collective-permute-start.9 = (bf16[128,2048]{1,0:T(8,128)(2,1)}, bf16[128,2048]{1,0:T(8,128)(2,1)S(1)}, u32[]{:S(2)}, u32[]{:S(2)}) collective-permute-start(bf16[128,2048]{1,0:T(8,128)(2,1)} %collective-permute-done.6.refs_5_), channel_id=1, source_target_pairs={{0,4},{1,3},{2,0},{3,7},{4,8},{5,1},{6,2},{7,11},{8,12},{9,5},{10,... | collective-permute-start | bytes 1572872 | tf_op jit(solution)/shard_map/ppermute | solution.py:276
  41.1 2.3 %pad_maximum_fusion.1.refs_0_ = bf16[512,1024]{1,0:T(8,128)(2,1)} fusion(bf16[256,1024]{1,0:T(8,128)(2,1)} %collective-permute-done.14, bf16[256,1024]{1,0:T(8,128)(2,1)} %copy-done.14), kind=kLoop, calls=%fused_computation.60 | loop fusion | flops 2097152 | bytes 2097152 | tf_op jit(solution)/shard_map/concatenate | solution.py:334
  43.4 6.5 %collective-permute-done.15.refs_0_ = bf16[784,704]{1,0:T(8,128)(2,1)} collective-permute-done((bf16[784,704]{1,0:T(8,128)(2,1)}, bf16[784,704]{1,0:T(8,128)(2,1)}, u32[]{:S(2)}, u32[]{:S(2)}) %collective-permute-start.15) | collective-permute-done | bytes 1103904 | tf_op jit(solution)/shard_map/ppermute | solution.py:254
  57.2 7.2 %gather_rows.2 = bf16[1,784,2048]{2,1,0:T(8,128)(2,1)} custom-call(s32[16]{0:T(128)} %get-tuple-element.80.js, s32[1,2048]{1,0:T(1,128)} %slice.69.slot_ref, f32[1,2048]{1,0:T(1,128)} %slice_bitcast_fusion.1.gate_ref, bf16[128,2048]{1,0:T(8,128)(2,1)} %refs_0_.1, bf16[128,2048]{1,0:T(8,128)(2,1)} %collective-permute-done.refs_1_, ...), custom_call_target="tpu_custom_call" | custom-call | bytes 23199744 | tf_op jit(solution)/shard_map/gather_rows/pallas_call | solution.py:120
  65.1 6.6 %fusion.10 = (bf16[784,704]{1,0:T(8,128)(2,1)S(1)}, bf16[784,704]{1,0:T(8,128)(2,1)S(1)}, bf16[784,704]{1,0:T(8,128)(2,1)}) fusion(bf16[784,1408]{1,0:T(8,128)(2,1)S(1)} %bitcast.58, bf16[784,2048]{1,0:T(8,128)(2,1)} %bitcast.53, bf16[1,704,2048]{2,1,0:T(8,128)(2,1)S(1)} %copy-done), kind=kOutput, calls=%fused_computation.20 | convolution fusion | flops 2269560832 | bytes 11614208 | tf_op jit(solution)/shard_map/dot_general | solution.py:360
  71.7 6.7 %fusion.3.grad_ref = bf16[784,2048]{1,0:T(8,128)(2,1)} fusion(bf16[1,2048,1408]{2,1,0:T(8,128)(2,1)S(1)} %bitcast.68, bf16[784,704]{1,0:T(8,128)(2,1)S(1)} %get-tuple-element.141, bf16[784,704]{1,0:T(8,128)(2,1)S(1)} %get-tuple-element.140), kind=kOutput, calls=%fused_computation.10 | convolution fusion | flops 4527480832 | bytes 11186176 | tf_op jit(solution)/shard_map/dot_general | solution.py:363
  80.4 2.3 %collective-permute-done.21.refs_0_ = bf16[784,704]{1,0:T(8,128)(2,1)} collective-permute-done((bf16[784,704]{1,0:T(8,128)(2,1)}, bf16[784,704]{1,0:T(8,128)(2,1)}, u32[]{:S(2)}, u32[]{:S(2)}) %collective-permute-start.21) | collective-permute-done | bytes 1103904 | tf_op jit(solution)/shard_map/ppermute | solution.py:254
  82.8 2.5 %fusion.61 = (bf16[392,704]{1,0:T(8,128)(2,1)}, bf16[392,704]{1,0:T(8,128)(2,1)}) fusion(bf16[784,704]{1,0:T(8,128)(2,1)} %get-tuple-element.142), kind=kLoop, calls=%fused_computation.96 | loop fusion | bytes 2207744 | tf_op jit(solution)/shard_map/slice | solution.py:51
  87.3 6.3 %scatter_rows.1 = (bf16[128,2048]{1,0:T(8,128)(2,1)}, bf16[256,2048]{1,0:T(8,128)(2,1)}, bf16[256,2048]{1,0:T(8,128)(2,1)}, bf16[256,2048]{1,0:T(8,128)(2,1)}, b...) custom-call(s32[16]{0:T(128)} %fusion.52.js, ...), custom_call_target="tpu_custom_call" | custom-call | flops 536870912 | bytes 23199744 | tf_op jit(solution)/shard_map/scatter_rows/pallas_call | solution.py:182
  95.3 3.1 %convolution_convert_fusion = bf16[704,1024]{1,0:T(8,128)(2,1)} fusion(bf16[784,2048]{1,0:T(8,128)(2,1)S(1)} %bitcast.54, s32[]{:T(128)S(6)} %select_n.46, bf16[784,1408]{1,0:T(8,128)(2,1)S(1)} %bitcast.59), kind=kOutput, calls=%fused_computation.43 | convolution fusion | flops 1135501312 | bytes 5455876 | tf_op jit(solution)/shard_map/dot_general | solution.py:353
  103.5 3.2 %convolution_convert_fusion.1 = bf16[704,1024]{1,0:T(8,128)(2,1)} fusion(bf16[784,2048]{1,0:T(8,128)(2,1)S(1)} %bitcast.55, s32[]{:T(128)S(6)} %select_n.48, bf16[784,1408]{1,0:T(8,128)(2,1)S(1)} %bitcast.60), kind=kOutput, calls=%fused_computation.44 | convolution fusion | flops 1135501312 | bytes 5455876 | tf_op jit(solution)/shard_map/dot_general | solution.py:353
  106.8 7.0 %collective-permute-done.29.refs_0_ = bf16[392,704]{1,0:T(8,128)(2,1)} collective-permute-done((bf16[392,704]{1,0:T(8,128)(2,1)}, bf16[392,704]{1,0:T(8,128)(2,1)}, u32[]{:S(2)}, u32[]{:S(2)}) %collective-permute-start.29) | collective-permute-done | bytes 551968 | tf_op jit(solution)/shard_map/ppermute | solution.py:254
  115.5 3.2 %add_convert_fusion.2 = bf16[256,2048]{1,0:T(8,128)(2,1)} fusion(bf16[256,2048]{1,0:T(8,128)(2,1)} %collective-permute-done.25, bf16[256,2048]{1,0:T(8,128)(2,1)} %get-tuple-element.111, bf16[128,2048]{1,0:T(8,128)(2,1)} %collective-permute-done.27), kind=kLoop, calls=%fused_computation.40 | loop fusion | flops 3145728 | bytes 3670016 | tf_op jit(solution)/shard_map/convert_element_type | solution.py:400
  125.6 7.6 %gather_rows.3 = bf16[2,784,1024]{2,1,0:T(8,128)(2,1)} custom-call(s32[16]{0:T(128)} %get-tuple-element.117.js, s32[2,2048]{1,0:T(2,128)} %bitcast.63, f32[2,2048]{1,0:T(2,128)} %convert_element_type.149.gate_ref, bf16[512,1024]{1,0:T(8,128)(2,1)} %pad_maximum_fusion.1.refs_0_, bf16[512,1024]{1,0:T(8,128)(2,1)} %collective-permute-done.19.refs_1_, ...), custom_call_target="tpu_custom_call" | custom-call | bytes 23199744 | tf_op jit(solution)/shard_map/gather_rows/pallas_call | solution.py:120
  135.5 3.2 %add_convert_fusion.1 = bf16[256,2048]{1,0:T(8,128)(2,1)} fusion(bf16[256,2048]{1,0:T(8,128)(2,1)} %collective-permute-done.30, bf16[256,2048]{1,0:T(8,128)(2,1)} %collective-permute-done.24, bf16[256,2048]{1,0:T(8,128)(2,1)S(1)} %copy-done.20), kind=kLoop, calls=%fused_computation.39 | loop fusion | flops 3145728 | bytes 4194304 | tf_op jit(solution)/shard_map/convert_element_type | solution.py:400
  138.7 3.4 %fusion.15 = bf16[784,704]{1,0:T(8,128)(2,1)} fusion(bf16[784,704]{1,0:T(8,128)(2,1)} %ahead_by.8, bf16[392,704]{1,0:T(8,128)(2,1)S(1)} %copy-done.12, bf16[392,704]{1,0:T(8,128)(2,1)} %ahead_by.11), kind=kLoop, calls=%fused_computation.25 | loop fusion | flops 6071296 | bytes 3311616 | tf_op jit(solution)/shard_map/convert_element_type | solution.py:350
  142.0 3.3 %fusion.31 = f32[704,1024]{1,0:T(8,128)} fusion(bf16[784,704]{1,0:T(8,128)(2,1)S(1)} %copy-done.34, bf16[2,784,1024]{2,1,0:T(8,128)(2,1)S(1)} %copy-done.2), kind=kOutput, calls=%fused_computation.49 | convolution fusion | flops 1130364928 | bytes 5693440 | tf_op jit(solution)/shard_map/dot_general | solution.py:389
  146.7 5.7 %convolution_add_fusion.1 = f32[704,1024]{1,0:T(8,128)S(1)} fusion(f32[704,1024]{1,0:T(8,128)} %fusion.31, bf16[2,784,1024]{2,1,0:T(8,128)(2,1)} %gather_rows.3, bf16[784,704]{1,0:T(8,128)(2,1)} %ahead_by.8, bf16[784,704]{1,0:T(8,128)(2,1)} %ahead_by.10, bf16[392,704]{1,0:T(8,128)(2,1)S(1)} %copy-done.12, bf16[392,704]{1,0:T(8,128)(2,1)} %ahead_by.11), kind=kOutput, calls=%fused_computation.42 | convolution fusion | flops 1139916800 | bytes 10935296 | tf_op jit(solution)/shard_map/dot_general | solution.py:389
  153.7 2.7 %add_convert_fusion = bf16[256,2048]{1,0:T(8,128)(2,1)S(1)} fusion(bf16[256,2048]{1,0:T(8,128)(2,1)S(1)} %collective-permute-done.36, bf16[256,2048]{1,0:T(8,128)(2,1)} %collective-permute-done.38, bf16[256,2048]{1,0:T(8,128)(2,1)S(1)} %copy-done.19), kind=kLoop, calls=%fused_computation.38 | loop fusion | flops 3145728 | bytes 4194304 | tf_op jit(solution)/shard_map/convert_element_type | solution.py:400
  157.8 3.4 %fusion.29 = f32[704,1024]{1,0:T(8,128)} fusion(bf16[784,704]{1,0:T(8,128)(2,1)S(1)} %copy-done.32, bf16[2,784,1024]{2,1,0:T(8,128)(2,1)S(1)} %copy-done.3), kind=kOutput, calls=%fused_computation.47 | convolution fusion | flops 1130364928 | bytes 5693440 | tf_op jit(solution)/shard_map/dot_general | solution.py:389
  162.5 4.4 %convolution_add_fusion = f32[704,1024]{1,0:T(8,128)S(1)} fusion(f32[704,1024]{1,0:T(8,128)} %fusion.29, bf16[784,704]{1,0:T(8,128)(2,1)} %fusion.15, bf16[2,784,1024]{2,1,0:T(8,128)(2,1)} %gather_rows.3), kind=kOutput, calls=%fused_computation.41 | convolution fusion | flops 1131085824 | bytes 8577024 | tf_op jit(solution)/shard_map/dot_general | solution.py:389
  167.0 5.3 %collective-permute-done.39 = bf16[128,2048]{1,0:T(8,128)(2,1)} collective-permute-done((bf16[128,2048]{1,0:T(8,128)(2,1)}, bf16[128,2048]{1,0:T(8,128)(2,1)}, u32[]{:S(2)}, u32[]{:S(2)}) %collective-permute-start.39) | collective-permute-done | bytes 524320 | tf_op jit(solution)/shard_map/ppermute | solution.py:405
  172.9 2.3 %convert_add_fusion = f32[704,1024]{1,0:T(8,128)S(1)} fusion(bf16[704,1024]{1,0:T(8,128)(2,1)} %convolution_convert_fusion.1, bf16[240,1024]{1,0:T(8,128)(2,1)} %ahead_by.15, bf16[240,1024]{1,0:T(8,128)(2,1)S(1)} %copy-done.16, bf16[224,1024]{1,0:T(8,128)(2,1)} %ahead_by.13), kind=kLoop, calls=%fused_computation.17 | loop fusion | flops 5767168 | bytes 5767168 | tf_op jit(solution)/shard_map/add | solution.py:450
  176.3 2.7 %fusion = bf16[2112,1024]{1,0:T(8,128)(2,1)} fusion(f32[704,1024]{1,0:T(8,128)S(1)} %convert_add_fusion, f32[704,1024]{1,0:T(8,128)S(1)} %copy-done.8, f32[704,1024]{1,0:T(8,128)S(1)} %copy-done.6, f32[]{:T(128)S(6)} %convert_element_type.163), kind=kLoop, calls=%fused_computation.1 | loop fusion | flops 8650752 | bytes 12976132 | tf_op jit(solution)/shard_map/convert_element_type | solution.py:453
  179.0 2.5 %add_convert_fusion.3 = bf16[128,2048]{1,0:T(8,128)(2,1)} fusion(bf16[128,2048]{1,0:T(8,128)(2,1)} %collective-permute-done.40, bf16[128,2048]{1,0:T(8,128)(2,1)} %collective-permute-done.39, bf16[128,2048]{1,0:T(8,128)(2,1)} %collective-permute-done.23, bf16[128,2048]{1,0:T(8,128)(2,1)S(1)} %copy-done.21), kind=kLoop, calls=%fused_computation.61 | loop fusion | flops 2097152 | bytes 2621440 | tf_op jit(solution)/shard_map/convert_element_type | solution.py:458
  (186 shorter events, 55.3 us)
Async XLA Ops:
  1.2 10.1 %collective-permute-start = (bf16[128,2048]{1,0:T(8,128)(2,1)}, bf16[128,2048]{1,0:T(8,128)(2,1)}, u32[]{:S(2)}, u32[]{:S(2)}) collective-permute-start(bf16[128,2048]{1,0:T(8,128)(2,1)} %refs_0_.1), channel_id=1, source_target_pairs={{0,4},{1,3},{2,0},{3,7},{4,8},{5,1},{6,2},{7,11},{8,12},{9,5},{10,... | collective-permute-start | bytes 1572872 | tf_op jit(solution)/shard_map/ppermute | solution.py:276
  3.8 13.8 %collective-permute-start.3 = (bf16[128,2048]{1,0:T(8,128)(2,1)}, bf16[128,2048]{1,0:T(8,128)(2,1)}, u32[]{:S(2)}, u32[]{:S(2)}) collective-permute-start(bf16[128,2048]{1,0:T(8,128)(2,1)} %collective-permute-done.2.refs_8_), channel_id=1, source_target_pairs={{0,4},{1,3},{2,0},{3,7},{4,8},{5,1},{6,2},{7,11},{8,12},{9,5},{10,... | collective-permute-start | bytes 1572872 | tf_op jit(solution)/shard_map/ppermute | solution.py:276
  11.3 15.6 %collective-permute-start.7 = (bf16[128,2048]{1,0:T(8,128)(2,1)}, bf16[128,2048]{1,0:T(8,128)(2,1)}, u32[]{:S(2)}, u32[]{:S(2)}) collective-permute-start(bf16[128,2048]{1,0:T(8,128)(2,1)} %collective-permute-done.refs_1_), channel_id=1, source_target_pairs={{0,1},{1,0},{2,3},{3,2},{4,5},{5,4},{6,7},{7,6},{8,9},{9,8},{10,11... | collective-permute-start | bytes 1572872 | tf_op jit(solution)/shard_map/ppermute | solution.py:280
  11.3 14.0 %collective-permute-start.1 = (bf16[128,2048]{1,0:T(8,128)(2,1)}, bf16[128,2048]{1,0:T(8,128)(2,1)}, u32[]{:S(2)}, u32[]{:S(2)}) collective-permute-start(bf16[128,2048]{1,0:T(8,128)(2,1)} %collective-permute-done.refs_1_), channel_id=1, source_target_pairs={{0,4},{1,3},{2,0},{3,7},{4,8},{5,1},{6,2},{7,11},{8,12},{9,5},{10,... | collective-permute-start | bytes 1572872 | tf_op jit(solution)/shard_map/ppermute | solution.py:276
  17.6 10.5 %collective-permute-start.11 = (bf16[128,2048]{1,0:T(8,128)(2,1)}, bf16[128,2048]{1,0:T(8,128)(2,1)}, u32[]{:S(2)}, u32[]{:S(2)}) collective-permute-start(bf16[128,2048]{1,0:T(8,128)(2,1)} %collective-permute-done.3.refs_2_), channel_id=1, source_target_pairs={{0,4},{1,3},{2,0},{3,7},{4,8},{5,1},{6,2},{7,11},{8,12},{9,5},{10,... | collective-permute-start | bytes 1572872 | tf_op jit(solution)/shard_map/ppermute | solution.py:276
  21.3 28.6 %collective-permute-start.15 = (bf16[784,704]{1,0:T(8,128)(2,1)}, bf16[784,704]{1,0:T(8,128)(2,1)}, u32[]{:S(2)}, u32[]{:S(2)}) collective-permute-start(bf16[784,704]{1,0:T(8,128)(2,1)} %slice.70), channel_id=1, source_target_pairs={{0,16},{16,0},{1,17},{17,1},{2,18},{18,2},{3,19},{19,3},{4,20},{20... | collective-permute-start | bytes 3311624 | tf_op jit(solution)/shard_map/ppermute | solution.py:254
  25.3 13.4 %collective-permute-start.6 = (bf16[128,2048]{1,0:T(8,128)(2,1)}, bf16[128,2048]{1,0:T(8,128)(2,1)}, u32[]{:S(2)}, u32[]{:S(2)}) collective-permute-start(bf16[128,2048]{1,0:T(8,128)(2,1)} %collective-permute-done.1.refs_3_), channel_id=1, source_target_pairs={{0,4},{1,3},{2,0},{3,7},{4,8},{5,1},{6,2},{7,11},{8,12},{9,5},{10,... | collective-permute-start | bytes 1572872 | tf_op jit(solution)/shard_map/ppermute | solution.py:276
  26.9 12.2 %collective-permute-start.8 = (bf16[128,2048]{1,0:T(8,128)(2,1)}, bf16[128,2048]{1,0:T(8,128)(2,1)}, u32[]{:S(2)}, u32[]{:S(2)}) collective-permute-start(bf16[128,2048]{1,0:T(8,128)(2,1)} %collective-permute-done.3.refs_2_), channel_id=1, source_target_pairs={{0,1},{1,0},{2,3},{3,2},{4,5},{5,4},{6,7},{7,6},{8,9},{9,8},{10,11... | collective-permute-start | bytes 1572872 | tf_op jit(solution)/shard_map/ppermute | solution.py:280
  26.9 12.3 %collective-permute-start.14 = (bf16[256,1024]{1,0:T(8,128)(2,1)S(1)}, bf16[256,1024]{1,0:T(8,128)(2,1)}, u32[]{:S(2)}, u32[]{:S(2)}) collective-permute-start(bf16[256,1024]{1,0:T(8,128)(2,1)S(1)} %pad_maximum_fusion.3), channel_id=1, source_target_pairs={{0,1},{1,0},{2,3},{3,2},{4,5},{5,4},{6,7},{7,6},{8,9},{9,8},{10,11... | collective-permute-start | bytes 1572872 | tf_op jit(solution)/shard_map/ppermute | solution.py:280
  28.1 15.3 %collective-permute-start.13 = (bf16[128,2048]{1,0:T(8,128)(2,1)}, bf16[128,2048]{1,0:T(8,128)(2,1)}, u32[]{:S(2)}, u32[]{:S(2)}) collective-permute-start(bf16[128,2048]{1,0:T(8,128)(2,1)} %collective-permute-done.11.refs_4_), channel_id=1, source_target_pairs={{0,4},{1,3},{2,0},{3,7},{4,8},{5,1},{6,2},{7,11},{8,12},{9,5},{10,... | collective-permute-start | bytes 1572872 | tf_op jit(solution)/shard_map/ppermute | solution.py:276
  30.8 12.6 %all-to-all-start = ((f32[16,3,128]{2,1,0:T(4,128)}), f32[16,3,128]{2,1,0:T(4,128)S(1)}, u32[]{:S(2)}, u32[]{:S(2)}) async-start(f32[16,3,128]{2,1,0:T(4,128)} %copy.27), calls=%async_computation | async-start | bytes 65536 | tf_op jit(solution)/shard_map/all_to_all | solution.py:327
  38.7 12.5 %collective-permute-start.10 = (bf16[128,2048]{1,0:T(8,128)(2,1)}, bf16[128,2048]{1,0:T(8,128)(2,1)}, u32[]{:S(2)}, u32[]{:S(2)}) collective-permute-start(bf16[128,2048]{1,0:T(8,128)(2,1)} %collective-permute-done.1.refs_3_), channel_id=1, source_target_pairs={{0,1},{1,0},{2,3},{3,2},{4,5},{5,4},{6,7},{7,6},{8,9},{9,8},{10,11... | collective-permute-start | bytes 1572872 | tf_op jit(solution)/shard_map/ppermute | solution.py:280
  39.1 16.5 %collective-permute-start.16 = (bf16[128,2048]{1,0:T(8,128)(2,1)}, bf16[128,2048]{1,0:T(8,128)(2,1)}, u32[]{:S(2)}, u32[]{:S(2)}) collective-permute-start(bf16[128,2048]{1,0:T(8,128)(2,1)} %collective-permute-done.6.refs_5_), channel_id=1, source_target_pairs={{0,1},{1,0},{2,3},{3,2},{4,5},{5,4},{6,7},{7,6},{8,9},{9,8},{10,11... | collective-permute-start | bytes 1572872 | tf_op jit(solution)/shard_map/ppermute | solution.py:280
  39.2 12.0 %collective-permute-start.9 = (bf16[128,2048]{1,0:T(8,128)(2,1)}, bf16[128,2048]{1,0:T(8,128)(2,1)S(1)}, u32[]{:S(2)}, u32[]{:S(2)}) collective-permute-start(bf16[128,2048]{1,0:T(8,128)(2,1)} %collective-permute-done.6.refs_5_), channel_id=1, source_target_pairs={{0,4},{1,3},{2,0},{3,7},{4,8},{5,1},{6,2},{7,11},{8,12},{9,5},{10,... | collective-permute-start | bytes 1572872 | tf_op jit(solution)/shard_map/ppermute | solution.py:276
  50.0 15.1 %collective-permute-start.19 = (bf16[512,1024]{1,0:T(8,128)(2,1)}, bf16[512,1024]{1,0:T(8,128)(2,1)}, u32[]{:S(2)}, u32[]{:S(2)}) collective-permute-start(bf16[512,1024]{1,0:T(8,128)(2,1)} %pad_maximum_fusion.1.refs_0_), channel_id=1, source_target_pairs={{0,4},{1,3},{2,0},{3,7},{4,8},{5,1},{6,2},{7,11},{8,12},{9,5},{10,... | collective-permute-start | bytes 3145736 | tf_op jit(solution)/shard_map/ppermute | solution.py:276
  53.5 29.2 %collective-permute-start.21 = (bf16[784,704]{1,0:T(8,128)(2,1)}, bf16[784,704]{1,0:T(8,128)(2,1)}, u32[]{:S(2)}, u32[]{:S(2)}) collective-permute-start(bf16[784,704]{1,0:T(8,128)(2,1)} %slice.65), channel_id=1, source_target_pairs={{0,16},{16,0},{1,17},{17,1},{2,18},{18,2},{3,19},{19,3},{4,20},{20... | collective-permute-start | bytes 3311624 | tf_op jit(solution)/shard_map/ppermute | solution.py:254
  65.1 15.1 %collective-permute-start.20 = (bf16[512,1024]{1,0:T(8,128)(2,1)}, bf16[512,1024]{1,0:T(8,128)(2,1)}, u32[]{:S(2)}, u32[]{:S(2)}) collective-permute-start(bf16[512,1024]{1,0:T(8,128)(2,1)} %collective-permute-done.19.refs_1_), channel_id=1, source_target_pairs={{0,4},{1,3},{2,0},{3,7},{4,8},{5,1},{6,2},{7,11},{8,12},{9,5},{10,... | collective-permute-start | bytes 3145736 | tf_op jit(solution)/shard_map/ppermute | solution.py:276
  80.2 15.1 %collective-permute-start.22 = (bf16[512,1024]{1,0:T(8,128)(2,1)}, bf16[512,1024]{1,0:T(8,128)(2,1)}, u32[]{:S(2)}, u32[]{:S(2)}) collective-permute-start(bf16[512,1024]{1,0:T(8,128)(2,1)} %collective-permute-done.20.refs_2_), channel_id=1, source_target_pairs={{0,4},{1,3},{2,0},{3,7},{4,8},{5,1},{6,2},{7,11},{8,12},{9,5},{10,... | collective-permute-start | bytes 3145736 | tf_op jit(solution)/shard_map/ppermute | solution.py:276
  85.3 33.6 %collective-permute-start.31 = (bf16[392,704]{1,0:T(8,128)(2,1)}, bf16[392,704]{1,0:T(8,128)(2,1)S(1)}, u32[]{:S(2)}, u32[]{:S(2)}) collective-permute-start(bf16[392,704]{1,0:T(8,128)(2,1)} %get-tuple-element.145), channel_id=1, source_target_pairs={{0,16},{16,0},{1,17},{17,1},{2,18},{18,2},{3,19},{19,3},{4,20},{20... | collective-permute-start | bytes 1655816 | tf_op jit(solution)/shard_map/ppermute | solution.py:254
  86.8 26.9 %collective-permute-start.29 = (bf16[392,704]{1,0:T(8,128)(2,1)}, bf16[392,704]{1,0:T(8,128)(2,1)}, u32[]{:S(2)}, u32[]{:S(2)}) collective-permute-start(bf16[392,704]{1,0:T(8,128)(2,1)} %get-tuple-element.146), channel_id=1, source_target_pairs={{0,16},{16,0},{1,17},{17,1},{2,18},{18,2},{3,19},{19,3},{4,20},{20... | collective-permute-start | bytes 1655816 | tf_op jit(solution)/shard_map/ppermute | solution.py:254
  100.3 13.4 %collective-permute-start.28 = (bf16[256,1024]{1,0:T(8,128)(2,1)}, bf16[256,1024]{1,0:T(8,128)(2,1)}, u32[]{:S(2)}, u32[]{:S(2)}) collective-permute-start(bf16[256,1024]{1,0:T(8,128)(2,1)} %slice.73), channel_id=1, source_target_pairs={{0,4},{1,3},{2,0},{3,7},{4,8},{5,1},{6,2},{7,11},{8,12},{9,5},{10,... | collective-permute-start | bytes 1572872 | tf_op jit(solution)/shard_map/ppermute | solution.py:376
  100.6 14.9 %collective-permute-start.25 = (bf16[256,2048]{1,0:T(8,128)(2,1)}, bf16[256,2048]{1,0:T(8,128)(2,1)}, u32[]{:S(2)}, u32[]{:S(2)}) collective-permute-start(bf16[256,2048]{1,0:T(8,128)(2,1)} %get-tuple-element.112), channel_id=1, source_target_pairs={{0,1},{1,0},{2,3},{3,2},{4,5},{5,4},{6,7},{7,6},{8,9},{9,8},{10,11... | collective-permute-start | bytes 3145736 | tf_op jit(solution)/shard_map/ppermute | solution.py:382
  103.2 12.3 %collective-permute-start.27 = (bf16[128,2048]{1,0:T(8,128)(2,1)}, bf16[128,2048]{1,0:T(8,128)(2,1)}, u32[]{:S(2)}, u32[]{:S(2)}) collective-permute-start(bf16[128,2048]{1,0:T(8,128)(2,1)} %add_convert_fusion.4), channel_id=1, source_target_pairs={{0,4},{1,3},{2,0},{3,7},{4,8},{5,1},{6,2},{7,11},{8,12},{9,5},{10,... | collective-permute-start | bytes 1572872 | tf_op jit(solution)/shard_map/ppermute | solution.py:402
  118.6 15.1 %collective-permute-start.30 = (bf16[256,2048]{1,0:T(8,128)(2,1)}, bf16[256,2048]{1,0:T(8,128)(2,1)}, u32[]{:S(2)}, u32[]{:S(2)}) collective-permute-start(bf16[256,2048]{1,0:T(8,128)(2,1)} %add_convert_fusion.2), channel_id=1, source_target_pairs={{0,4},{1,3},{2,0},{3,7},{4,8},{5,1},{6,2},{7,11},{8,12},{9,5},{10,... | collective-permute-start | bytes 3145736 | tf_op jit(solution)/shard_map/ppermute | solution.py:402
  118.9 16.6 %collective-permute-start.24 = (bf16[256,2048]{1,0:T(8,128)(2,1)}, bf16[256,2048]{1,0:T(8,128)(2,1)}, u32[]{:S(2)}, u32[]{:S(2)}) collective-permute-start(bf16[256,2048]{1,0:T(8,128)(2,1)} %get-tuple-element.110), channel_id=1, source_target_pairs={{0,1},{1,0},{2,3},{3,2},{4,5},{5,4},{6,7},{7,6},{8,9},{9,8},{10,11... | collective-permute-start | bytes 3145736 | tf_op jit(solution)/shard_map/ppermute | solution.py:382
  123.6 55.4 %collective-permute-start.23 = (bf16[128,2048]{1,0:T(8,128)(2,1)}, bf16[128,2048]{1,0:T(8,128)(2,1)}, u32[]{:S(2)}, u32[]{:S(2)}) collective-permute-start(bf16[128,2048]{1,0:T(8,128)(2,1)} %get-tuple-element.108), channel_id=1, source_target_pairs={{0,1},{1,0},{2,3},{3,2},{4,5},{5,4},{6,7},{7,6},{8,9},{9,8},{10,11... | collective-permute-start | bytes 1572872 | tf_op jit(solution)/shard_map/ppermute | solution.py:382
  124.0 29.6 %collective-permute-start.38 = (bf16[256,2048]{1,0:T(8,128)(2,1)}, bf16[256,2048]{1,0:T(8,128)(2,1)}, u32[]{:S(2)}, u32[]{:S(2)}) collective-permute-start(bf16[256,2048]{1,0:T(8,128)(2,1)} %get-tuple-element.128), channel_id=1, source_target_pairs={{0,1},{1,0},{2,3},{3,2},{4,5},{5,4},{6,7},{7,6},{8,9},{9,8},{10,11... | collective-permute-start | bytes 3145736 | tf_op jit(solution)/shard_map/ppermute | solution.py:382
  124.1 21.8 %collective-permute-start.37 = (bf16[224,1024]{1,0:T(8,128)(2,1)S(1)}, bf16[224,1024]{1,0:T(8,128)(2,1)S(1)}, u32[]{:S(2)}, u32[]{:S(2)}) collective-permute-start(bf16[224,1024]{1,0:T(8,128)(2,1)S(1)} %slice.78), channel_id=1, source_target_pairs={{0,16},{16,0},{1,17},{17,1},{2,18},{18,2},{3,19},{19,3},{4,20},{20... | collective-permute-start | bytes 1376264 | tf_op jit(solution)/shard_map/ppermute | solution.py:254
  133.8 28.0 %collective-permute-start.41 = (bf16[240,1024]{1,0:T(8,128)(2,1)}, bf16[240,1024]{1,0:T(8,128)(2,1)S(1)}, u32[]{:S(2)}, u32[]{:S(2)}) collective-permute-start(bf16[240,1024]{1,0:T(8,128)(2,1)} %get-tuple-element.143), channel_id=1, source_target_pairs={{0,16},{16,0},{1,17},{17,1},{2,18},{18,2},{3,19},{19,3},{4,20},{20... | collective-permute-start | bytes 1474568 | tf_op jit(solution)/shard_map/ppermute | solution.py:254
  138.7 15.0 %collective-permute-start.36 = (bf16[256,2048]{1,0:T(8,128)(2,1)}, bf16[256,2048]{1,0:T(8,128)(2,1)S(1)}, u32[]{:S(2)}, u32[]{:S(2)}) collective-permute-start(bf16[256,2048]{1,0:T(8,128)(2,1)} %add_convert_fusion.1), channel_id=1, source_target_pairs={{0,4},{1,3},{2,0},{3,7},{4,8},{5,1},{6,2},{7,11},{8,12},{9,5},{10,... | collective-permute-start | bytes 3145736 | tf_op jit(solution)/shard_map/ppermute | solution.py:402
  145.9 27.0 %collective-permute-start.42 = (bf16[240,1024]{1,0:T(8,128)(2,1)}, bf16[240,1024]{1,0:T(8,128)(2,1)}, u32[]{:S(2)}, u32[]{:S(2)}) collective-permute-start(bf16[240,1024]{1,0:T(8,128)(2,1)} %get-tuple-element.144), channel_id=1, source_target_pairs={{0,16},{16,0},{1,17},{17,1},{2,18},{18,2},{3,19},{19,3},{4,20},{20... | collective-permute-start | bytes 1474568 | tf_op jit(solution)/shard_map/ppermute | solution.py:254
  157.4 14.9 %collective-permute-start.39 = (bf16[128,2048]{1,0:T(8,128)(2,1)}, bf16[128,2048]{1,0:T(8,128)(2,1)}, u32[]{:S(2)}, u32[]{:S(2)}) collective-permute-start(bf16[128,2048]{1,0:T(8,128)(2,1)} %get-tuple-element.148), channel_id=1, source_target_pairs={{0,4},{1,3},{2,0},{3,7},{4,8},{5,1},{6,2},{7,11},{8,12},{9,5},{10,... | collective-permute-start | bytes 1572872 | tf_op jit(solution)/shard_map/ppermute | solution.py:405
  (49 other events, 475.2 us)

commit v4 on v3

--- a/solution.py
+++ b/solution.py
@@ -402,10 +402,15 @@
             sums["sum"] = lax.ppermute(value, AXIS, along)
             moved = [(sums, "sum")]
         else:
-            sums["a"] = lax.ppermute(value[:tok_count], AXIS, along)
+            terms = [kept[n], swapped[n]] + [sums["sum"]] * (n > 1)
+            last = []
+            for half in (slice(0, tok_count), slice(tok_count, None)):
+                rows = [term[half].astype(jnp.float32) for term in terms]
+                last.append(sum(rows[1:], rows[0]).astype(jnp.bfloat16))
+            sums["a"] = lax.ppermute(last[0] if n > 1 else value[:tok_count], AXIS, along)
             moved = [(sums, "a")]
             if far > 1:
-                sums["b"] = lax.ppermute(value[tok_count:], AXIS, across)
+                sums["b"] = lax.ppermute(last[1] if n > 1 else value[tok_count:], AXIS, across)
                 moved.append((sums, "b"))
         if n == 0:
             moved += [(held, ("a", far)), (work, "down")]

time: 182 us -> 182 us (level)
    convert_element_type x0 -> x1, other arithmetic: none -> 3.48 us  [per_device(): last.append(sum(rows[1:], rows[0]).astype(jnp.bfloat16))]
    convert_element_type x4 -> x3, other arithmetic: 9.94 us -> 7.25 us  [per_device(): value = value.astype(jnp.bfloat16)]
where the time goes in v4:
time: 182 us; the launch traced here: 181 us
  starting transfers between devices  39.6 us (22%)
  matrix products  36.6 us (20%)
  waiting for transfers between devices  31.4 us (17%)
  other arithmetic  26.9 us (15%)
  local copies, waits for them, and re-layouts  24 us (13%)
  Pallas kernels  21.2 us (12%)
    dot_general x4, matrix products, over_slots(): lax.dot_general(values[i], x[i], CONTRACT_FIRST, preferred_element_type=j...  16.8 us
    ppermute x9, waiting for transfers between devices, shifted(): lax.ppermute(value, 'dp', [(r, (r + shift) % replicas) for r in range(rep...  16.7 us
    pallas_call x2, Pallas kernels, gather_rows(): pl.pallas_call(functools.partial(gather_kernel, count=count, planes=plane...  14.8 us
    ppermute x10, starting transfers between devices, hop(): blocks[kind, step] = lax.ppermute(blocks[kind, step - 1], AXIS, along)  14 us
    ppermute x9, starting transfers between devices, shifted(): lax.ppermute(value, 'dp', [(r, (r + shift) % replicas) for r in range(rep...  11.7 us
    convert_element_type x3, other arithmetic, per_device(): value = value.astype(jnp.bfloat16)  7.25 us
    dot_general x1, matrix products, per_device(): lax.dot_general(jnp.concatenate([gate_grad, up_grad], axis=1), w_in[0], C...  6.69 us
    dot_general x1, matrix products, per_device(): lax.dot_general(s, w_down[0], CONTRACT_LAST, preferred_element_type=jnp.f...  6.58 us
  transfers between devices with their start and end apart: 44, of which 14 were waited for; matrix products, arithmetic and copies ran while one was open for 44% of the time, Pallas kernels for 12%

profile of v4, /device:TPU:0, one launch (start us, length us, event | category | flops | bytes accessed | tf_op | source)
XLA Modules:
  0.0 181.4 jit_solution(7932464205946035589)
XLA Ops:
  1.2 2.6 %collective-permute-start = (bf16[128,2048]{1,0:T(8,128)(2,1)}, bf16[128,2048]{1,0:T(8,128)(2,1)}, u32[]{:S(2)}, u32[]{:S(2)}) collective-permute-start(bf16[128,2048]{1,0:T(8,128)(2,1)} %refs_0_.1), channel_id=1, source_target_pairs={{0,4},{1,3},{2,0},{3,7},{4,8},{5,1},{6,2},{7,11},{8,12},{9,5},{10,... | collective-permute-start | bytes 1572872 | tf_op jit(solution)/shard_map/ppermute | solution.py:276
  3.8 2.2 %collective-permute-start.3 = (bf16[128,2048]{1,0:T(8,128)(2,1)}, bf16[128,2048]{1,0:T(8,128)(2,1)}, u32[]{:S(2)}, u32[]{:S(2)}) collective-permute-start(bf16[128,2048]{1,0:T(8,128)(2,1)} %collective-permute-done.2.refs_8_), channel_id=1, source_target_pairs={{0,4},{1,3},{2,0},{3,7},{4,8},{5,1},{6,2},{7,11},{8,12},{9,5},{10,... | collective-permute-start | bytes 1572872 | tf_op jit(solution)/shard_map/ppermute | solution.py:276
  11.3 2.1 %collective-permute-start.1 = (bf16[128,2048]{1,0:T(8,128)(2,1)}, bf16[128,2048]{1,0:T(8,128)(2,1)}, u32[]{:S(2)}, u32[]{:S(2)}) collective-permute-start(bf16[128,2048]{1,0:T(8,128)(2,1)} %collective-permute-done.refs_1_), channel_id=1, source_target_pairs={{0,4},{1,3},{2,0},{3,7},{4,8},{5,1},{6,2},{7,11},{8,12},{9,5},{10,... | collective-permute-start | bytes 1572872 | tf_op jit(solution)/shard_map/ppermute | solution.py:276
  18.9 2.4 %slice.82 = bf16[784,704]{1,0:T(8,128)(2,1)} slice(bf16[784,1408]{1,0:T(8,128)(2,1)} %bitcast.56), slice={[0:784], [0:704]} | slice | bytes 2207744 | tf_op jit(solution)/shard_map/slice | solution.py:326
  28.1 2.1 %collective-permute-start.13 = (bf16[128,2048]{1,0:T(8,128)(2,1)}, bf16[128,2048]{1,0:T(8,128)(2,1)}, u32[]{:S(2)}, u32[]{:S(2)}) collective-permute-start(bf16[128,2048]{1,0:T(8,128)(2,1)} %collective-permute-done.11.refs_4_), channel_id=1, source_target_pairs={{0,4},{1,3},{2,0},{3,7},{4,8},{5,1},{6,2},{7,11},{8,12},{9,5},{10,... | collective-permute-start | bytes 1572872 | tf_op jit(solution)/shard_map/ppermute | solution.py:276
  30.8 4.9 %all-to-all-start = ((f32[16,3,128]{2,1,0:T(4,128)}), f32[16,3,128]{2,1,0:T(4,128)S(1)}, u32[]{:S(2)}, u32[]{:S(2)}) async-start(f32[16,3,128]{2,1,0:T(4,128)} %copy.27), calls=%async_computation | async-start | bytes 65536 | tf_op jit(solution)/shard_map/all_to_all | solution.py:327
  35.8 2.9 %slice.77 = bf16[784,704]{1,0:T(8,128)(2,1)} slice(bf16[784,1408]{1,0:T(8,128)(2,1)} %bitcast.57), slice={[0:784], [704:1408]} | slice | bytes 2207744 | tf_op jit(solution)/shard_map/slice | solution.py:324
  39.2 1.9 %collective-permute-start.9 = (bf16[128,2048]{1,0:T(8,128)(2,1)}, bf16[128,2048]{1,0:T(8,128)(2,1)S(1)}, u32[]{:S(2)}, u32[]{:S(2)}) collective-permute-start(bf16[128,2048]{1,0:T(8,128)(2,1)} %collective-permute-done.6.refs_5_), channel_id=1, source_target_pairs={{0,4},{1,3},{2,0},{3,7},{4,8},{5,1},{6,2},{7,11},{8,12},{9,5},{10,... | collective-permute-start | bytes 1572872 | tf_op jit(solution)/shard_map/ppermute | solution.py:276
  41.1 2.3 %pad_maximum_fusion.1.refs_0_ = bf16[512,1024]{1,0:T(8,128)(2,1)} fusion(bf16[256,1024]{1,0:T(8,128)(2,1)} %collective-permute-done.14, bf16[256,1024]{1,0:T(8,128)(2,1)} %copy-done.14), kind=kLoop, calls=%fused_computation.59 | loop fusion | flops 2097152 | bytes 2097152 | tf_op jit(solution)/shard_map/concatenate | solution.py:334
  43.4 6.5 %collective-permute-done.15.refs_0_ = bf16[784,704]{1,0:T(8,128)(2,1)} collective-permute-done((bf16[784,704]{1,0:T(8,128)(2,1)}, bf16[784,704]{1,0:T(8,128)(2,1)}, u32[]{:S(2)}, u32[]{:S(2)}) %collective-permute-start.15) | collective-permute-done | bytes 1103904 | tf_op jit(solution)/shard_map/ppermute | solution.py:254
  57.2 7.2 %gather_rows.2 = bf16[1,784,2048]{2,1,0:T(8,128)(2,1)} custom-call(s32[16]{0:T(128)} %get-tuple-element.80.js, s32[1,2048]{1,0:T(1,128)} %slice.81.slot_ref, f32[1,2048]{1,0:T(1,128)} %slice_bitcast_fusion.1.gate_ref, bf16[128,2048]{1,0:T(8,128)(2,1)} %refs_0_.1, bf16[128,2048]{1,0:T(8,128)(2,1)} %collective-permute-done.refs_1_, ...), custom_call_target="tpu_custom_call" | custom-call | bytes 23199744 | tf_op jit(solution)/shard_map/gather_rows/pallas_call | solution.py:120
  65.1 6.6 %fusion.10 = (bf16[784,704]{1,0:T(8,128)(2,1)S(1)}, bf16[784,704]{1,0:T(8,128)(2,1)S(1)}, bf16[784,704]{1,0:T(8,128)(2,1)}) fusion(bf16[784,1408]{1,0:T(8,128)(2,1)S(1)} %bitcast.58, bf16[784,2048]{1,0:T(8,128)(2,1)} %bitcast.53, bf16[1,704,2048]{2,1,0:T(8,128)(2,1)S(1)} %copy-done), kind=kOutput, calls=%fused_computation.20 | convolution fusion | flops 2269560832 | bytes 11614208 | tf_op jit(solution)/shard_map/dot_general | solution.py:360
  71.7 6.7 %fusion.3.grad_ref = bf16[784,2048]{1,0:T(8,128)(2,1)} fusion(bf16[1,2048,1408]{2,1,0:T(8,128)(2,1)S(1)} %bitcast.68, bf16[784,704]{1,0:T(8,128)(2,1)S(1)} %get-tuple-element.141, bf16[784,704]{1,0:T(8,128)(2,1)S(1)} %get-tuple-element.140), kind=kOutput, calls=%fused_computation.10 | convolution fusion | flops 4527480832 | bytes 11186176 | tf_op jit(solution)/shard_map/dot_general | solution.py:363
  80.4 2.3 %collective-permute-done.21.refs_0_ = bf16[784,704]{1,0:T(8,128)(2,1)} collective-permute-done((bf16[784,704]{1,0:T(8,128)(2,1)}, bf16[784,704]{1,0:T(8,128)(2,1)}, u32[]{:S(2)}, u32[]{:S(2)}) %collective-permute-start.21) | collective-permute-done | bytes 1103904 | tf_op jit(solution)/shard_map/ppermute | solution.py:254
  82.8 2.5 %fusion.61 = (bf16[392,704]{1,0:T(8,128)(2,1)}, bf16[392,704]{1,0:T(8,128)(2,1)}) fusion(bf16[784,704]{1,0:T(8,128)(2,1)} %get-tuple-element.144), kind=kLoop, calls=%fused_computation.97 | loop fusion | bytes 2207744 | tf_op jit(solution)/shard_map/slice | solution.py:51
  87.3 6.3 %scatter_rows.1 = (bf16[128,2048]{1,0:T(8,128)(2,1)}, bf16[256,2048]{1,0:T(8,128)(2,1)}, bf16[256,2048]{1,0:T(8,128)(2,1)}, bf16[256,2048]{1,0:T(8,128)(2,1)}, b...) custom-call(s32[16]{0:T(128)} %fusion.52.js, ...), custom_call_target="tpu_custom_call" | custom-call | flops 536870912 | bytes 23199744 | tf_op jit(solution)/shard_map/scatter_rows/pallas_call | solution.py:182
  95.3 3.1 %convolution_convert_fusion = bf16[704,1024]{1,0:T(8,128)(2,1)} fusion(bf16[784,2048]{1,0:T(8,128)(2,1)S(1)} %bitcast.54, s32[]{:T(128)S(6)} %select_n.46, bf16[784,1408]{1,0:T(8,128)(2,1)S(1)} %bitcast.59), kind=kOutput, calls=%fused_computation.42 | convolution fusion | flops 1135501312 | bytes 5455876 | tf_op jit(solution)/shard_map/dot_general | solution.py:353
  103.5 3.2 %convolution_convert_fusion.1 = bf16[704,1024]{1,0:T(8,128)(2,1)} fusion(bf16[784,2048]{1,0:T(8,128)(2,1)S(1)} %bitcast.55, s32[]{:T(128)S(6)} %select_n.48, bf16[784,1408]{1,0:T(8,128)(2,1)S(1)} %bitcast.60), kind=kOutput, calls=%fused_computation.43 | convolution fusion | flops 1135501312 | bytes 5455876 | tf_op jit(solution)/shard_map/dot_general | solution.py:353
  106.8 7.0 %collective-permute-done.29.refs_0_ = bf16[392,704]{1,0:T(8,128)(2,1)} collective-permute-done((bf16[392,704]{1,0:T(8,128)(2,1)}, bf16[392,704]{1,0:T(8,128)(2,1)}, u32[]{:S(2)}, u32[]{:S(2)}) %collective-permute-start.29) | collective-permute-done | bytes 551968 | tf_op jit(solution)/shard_map/ppermute | solution.py:254
  115.5 3.2 %add_convert_fusion.1 = bf16[256,2048]{1,0:T(8,128)(2,1)} fusion(bf16[256,2048]{1,0:T(8,128)(2,1)} %collective-permute-done.25, bf16[256,2048]{1,0:T(8,128)(2,1)} %get-tuple-element.111, bf16[128,2048]{1,0:T(8,128)(2,1)} %collective-permute-done.27), kind=kLoop, calls=%fused_computation.39 | loop fusion | flops 3145728 | bytes 3670016 | tf_op jit(solution)/shard_map/convert_element_type | solution.py:400
  125.6 7.6 %gather_rows.3 = bf16[2,784,1024]{2,1,0:T(8,128)(2,1)} custom-call(s32[16]{0:T(128)} %get-tuple-element.117.js, s32[2,2048]{1,0:T(2,128)} %bitcast.63, f32[2,2048]{1,0:T(2,128)} %convert_element_type.161.gate_ref, bf16[512,1024]{1,0:T(8,128)(2,1)} %pad_maximum_fusion.1.refs_0_, bf16[512,1024]{1,0:T(8,128)(2,1)} %collective-permute-done.19.refs_1_, ...), custom_call_target="tpu_custom_call" | custom-call | bytes 23199744 | tf_op jit(solution)/shard_map/gather_rows/pallas_call | solution.py:120
  135.5 3.2 %add_convert_fusion = bf16[256,2048]{1,0:T(8,128)(2,1)} fusion(bf16[256,2048]{1,0:T(8,128)(2,1)} %collective-permute-done.30, bf16[256,2048]{1,0:T(8,128)(2,1)} %collective-permute-done.24, bf16[256,2048]{1,0:T(8,128)(2,1)S(1)} %copy-done.20), kind=kLoop, calls=%fused_computation.38 | loop fusion | flops 3145728 | bytes 4194304 | tf_op jit(solution)/shard_map/convert_element_type | solution.py:400
  138.7 3.4 %fusion.15 = bf16[784,704]{1,0:T(8,128)(2,1)} fusion(bf16[784,704]{1,0:T(8,128)(2,1)} %ahead_by.8, bf16[392,704]{1,0:T(8,128)(2,1)S(1)} %copy-done.12, bf16[392,704]{1,0:T(8,128)(2,1)} %ahead_by.11), kind=kLoop, calls=%fused_computation.25 | loop fusion | flops 6071296 | bytes 3311616 | tf_op jit(solution)/shard_map/convert_element_type | solution.py:350
  142.0 3.3 %fusion.31 = f32[704,1024]{1,0:T(8,128)} fusion(bf16[784,704]{1,0:T(8,128)(2,1)S(1)} %copy-done.34, bf16[2,784,1024]{2,1,0:T(8,128)(2,1)S(1)} %copy-done.2), kind=kOutput, calls=%fused_computation.48 | convolution fusion | flops 1130364928 | bytes 5693440 | tf_op jit(solution)/shard_map/dot_general | solution.py:389
  146.7 5.8 %convolution_add_fusion.1 = f32[704,1024]{1,0:T(8,128)S(1)} fusion(f32[704,1024]{1,0:T(8,128)} %fusion.31, bf16[2,784,1024]{2,1,0:T(8,128)(2,1)} %gather_rows.3, bf16[784,704]{1,0:T(8,128)(2,1)} %ahead_by.8, bf16[784,704]{1,0:T(8,128)(2,1)} %ahead_by.10, bf16[392,704]{1,0:T(8,128)(2,1)S(1)} %copy-done.12, bf16[392,704]{1,0:T(8,128)(2,1)} %ahead_by.11), kind=kOutput, calls=%fused_computation.41 | convolution fusion | flops 1139916800 | bytes 10935296 | tf_op jit(solution)/shard_map/dot_general | solution.py:389
  153.7 3.5 %add_convert_fusion.3 = (bf16[128,2048]{1,0:T(8,128)(2,1)}, bf16[128,2048]{1,0:T(8,128)(2,1)}) fusion(bf16[256,2048]{1,0:T(8,128)(2,1)} %collective-permute-done.38, bf16[256,2048]{1,0:T(8,128)(2,1)S(1)} %collective-permute-done.36, bf16[256,2048]{1,0:T(8,128)(2,1)S(1)} %copy-done.19), kind=kLoop, calls=%fused_computation.61 | loop fusion | flops 3145728 | bytes 4194304 | tf_op jit(solution)/shard_map/convert_element_type | solution.py:409
  157.7 3.4 %fusion.29 = f32[704,1024]{1,0:T(8,128)} fusion(bf16[784,704]{1,0:T(8,128)(2,1)S(1)} %copy-done.32, bf16[2,784,1024]{2,1,0:T(8,128)(2,1)S(1)} %copy-done.3), kind=kOutput, calls=%fused_computation.46 | convolution fusion | flops 1130364928 | bytes 5693440 | tf_op jit(solution)/shard_map/dot_general | solution.py:389
  162.5 4.4 %convolution_add_fusion = f32[704,1024]{1,0:T(8,128)S(1)} fusion(f32[704,1024]{1,0:T(8,128)} %fusion.29, bf16[784,704]{1,0:T(8,128)(2,1)} %fusion.15, bf16[2,784,1024]{2,1,0:T(8,128)(2,1)} %gather_rows.3), kind=kOutput, calls=%fused_computation.40 | convolution fusion | flops 1131085824 | bytes 8577024 | tf_op jit(solution)/shard_map/dot_general | solution.py:389
  166.9 5.2 %collective-permute-done.39 = bf16[128,2048]{1,0:T(8,128)(2,1)} collective-permute-done((bf16[128,2048]{1,0:T(8,128)(2,1)}, bf16[128,2048]{1,0:T(8,128)(2,1)}, u32[]{:S(2)}, u32[]{:S(2)}) %collective-permute-start.39) | collective-permute-done | bytes 524320 | tf_op jit(solution)/shard_map/ppermute | solution.py:410
  172.8 2.3 %convert_add_fusion = f32[704,1024]{1,0:T(8,128)S(1)} fusion(bf16[704,1024]{1,0:T(8,128)(2,1)} %convolution_convert_fusion.1, bf16[240,1024]{1,0:T(8,128)(2,1)} %ahead_by.15, bf16[240,1024]{1,0:T(8,128)(2,1)S(1)} %copy-done.16, bf16[224,1024]{1,0:T(8,128)(2,1)} %ahead_by.13), kind=kLoop, calls=%fused_computation.17 | loop fusion | flops 5767168 | bytes 5767168 | tf_op jit(solution)/shard_map/add | solution.py:455
  176.2 2.7 %fusion = bf16[2112,1024]{1,0:T(8,128)(2,1)} fusion(f32[704,1024]{1,0:T(8,128)S(1)} %convert_add_fusion, f32[704,1024]{1,0:T(8,128)S(1)} %copy-done.8, f32[704,1024]{1,0:T(8,128)S(1)} %copy-done.6, f32[]{:T(128)S(6)} %convert_element_type.179), kind=kLoop, calls=%fused_computation.1 | loop fusion | flops 8650752 | bytes 12976132 | tf_op jit(solution)/shard_map/convert_element_type | solution.py:458
  178.9 2.5 %add_convert_fusion.2 = bf16[128,2048]{1,0:T(8,128)(2,1)} fusion(bf16[128,2048]{1,0:T(8,128)(2,1)} %collective-permute-done.40, bf16[128,2048]{1,0:T(8,128)(2,1)} %collective-permute-done.39, bf16[128,2048]{1,0:T(8,128)(2,1)} %collective-permute-done.23, bf16[128,2048]{1,0:T(8,128)(2,1)S(1)} %copy-done.21), kind=kLoop, calls=%fused_computation.60 | loop fusion | flops 2097152 | bytes 2621440 | tf_op jit(solution)/shard_map/convert_element_type | solution.py:463
  (185 shorter events, 54.4 us)
Async XLA Ops:
  1.2 10.1 %collective-permute-start = (bf16[128,2048]{1,0:T(8,128)(2,1)}, bf16[128,2048]{1,0:T(8,128)(2,1)}, u32[]{:S(2)}, u32[]{:S(2)}) collective-permute-start(bf16[128,2048]{1,0:T(8,128)(2,1)} %refs_0_.1), channel_id=1, source_target_pairs={{0,4},{1,3},{2,0},{3,7},{4,8},{5,1},{6,2},{7,11},{8,12},{9,5},{10,... | collective-permute-start | bytes 1572872 | tf_op jit(solution)/shard_map/ppermute | solution.py:276
  3.8 13.8 %collective-permute-start.3 = (bf16[128,2048]{1,0:T(8,128)(2,1)}, bf16[128,2048]{1,0:T(8,128)(2,1)}, u32[]{:S(2)}, u32[]{:S(2)}) collective-permute-start(bf16[128,2048]{1,0:T(8,128)(2,1)} %collective-permute-done.2.refs_8_), channel_id=1, source_target_pairs={{0,4},{1,3},{2,0},{3,7},{4,8},{5,1},{6,2},{7,11},{8,12},{9,5},{10,... | collective-permute-start | bytes 1572872 | tf_op jit(solution)/shard_map/ppermute | solution.py:276
  11.3 15.6 %collective-permute-start.7 = (bf16[128,2048]{1,0:T(8,128)(2,1)}, bf16[128,2048]{1,0:T(8,128)(2,1)}, u32[]{:S(2)}, u32[]{:S(2)}) collective-permute-start(bf16[128,2048]{1,0:T(8,128)(2,1)} %collective-permute-done.refs_1_), channel_id=1, source_target_pairs={{0,1},{1,0},{2,3},{3,2},{4,5},{5,4},{6,7},{7,6},{8,9},{9,8},{10,11... | collective-permute-start | bytes 1572872 | tf_op jit(solution)/shard_map/ppermute | solution.py:280
  11.3 14.0 %collective-permute-start.1 = (bf16[128,2048]{1,0:T(8,128)(2,1)}, bf16[128,2048]{1,0:T(8,128)(2,1)}, u32[]{:S(2)}, u32[]{:S(2)}) collective-permute-start(bf16[128,2048]{1,0:T(8,128)(2,1)} %collective-permute-done.refs_1_), channel_id=1, source_target_pairs={{0,4},{1,3},{2,0},{3,7},{4,8},{5,1},{6,2},{7,11},{8,12},{9,5},{10,... | collective-permute-start | bytes 1572872 | tf_op jit(solution)/shard_map/ppermute | solution.py:276
  17.6 10.5 %collective-permute-start.11 = (bf16[128,2048]{1,0:T(8,128)(2,1)}, bf16[128,2048]{1,0:T(8,128)(2,1)}, u32[]{:S(2)}, u32[]{:S(2)}) collective-permute-start(bf16[128,2048]{1,0:T(8,128)(2,1)} %collective-permute-done.3.refs_2_), channel_id=1, source_target_pairs={{0,4},{1,3},{2,0},{3,7},{4,8},{5,1},{6,2},{7,11},{8,12},{9,5},{10,... | collective-permute-start | bytes 1572872 | tf_op jit(solution)/shard_map/ppermute | solution.py:276
  21.3 28.6 %collective-permute-start.15 = (bf16[784,704]{1,0:T(8,128)(2,1)}, bf16[784,704]{1,0:T(8,128)(2,1)}, u32[]{:S(2)}, u32[]{:S(2)}) collective-permute-start(bf16[784,704]{1,0:T(8,128)(2,1)} %slice.82), channel_id=1, source_target_pairs={{0,16},{16,0},{1,17},{17,1},{2,18},{18,2},{3,19},{19,3},{4,20},{20... | collective-permute-start | bytes 3311624 | tf_op jit(solution)/shard_map/ppermute | solution.py:254
  25.3 13.4 %collective-permute-start.6 = (bf16[128,2048]{1,0:T(8,128)(2,1)}, bf16[128,2048]{1,0:T(8,128)(2,1)}, u32[]{:S(2)}, u32[]{:S(2)}) collective-permute-start(bf16[128,2048]{1,0:T(8,128)(2,1)} %collective-permute-done.1.refs_3_), channel_id=1, source_target_pairs={{0,4},{1,3},{2,0},{3,7},{4,8},{5,1},{6,2},{7,11},{8,12},{9,5},{10,... | collective-permute-start | bytes 1572872 | tf_op jit(solution)/shard_map/ppermute | solution.py:276
  26.9 12.2 %collective-permute-start.8 = (bf16[128,2048]{1,0:T(8,128)(2,1)}, bf16[128,2048]{1,0:T(8,128)(2,1)}, u32[]{:S(2)}, u32[]{:S(2)}) collective-permute-start(bf16[128,2048]{1,0:T(8,128)(2,1)} %collective-permute-done.3.refs_2_), channel_id=1, source_target_pairs={{0,1},{1,0},{2,3},{3,2},{4,5},{5,4},{6,7},{7,6},{8,9},{9,8},{10,11... | collective-permute-start | bytes 1572872 | tf_op jit(solution)/shard_map/ppermute | solution.py:280
  26.9 12.3 %collective-permute-start.14 = (bf16[256,1024]{1,0:T(8,128)(2,1)S(1)}, bf16[256,1024]{1,0:T(8,128)(2,1)}, u32[]{:S(2)}, u32[]{:S(2)}) collective-permute-start(bf16[256,1024]{1,0:T(8,128)(2,1)S(1)} %pad_maximum_fusion.3), channel_id=1, source_target_pairs={{0,1},{1,0},{2,3},{3,2},{4,5},{5,4},{6,7},{7,6},{8,9},{9,8},{10,11... | collective-permute-start | bytes 1572872 | tf_op jit(solution)/shard_map/ppermute | solution.py:280
  28.1 15.3 %collective-permute-start.13 = (bf16[128,2048]{1,0:T(8,128)(2,1)}, bf16[128,2048]{1,0:T(8,128)(2,1)}, u32[]{:S(2)}, u32[]{:S(2)}) collective-permute-start(bf16[128,2048]{1,0:T(8,128)(2,1)} %collective-permute-done.11.refs_4_), channel_id=1, source_target_pairs={{0,4},{1,3},{2,0},{3,7},{4,8},{5,1},{6,2},{7,11},{8,12},{9,5},{10,... | collective-permute-start | bytes 1572872 | tf_op jit(solution)/shard_map/ppermute | solution.py:276
  30.8 12.6 %all-to-all-start = ((f32[16,3,128]{2,1,0:T(4,128)}), f32[16,3,128]{2,1,0:T(4,128)S(1)}, u32[]{:S(2)}, u32[]{:S(2)}) async-start(f32[16,3,128]{2,1,0:T(4,128)} %copy.27), calls=%async_computation | async-start | bytes 65536 | tf_op jit(solution)/shard_map/all_to_all | solution.py:327
  38.7 12.5 %collective-permute-start.10 = (bf16[128,2048]{1,0:T(8,128)(2,1)}, bf16[128,2048]{1,0:T(8,128)(2,1)}, u32[]{:S(2)}, u32[]{:S(2)}) collective-permute-start(bf16[128,2048]{1,0:T(8,128)(2,1)} %collective-permute-done.1.refs_3_), channel_id=1, source_target_pairs={{0,1},{1,0},{2,3},{3,2},{4,5},{5,4},{6,7},{7,6},{8,9},{9,8},{10,11... | collective-permute-start | bytes 1572872 | tf_op jit(solution)/shard_map/ppermute | solution.py:280
  39.1 16.5 %collective-permute-start.16 = (bf16[128,2048]{1,0:T(8,128)(2,1)}, bf16[128,2048]{1,0:T(8,128)(2,1)}, u32[]{:S(2)}, u32[]{:S(2)}) collective-permute-start(bf16[128,2048]{1,0:T(8,128)(2,1)} %collective-permute-done.6.refs_5_), channel_id=1, source_target_pairs={{0,1},{1,0},{2,3},{3,2},{4,5},{5,4},{6,7},{7,6},{8,9},{9,8},{10,11... | collective-permute-start | bytes 1572872 | tf_op jit(solution)/shard_map/ppermute | solution.py:280
  39.2 12.0 %collective-permute-start.9 = (bf16[128,2048]{1,0:T(8,128)(2,1)}, bf16[128,2048]{1,0:T(8,128)(2,1)S(1)}, u32[]{:S(2)}, u32[]{:S(2)}) collective-permute-start(bf16[128,2048]{1,0:T(8,128)(2,1)} %collective-permute-done.6.refs_5_), channel_id=1, source_target_pairs={{0,4},{1,3},{2,0},{3,7},{4,8},{5,1},{6,2},{7,11},{8,12},{9,5},{10,... | collective-permute-start | bytes 1572872 | tf_op jit(solution)/shard_map/ppermute | solution.py:276
  50.0 15.1 %collective-permute-start.19 = (bf16[512,1024]{1,0:T(8,128)(2,1)}, bf16[512,1024]{1,0:T(8,128)(2,1)}, u32[]{:S(2)}, u32[]{:S(2)}) collective-permute-start(bf16[512,1024]{1,0:T(8,128)(2,1)} %pad_maximum_fusion.1.refs_0_), channel_id=1, source_target_pairs={{0,4},{1,3},{2,0},{3,7},{4,8},{5,1},{6,2},{7,11},{8,12},{9,5},{10,... | collective-permute-start | bytes 3145736 | tf_op jit(solution)/shard_map/ppermute | solution.py:276
  53.5 29.2 %collective-permute-start.21 = (bf16[784,704]{1,0:T(8,128)(2,1)}, bf16[784,704]{1,0:T(8,128)(2,1)}, u32[]{:S(2)}, u32[]{:S(2)}) collective-permute-start(bf16[784,704]{1,0:T(8,128)(2,1)} %slice.77), channel_id=1, source_target_pairs={{0,16},{16,0},{1,17},{17,1},{2,18},{18,2},{3,19},{19,3},{4,20},{20... | collective-permute-start | bytes 3311624 | tf_op jit(solution)/shard_map/ppermute | solution.py:254
  65.1 15.1 %collective-permute-start.20 = (bf16[512,1024]{1,0:T(8,128)(2,1)}, bf16[512,1024]{1,0:T(8,128)(2,1)}, u32[]{:S(2)}, u32[]{:S(2)}) collective-permute-start(bf16[512,1024]{1,0:T(8,128)(2,1)} %collective-permute-done.19.refs_1_), channel_id=1, source_target_pairs={{0,4},{1,3},{2,0},{3,7},{4,8},{5,1},{6,2},{7,11},{8,12},{9,5},{10,... | collective-permute-start | bytes 3145736 | tf_op jit(solution)/shard_map/ppermute | solution.py:276
  80.2 15.1 %collective-permute-start.22 = (bf16[512,1024]{1,0:T(8,128)(2,1)}, bf16[512,1024]{1,0:T(8,128)(2,1)}, u32[]{:S(2)}, u32[]{:S(2)}) collective-permute-start(bf16[512,1024]{1,0:T(8,128)(2,1)} %collective-permute-done.20.refs_2_), channel_id=1, source_target_pairs={{0,4},{1,3},{2,0},{3,7},{4,8},{5,1},{6,2},{7,11},{8,12},{9,5},{10,... | collective-permute-start | bytes 3145736 | tf_op jit(solution)/shard_map/ppermute | solution.py:276
  85.3 33.6 %collective-permute-start.31 = (bf16[392,704]{1,0:T(8,128)(2,1)}, bf16[392,704]{1,0:T(8,128)(2,1)S(1)}, u32[]{:S(2)}, u32[]{:S(2)}) collective-permute-start(bf16[392,704]{1,0:T(8,128)(2,1)} %get-tuple-element.147), channel_id=1, source_target_pairs={{0,16},{16,0},{1,17},{17,1},{2,18},{18,2},{3,19},{19,3},{4,20},{20... | collective-permute-start | bytes 1655816 | tf_op jit(solution)/shard_map/ppermute | solution.py:254
  86.8 26.9 %collective-permute-start.29 = (bf16[392,704]{1,0:T(8,128)(2,1)}, bf16[392,704]{1,0:T(8,128)(2,1)}, u32[]{:S(2)}, u32[]{:S(2)}) collective-permute-start(bf16[392,704]{1,0:T(8,128)(2,1)} %get-tuple-element.148), channel_id=1, source_target_pairs={{0,16},{16,0},{1,17},{17,1},{2,18},{18,2},{3,19},{19,3},{4,20},{20... | collective-permute-start | bytes 1655816 | tf_op jit(solution)/shard_map/ppermute | solution.py:254
  100.3 13.4 %collective-permute-start.28 = (bf16[256,1024]{1,0:T(8,128)(2,1)}, bf16[256,1024]{1,0:T(8,128)(2,1)}, u32[]{:S(2)}, u32[]{:S(2)}) collective-permute-start(bf16[256,1024]{1,0:T(8,128)(2,1)} %slice.85), channel_id=1, source_target_pairs={{0,4},{1,3},{2,0},{3,7},{4,8},{5,1},{6,2},{7,11},{8,12},{9,5},{10,... | collective-permute-start | bytes 1572872 | tf_op jit(solution)/shard_map/ppermute | solution.py:376
  100.6 14.9 %collective-permute-start.25 = (bf16[256,2048]{1,0:T(8,128)(2,1)}, bf16[256,2048]{1,0:T(8,128)(2,1)}, u32[]{:S(2)}, u32[]{:S(2)}) collective-permute-start(bf16[256,2048]{1,0:T(8,128)(2,1)} %get-tuple-element.112), channel_id=1, source_target_pairs={{0,1},{1,0},{2,3},{3,2},{4,5},{5,4},{6,7},{7,6},{8,9},{9,8},{10,11... | collective-permute-start | bytes 3145736 | tf_op jit(solution)/shard_map/ppermute | solution.py:382
  103.2 12.3 %collective-permute-start.27 = (bf16[128,2048]{1,0:T(8,128)(2,1)}, bf16[128,2048]{1,0:T(8,128)(2,1)}, u32[]{:S(2)}, u32[]{:S(2)}) collective-permute-start(bf16[128,2048]{1,0:T(8,128)(2,1)} %add_convert_fusion.5), channel_id=1, source_target_pairs={{0,4},{1,3},{2,0},{3,7},{4,8},{5,1},{6,2},{7,11},{8,12},{9,5},{10,... | collective-permute-start | bytes 1572872 | tf_op jit(solution)/shard_map/ppermute | solution.py:402
  118.6 15.1 %collective-permute-start.30 = (bf16[256,2048]{1,0:T(8,128)(2,1)}, bf16[256,2048]{1,0:T(8,128)(2,1)}, u32[]{:S(2)}, u32[]{:S(2)}) collective-permute-start(bf16[256,2048]{1,0:T(8,128)(2,1)} %add_convert_fusion.1), channel_id=1, source_target_pairs={{0,4},{1,3},{2,0},{3,7},{4,8},{5,1},{6,2},{7,11},{8,12},{9,5},{10,... | collective-permute-start | bytes 3145736 | tf_op jit(solution)/shard_map/ppermute | solution.py:402
  118.9 16.6 %collective-permute-start.24 = (bf16[256,2048]{1,0:T(8,128)(2,1)}, bf16[256,2048]{1,0:T(8,128)(2,1)}, u32[]{:S(2)}, u32[]{:S(2)}) collective-permute-start(bf16[256,2048]{1,0:T(8,128)(2,1)} %get-tuple-element.110), channel_id=1, source_target_pairs={{0,1},{1,0},{2,3},{3,2},{4,5},{5,4},{6,7},{7,6},{8,9},{9,8},{10,11... | collective-permute-start | bytes 3145736 | tf_op jit(solution)/shard_map/ppermute | solution.py:382
  123.6 55.3 %collective-permute-start.23 = (bf16[128,2048]{1,0:T(8,128)(2,1)}, bf16[128,2048]{1,0:T(8,128)(2,1)}, u32[]{:S(2)}, u32[]{:S(2)}) collective-permute-start(bf16[128,2048]{1,0:T(8,128)(2,1)} %get-tuple-element.108), channel_id=1, source_target_pairs={{0,1},{1,0},{2,3},{3,2},{4,5},{5,4},{6,7},{7,6},{8,9},{9,8},{10,11... | collective-permute-start | bytes 1572872 | tf_op jit(solution)/shard_map/ppermute | solution.py:382
  124.0 29.6 %collective-permute-start.38 = (bf16[256,2048]{1,0:T(8,128)(2,1)}, bf16[256,2048]{1,0:T(8,128)(2,1)}, u32[]{:S(2)}, u32[]{:S(2)}) collective-permute-start(bf16[256,2048]{1,0:T(8,128)(2,1)} %get-tuple-element.128), channel_id=1, source_target_pairs={{0,1},{1,0},{2,3},{3,2},{4,5},{5,4},{6,7},{7,6},{8,9},{9,8},{10,11... | collective-permute-start | bytes 3145736 | tf_op jit(solution)/shard_map/ppermute | solution.py:382
  124.1 21.8 %collective-permute-start.37 = (bf16[224,1024]{1,0:T(8,128)(2,1)S(1)}, bf16[224,1024]{1,0:T(8,128)(2,1)S(1)}, u32[]{:S(2)}, u32[]{:S(2)}) collective-permute-start(bf16[224,1024]{1,0:T(8,128)(2,1)S(1)} %slice.90), channel_id=1, source_target_pairs={{0,16},{16,0},{1,17},{17,1},{2,18},{18,2},{3,19},{19,3},{4,20},{20... | collective-permute-start | bytes 1376264 | tf_op jit(solution)/shard_map/ppermute | solution.py:254
  133.8 28.0 %collective-permute-start.41 = (bf16[240,1024]{1,0:T(8,128)(2,1)}, bf16[240,1024]{1,0:T(8,128)(2,1)S(1)}, u32[]{:S(2)}, u32[]{:S(2)}) collective-permute-start(bf16[240,1024]{1,0:T(8,128)(2,1)} %get-tuple-element.145), channel_id=1, source_target_pairs={{0,16},{16,0},{1,17},{17,1},{2,18},{18,2},{3,19},{19,3},{4,20},{20... | collective-permute-start | bytes 1474568 | tf_op jit(solution)/shard_map/ppermute | solution.py:254
  138.7 15.0 %collective-permute-start.36 = (bf16[256,2048]{1,0:T(8,128)(2,1)}, bf16[256,2048]{1,0:T(8,128)(2,1)S(1)}, u32[]{:S(2)}, u32[]{:S(2)}) collective-permute-start(bf16[256,2048]{1,0:T(8,128)(2,1)} %add_convert_fusion), channel_id=1, source_target_pairs={{0,4},{1,3},{2,0},{3,7},{4,8},{5,1},{6,2},{7,11},{8,12},{9,5},{10,... | collective-permute-start | bytes 3145736 | tf_op jit(solution)/shard_map/ppermute | solution.py:402
  145.9 26.8 %collective-permute-start.42 = (bf16[240,1024]{1,0:T(8,128)(2,1)}, bf16[240,1024]{1,0:T(8,128)(2,1)}, u32[]{:S(2)}, u32[]{:S(2)}) collective-permute-start(bf16[240,1024]{1,0:T(8,128)(2,1)} %get-tuple-element.146), channel_id=1, source_target_pairs={{0,16},{16,0},{1,17},{17,1},{2,18},{18,2},{3,19},{19,3},{4,20},{20... | collective-permute-start | bytes 1474568 | tf_op jit(solution)/shard_map/ppermute | solution.py:254
  157.2 15.0 %collective-permute-start.39 = (bf16[128,2048]{1,0:T(8,128)(2,1)}, bf16[128,2048]{1,0:T(8,128)(2,1)}, u32[]{:S(2)}, u32[]{:S(2)}) collective-permute-start(bf16[128,2048]{1,0:T(8,128)(2,1)} %get-tuple-element.143), channel_id=1, source_target_pairs={{0,4},{1,3},{2,0},{3,7},{4,8},{5,1},{6,2},{7,11},{8,12},{9,5},{10,... | collective-permute-start | bytes 1572872 | tf_op jit(solution)/shard_map/ppermute | solution.py:410
  (49 other events, 480.7 us)
